TPU v7x, 256 devices: a whole 4x4x8 slice. The times are simulated.
256 devices in a mesh: ctx: 128 (over z, x, y), ch: 2 (over core).
Axes of the slice: x: 4, y: 4, z: 8, core: 2. Of those that a mesh axis runs over, the one named last changes fastest.
Arguments:
- query_in: bfloat16 [16384, 2048], P('ctx', 'ch'), may hold values from -6 to 6
- key_in: bfloat16 [16384, 2048], P('ctx', 'ch'), may hold values from -6 to 6
- value_in: bfloat16 [16384, 2048], P('ctx', 'ch'), may hold values from -6 to 6
- taps: float32 [3, 7, 2048], P(None, None, 'ch'), may hold values from -2 to 2
- long_filter: float32 [16384, 2048], P('ctx', 'ch'), may hold values from -181.01934 to 181.01934
- out_weight: bfloat16 [2048, 2048], P('ch'), may hold values from -0.125 to 0.125
- out_grad: bfloat16 [16384, 2048], P('ctx', 'ch'), may hold values from -6 to 6
Outputs:
- block_out: bfloat16 [16384, 2048], P('ctx', 'ch')
- grad_query: bfloat16 [16384, 2048], P('ctx', 'ch')
- grad_key: bfloat16 [16384, 2048], P('ctx', 'ch')
- grad_value: bfloat16 [16384, 2048], P('ctx', 'ch')
- grad_filter: float32 [16384, 2048], P('ctx', 'ch')
All inputs are finite; a program needn't handle non-finite values.
Results may differ from a plain program's by a relative error of at most 0.0049.
Values may be sent and summed in bfloat16 or wider, within the bound.
No kernel may reach another device: no remote copies, remote signals or barrier semaphores. Data moves between devices by JAX's collectives and lax.ppermute only.
A program may use at most 128 MiB of HBM per device.

v0:
```python
import math

import jax
import jax.numpy as jnp
from jax import lax
from jax.sharding import PartitionSpec as P

exact = lax.Precision.HIGHEST


def shifted(value, axis, steps):
    count = lax.axis_size(axis)
    first, last = (max(0, -steps), min(count, count - steps))
    return lax.ppermute(value, axis, [(source, source + steps) for source in range(first, last)])


def tables(parts, rows):
    length = 2 * parts * rows
    freqs = jnp.arange(2 * parts, dtype=jnp.int32)
    places = jnp.arange(parts, dtype=jnp.int32)
    offsets = jnp.arange(rows, dtype=jnp.int32)
    first = (freqs[:, None] * places[None, :] % (2 * parts)).astype(jnp.float32) * (
        -2.0 * math.pi / (2 * parts)
    )
    second = (offsets[:, None] * offsets[None, :] % rows).astype(jnp.float32) * (
        -2.0 * math.pi / rows
    )
    turning = (freqs[:, None] * offsets[None, :] % length).astype(jnp.float32) * (
        -2.0 * math.pi / length
    )
    outer = (jnp.cos(first), jnp.sin(first))
    inner = (jnp.cos(second), jnp.sin(second))
    twist = (jnp.cos(turning), jnp.sin(turning))
    return (outer, inner, twist, length)


def product(form, left, right):
    return jnp.einsum(form, left, right, precision=exact)


def complex_product(form, left, right):
    real_part = product(form, left[0], right[0]) - product(form, left[1], right[1])
    imag_part = product(form, left[0], right[1]) + product(form, left[1], right[0])
    return (real_part, imag_part)


def times(left, right):
    return (left[0] * right[0] - left[1] * right[1], left[0] * right[1] + left[1] * right[0])


def times_conj(left, right):
    return (left[0] * right[0] + left[1] * right[1], left[0] * right[1] - left[1] * right[0])


def spectra(fields):
    count, rows, width = fields.shape
    parts = lax.axis_size("ctx")
    outer, inner, twist, length = tables(parts, rows)
    share = rows // parts
    here = lax.axis_index("ctx")
    arrived = lax.all_to_all(fields[:, None], "ctx", split_axis=2, concat_axis=1, tiled=True)
    turned = (
        product("kp,mpjc->mkjc", outer[0], arrived),
        product("kp,mpjc->mkjc", outer[1], arrived),
    )
    angle = (
        lax.dynamic_slice_in_dim(twist[0], here * share, share, 1)[None, :, :, None],
        lax.dynamic_slice_in_dim(twist[1], here * share, share, 1)[None, :, :, None],
    )
    rotated = times(turned, angle)
    moved = lax.all_to_all(jnp.stack(rotated), "ctx", split_axis=2, concat_axis=3, tiled=True)
    result = complex_product("mkbc,bn->mknc", (moved[0], moved[1]), inner)
    return result


def inverse(pair):
    parts = lax.axis_size("ctx")
    rows = pair[0].shape[2]
    outer, inner, twist, length = tables(parts, rows)
    here = lax.axis_index("ctx")
    back = complex_product("mknc,nb->mkbc", pair, (inner[0], -inner[1]))
    angle = (
        lax.dynamic_slice_in_dim(twist[0], here * 2, 2, 0)[None, :, :, None],
        lax.dynamic_slice_in_dim(twist[1], here * 2, 2, 0)[None, :, :, None],
    )
    reverted = times_conj(angle, back)
    moved = lax.all_to_all(jnp.stack(reverted), "ctx", split_axis=3, concat_axis=2, tiled=True)
    summed = (
        product("kp,mkjc->mpjc", outer[0], moved[0]) + product("kp,mkjc->mpjc", outer[1], moved[1])
    ) / length
    landed = lax.all_to_all(summed, "ctx", split_axis=1, concat_axis=2, tiled=True)
    result = landed[:, 0]
    return result


def on_device(query_in, key_in, value_in, taps, long_filter, out_weight, out_grad):
    rows = query_in.shape[0]
    reach = taps.shape[1] - 1
    seq_total = lax.axis_size("ctx") * rows
    scale = 1.0 / math.sqrt(seq_total)
    stacked = jnp.stack([query_in, key_in, value_in])
    before = shifted(stacked[:, rows - reach :, :], "ctx", 1)
    extended = jnp.concatenate([before, stacked], axis=1).astype(jnp.float32)
    shorted = jnp.zeros(stacked.shape, jnp.float32)
    for shift in range(reach + 1):
        start = reach - shift
        shorted = shorted + taps[:, shift, None, :] * extended[:, start : start + rows, :]
    q_short = shorted[0]
    k_short = shorted[1]
    v_short = shorted[2]
    mixed = k_short * v_short
    kernel = long_filter * scale
    forward_re, forward_im = spectra(jnp.stack([mixed, kernel]))
    mixed_spec = (forward_re[0], forward_im[0])
    kernel_spec = (forward_re[1], forward_im[1])
    long_spec = times(mixed_spec, kernel_spec)
    long_out = inverse((long_spec[0][None], long_spec[1][None]))[0]
    gated = (q_short * long_out).astype(jnp.bfloat16)
    partial_sum = jnp.dot(gated, out_weight, preferred_element_type=jnp.float32)
    block_out = lax.psum_scatter(partial_sum, "ch", scatter_dimension=1, tiled=True).astype(
        jnp.bfloat16
    )
    full_grad = lax.all_gather(out_grad, "ch", axis=1, tiled=True)
    grad_gated = lax.dot_general(
        full_grad, out_weight, (((1,), (1,)), ((), ())), preferred_element_type=jnp.float32
    )
    grad_qs = grad_gated * long_out
    grad_long = grad_gated * q_short
    grad_re, grad_im = spectra(grad_long[None])
    grad_spec = (grad_re[0], grad_im[0])
    back_mixed = times_conj(kernel_spec, grad_spec)
    back_kernel = times_conj(mixed_spec, grad_spec)
    returned = inverse(
        (jnp.stack([back_mixed[0], back_kernel[0]]), jnp.stack([back_mixed[1], back_kernel[1]]))
    )
    grad_mixed = returned[0]
    grad_filter = returned[1] * scale
    gradients = jnp.stack([grad_qs, grad_mixed * v_short, grad_mixed * k_short])
    after = shifted(gradients[:, :reach, :].astype(jnp.bfloat16), "ctx", -1).astype(jnp.float32)
    extended_grad = jnp.concatenate([gradients, after], axis=1)
    total = jnp.zeros(gradients.shape, jnp.float32)
    for shift in range(reach + 1):
        total = total + taps[:, shift, None, :] * extended_grad[:, shift : shift + rows, :]
    grad_query = total[0].astype(jnp.bfloat16)
    grad_key = total[1].astype(jnp.bfloat16)
    grad_value = total[2].astype(jnp.bfloat16)
    return (block_out, grad_query, grad_key, grad_value, grad_filter)


def solution(mesh):
    return jax.shard_map(
        on_device,
        mesh=mesh,
        in_specs=(
            P("ctx", "ch"),
            P("ctx", "ch"),
            P("ctx", "ch"),
            P(None, None, "ch"),
            P("ctx", "ch"),
            P("ch", None),
            P("ctx", "ch"),
        ),
        out_specs=(P("ctx", "ch"), P("ctx", "ch"), P("ctx", "ch"), P("ctx", "ch"), P("ctx", "ch")),
        check_vma=False,
    )
```

profile of v0, /device:TPU:30, one launch (start us, length us, event | category | flops | bytes accessed | tf_op | source)
XLA Modules:
  0.0 528.1 jit_solution(16107034123511136146)
XLA Ops:
  7.9 3.4 collective-permute-start
  11.3 1.5 fusion.246
  12.8 2.4 all_gather.3
  15.3 3.8 fusion.261
  19.4 1.3 fusion.29
  20.8 1.3 copy.64
  22.2 14.8 %all-to-all-start.4 = ((f32[1,1,128,1024]{3,1,0,2:T(1,128)}), f32[1,1,128,1024]{3,1,0,2:T(1,128)S(1)}, u32[]{:S(2)}, u32[]{:S(2)}) async-start(f32[1,1,128,1024]{3,1,0,2:T(1,128)} %copy.64), calls=%async_computation.5 | async-start | bytes 1048576 | tf_op jit(solution)/shard_map/all_to_all | solution.py:61
  37.2 1.8 copy.53
  39.0 15.0 %all-to-all-done.4 = f32[1,1,128,1024]{3,1,0,2:T(1,128)S(1)} async-done(((f32[1,1,128,1024]{3,1,0,2:T(1,128)}), f32[1,1,128,1024]{3,1,0,2:T(1,128)S(1)}, u32[]{:S(2)}, u32[]{:S(2)}) %all-to-all-start.4) | async-done | bytes 524320 | tf_op jit(solution)/shard_map/all_to_all | solution.py:61
  54.0 10.4 %all-to-all-start = ((f32[2,1,128,1024]{3,0,1,2:T(2,128)}), f32[2,1,128,1024]{3,0,1,2:T(2,128)S(1)}, u32[]{:S(2)}, u32[]{:S(2)}) async-start(f32[2,1,128,1024]{3,0,1,2:T(2,128)} %copy.53), calls=%async_computation | async-start | bytes 2097152 | tf_op jit(solution)/shard_map/all_to_all | solution.py:61
  65.5 1.5 convolution_bitcast_fusion
  67.0 1.6 subtract_bitcast_fusion.1
  68.7 3.7 copy.65
  72.5 18.1 %all-to-all-done = f32[2,1,128,1024]{3,0,1,2:T(2,128)S(1)} async-done(((f32[2,1,128,1024]{3,0,1,2:T(2,128)}), f32[2,1,128,1024]{3,0,1,2:T(2,128)S(1)}, u32[]{:S(2)}, u32[]{:S(2)}) %all-to-all-start) | async-done | bytes 1048608 | tf_op jit(solution)/shard_map/all_to_all | solution.py:61
  91.6 10.3 %all-to-all-start.5 = ((f32[2,1,256,1,1024]{4,3,1,0,2:T(1,128)}), f32[2,1,256,1,1024]{4,3,1,0,2:T(1,128)S(1)}, u32[]{:S(2)}, u32[]{:S(2)}) async-start(f32[2,1,256,1,1024]{4,3,1,0,2:T(1,128)} %copy.65), calls=%async_computation.6 | async-start | bytes 4194304 | tf_op jit(solution)/shard_map/all_to_all | solution.py:71
  101.9 1.5 copy.54
  103.4 2.3 fusion.56
  105.7 2.5 fusion.5
  108.2 2.3 pad_maximum_fusion
  110.5 7.4 %copy.57 = f32[2,2,256,1,1024]{4,1,3,0,2:T(2,128)} copy(f32[2,2,256,1,1024]{2,4,1,3,0:T(8,128)} %pad_maximum_fusion) | data formatting | bytes 8388608 | tf_op jit(solution)/shard_map/stack | solution.py:71
  117.9 32.2 %all-to-all-done.5 = f32[2,1,256,1,1024]{4,3,1,0,2:T(1,128)S(1)} async-done(((f32[2,1,256,1,1024]{4,3,1,0,2:T(1,128)}), f32[2,1,256,1,1024]{4,3,1,0,2:T(1,128)S(1)}, u32[]{:S(2)}, u32[]{:S(2)}) %all-to-all-start.5) | async-done | bytes 2097184 | tf_op jit(solution)/shard_map/all_to_all | solution.py:71
  150.1 11.1 %all-to-all-start.1 = ((f32[2,2,256,1,1024]{4,1,3,0,2:T(2,128)}), f32[2,2,256,1,1024]{4,1,3,0,2:T(2,128)}, u32[]{:S(2)}, u32[]{:S(2)}) async-start(f32[2,2,256,1,1024]{4,1,3,0,2:T(2,128)} %copy.57), calls=%async_computation.1 | async-start | bytes 8388608 | tf_op jit(solution)/shard_map/all_to_all | solution.py:71
  161.4 1.1 copy.99
  162.5 1.2 copy.141
  163.8 1.3 fusion.61
  165.1 2.2 fusion.39
  167.3 2.2 fusion.60
  169.5 84.0 %all-to-all-done.1 = f32[2,2,256,1,1024]{4,1,3,0,2:T(2,128)} async-done(((f32[2,2,256,1,1024]{4,1,3,0,2:T(2,128)}), f32[2,2,256,1,1024]{4,1,3,0,2:T(2,128)}, u32[]{:S(2)}, u32[]{:S(2)}) %all-to-all-start.1) | async-done | bytes 4194336 | tf_op jit(solution)/shard_map/all_to_all | solution.py:71
  253.5 4.6 copy.140
  258.1 2.1 fusion.12
  260.3 2.3 fusion.13
  262.6 2.2 add_bitcast_fusion
  264.8 2.2 subtract_bitcast_fusion
  267.1 3.6 multiply_add_fusion.1
  270.7 1.3 fusion.52
  272.0 1.3 fusion.54
  273.3 1.3 fusion.40
  274.6 2.0 add_bitcast_fusion.2
  276.7 3.0 copy.61
  279.7 10.2 %all-to-all-start.2 = ((f32[2,1,2,128,1024]{4,2,1,0,3:T(2,128)}), f32[2,1,2,128,1024]{4,2,1,0,3:T(2,128)}, u32[]{:S(2)}, u32[]{:S(2)}) async-start(f32[2,1,2,128,1024]{4,2,1,0,3:T(2,128)} %copy.61), calls=%async_computation.2 | async-start | bytes 4194304 | tf_op jit(solution)/shard_map/all_to_all | solution.py:87
  289.9 2.1 fusion.16
  292.1 2.1 fusion.17
  294.3 2.2 fusion.20
  296.5 2.7 fusion.1
  299.5 5.4 %copy.68 = f32[2,2,2,128,1024]{4,2,1,0,3:T(2,128)} copy(f32[2,2,2,128,1024]{4,3,2,1,0:T(8,128)S(1)} %pad_maximum_fusion.1) | data formatting | bytes 8388608 | tf_op jit(solution)/shard_map/stack | solution.py:87
  304.9 32.4 %all-to-all-done.2 = f32[2,1,2,128,1024]{4,2,1,0,3:T(2,128)} async-done(((f32[2,1,2,128,1024]{4,2,1,0,3:T(2,128)}), f32[2,1,2,128,1024]{4,2,1,0,3:T(2,128)}, u32[]{:S(2)}, u32[]{:S(2)}) %all-to-all-start.2) | async-done | bytes 2097184 | tf_op jit(solution)/shard_map/all_to_all | solution.py:87
  337.3 10.5 %all-to-all-start.6 = ((f32[2,2,2,128,1024]{4,2,1,0,3:T(2,128)}), f32[2,2,2,128,1024]{4,2,1,0,3:T(2,128)}, u32[]{:S(2)}, u32[]{:S(2)}) async-start(f32[2,2,2,128,1024]{4,2,1,0,3:T(2,128)} %copy.68), calls=%async_computation.7 | async-start | bytes 8388608 | tf_op jit(solution)/shard_map/all_to_all | solution.py:87
  347.7 2.3 fusion.245
  351.5 2.2 fusion.112
  353.6 2.2 fusion.49
  356.9 83.0 %all-to-all-done.6 = f32[2,2,2,128,1024]{4,2,1,0,3:T(2,128)} async-done(((f32[2,2,2,128,1024]{4,2,1,0,3:T(2,128)}), f32[2,2,2,128,1024]{4,2,1,0,3:T(2,128)}, u32[]{:S(2)}, u32[]{:S(2)}) %all-to-all-start.6) | async-done | bytes 4194336 | tf_op jit(solution)/shard_map/all_to_all | solution.py:87
  439.9 9.7 %all-to-all-start.3 = ((f32[1,128,1,1024]{3,2,0,1:T(1,128)}), f32[1,128,1,1024]{3,2,0,1:T(1,128)S(1)}, u32[]{:S(2)}, u32[]{:S(2)}) async-start(f32[1,128,1,1024]{3,2,0,1:T(1,128)} %copy.62), calls=%async_computation.3 | async-start | bytes 1048576 | tf_op jit(solution)/shard_map/all_to_all | solution.py:91
  449.6 4.2 fusion.244
  456.0 4.2 fusion.8
  460.2 4.4 fusion.45
  464.6 2.0 copy.75
  466.7 14.2 %all-to-all-start.7 = ((f32[2,128,1,1024]{3,2,0,1:T(1,128)}), f32[2,128,1,1024]{3,2,0,1:T(1,128)}, u32[]{:S(2)}, u32[]{:S(2)}) async-start(f32[2,128,1,1024]{3,2,0,1:T(1,128)} %copy.75), calls=%async_computation.8 | async-start | bytes 2097152 | tf_op jit(solution)/shard_map/all_to_all | solution.py:91
  480.9 4.0 fusion.70
  485.1 19.9 %all-to-all-done.7 = f32[2,128,1,1024]{3,2,0,1:T(1,128)} async-done(((f32[2,128,1,1024]{3,2,0,1:T(1,128)}), f32[2,128,1,1024]{3,2,0,1:T(1,128)}, u32[]{:S(2)}, u32[]{:S(2)}) %all-to-all-start.7) | async-done | bytes 1048608 | tf_op jit(solution)/shard_map/all_to_all | solution.py:91
  505.0 2.9 slice_multiply_fusion.13
  508.2 3.6 collective-permute-start.1
  511.8 1.8 convert_element_type.98
  514.5 3.9 collective-permute-done.1
  518.6 1.3 fusion.23
  (67 shorter events, 11.3 us)
Async XLA Ops:
  7.9 11.2 %collective-permute-start = (bf16[3,6,1024]{2,1,0:T(8,128)(2,1)S(1)}, bf16[3,6,1024]{2,1,0:T(8,128)(2,1)S(1)}, u32[]{:S(2)}, u32[]{:S(2)}) collective-permute-start(bf16[3,6,1024]{2,1,0:T(8,128)(2,1)S(1)} %pad_maximum_fusion.16), channel_id=1, source_target_pairs={{0,2},{2,4},{4,6},{6,8},{8,10},{10,12},{12,14},{14,16},{16,18},{18... | collective-permute-start | bytes 110600 | tf_op jit(solution)/shard_map/ppermute | solution.py:14
  15.3 3.9 copy-start.11
  15.3 3.9 copy-start.12
  15.3 3.9 copy-start.13
  19.1 1.6 copy-start.5
  20.7 16.3 %copy-start = (f32[3,128,1024]{2,1,0:T(8,128)}, f32[3,128,1024]{2,1,0:T(8,128)S(1)}, u32[]{:S(2)}) copy-start(f32[3,128,1024]{2,1,0:T(8,128)S(1)} %fusion.29) | copy-start | bytes 4718596
  20.7 16.3 %copy-start.14 = (f32[128,1024]{1,0:T(8,128)S(1)}, f32[128,1024]{1,0:T(8,128)}, u32[]{:S(2)}) copy-start(f32[128,1024]{1,0:T(8,128)} %param.11) | copy-start | bytes 1572868
  22.2 31.9 %all-to-all-start.4 = ((f32[1,1,128,1024]{3,1,0,2:T(1,128)}), f32[1,1,128,1024]{3,1,0,2:T(1,128)S(1)}, u32[]{:S(2)}, u32[]{:S(2)}) async-start(f32[1,1,128,1024]{3,1,0,2:T(1,128)} %copy.64), calls=%async_computation.5 | async-start | bytes 1048576 | tf_op jit(solution)/shard_map/all_to_all | solution.py:61
  54.0 36.5 %all-to-all-start = ((f32[2,1,128,1024]{3,0,1,2:T(2,128)}), f32[2,1,128,1024]{3,0,1,2:T(2,128)S(1)}, u32[]{:S(2)}, u32[]{:S(2)}) async-start(f32[2,1,128,1024]{3,0,1,2:T(2,128)} %copy.53), calls=%async_computation | async-start | bytes 2097152 | tf_op jit(solution)/shard_map/all_to_all | solution.py:61
  90.6 1.0 copy-start.7
  91.6 58.5 %all-to-all-start.5 = ((f32[2,1,256,1,1024]{4,3,1,0,2:T(1,128)}), f32[2,1,256,1,1024]{4,3,1,0,2:T(1,128)S(1)}, u32[]{:S(2)}, u32[]{:S(2)}) async-start(f32[2,1,256,1,1024]{4,3,1,0,2:T(1,128)} %copy.65), calls=%async_computation.6 | async-start | bytes 4194304 | tf_op jit(solution)/shard_map/all_to_all | solution.py:71
  150.1 103.4 %all-to-all-start.1 = ((f32[2,2,256,1,1024]{4,1,3,0,2:T(2,128)}), f32[2,2,256,1,1024]{4,1,3,0,2:T(2,128)}, u32[]{:S(2)}, u32[]{:S(2)}) async-start(f32[2,2,256,1,1024]{4,1,3,0,2:T(2,128)} %copy.57), calls=%async_computation.1 | async-start | bytes 8388608 | tf_op jit(solution)/shard_map/all_to_all | solution.py:71
  264.8 2.2 copy-start.8
  264.8 2.2 copy-start.9
  279.7 10.2 %copy-start.3 = (f32[1,2,128,1024]{3,2,1,0:T(8,128)S(1)}, f32[1,2,128,1024]{3,2,1,0:T(8,128)}, u32[]{:S(2)}) copy-start(f32[1,2,128,1024]{3,2,1,0:T(8,128)} %get-tuple-element.16) | copy-start | bytes 3145732
  279.7 10.2 %copy-start.4 = (f32[1,2,128,1024]{3,2,1,0:T(8,128)S(1)}, f32[1,2,128,1024]{3,2,1,0:T(8,128)}, u32[]{:S(2)}) copy-start(f32[1,2,128,1024]{3,2,1,0:T(8,128)} %get-tuple-element.17) | copy-start | bytes 3145732
  279.7 57.6 %all-to-all-start.2 = ((f32[2,1,2,128,1024]{4,2,1,0,3:T(2,128)}), f32[2,1,2,128,1024]{4,2,1,0,3:T(2,128)}, u32[]{:S(2)}, u32[]{:S(2)}) async-start(f32[2,1,2,128,1024]{4,2,1,0,3:T(2,128)} %copy.61), calls=%async_computation.2 | async-start | bytes 4194304 | tf_op jit(solution)/shard_map/all_to_all | solution.py:87
  292.1 2.2 copy-start.2
  337.3 102.6 %all-to-all-start.6 = ((f32[2,2,2,128,1024]{4,2,1,0,3:T(2,128)}), f32[2,2,2,128,1024]{4,2,1,0,3:T(2,128)}, u32[]{:S(2)}, u32[]{:S(2)}) async-start(f32[2,2,2,128,1024]{4,2,1,0,3:T(2,128)} %copy.68), calls=%async_computation.7 | async-start | bytes 8388608 | tf_op jit(solution)/shard_map/all_to_all | solution.py:87
  439.9 26.8 %all-to-all-start.3 = ((f32[1,128,1,1024]{3,2,0,1:T(1,128)}), f32[1,128,1,1024]{3,2,0,1:T(1,128)S(1)}, u32[]{:S(2)}, u32[]{:S(2)}) async-start(f32[1,128,1,1024]{3,2,0,1:T(1,128)} %copy.62), calls=%async_computation.3 | async-start | bytes 1048576 | tf_op jit(solution)/shard_map/all_to_all | solution.py:91
  464.6 16.3 %copy-start.1 = (f32[3,128,1024]{2,1,0:T(8,128)S(1)}, f32[3,128,1024]{2,1,0:T(8,128)}, u32[]{:S(2)}) copy-start(f32[3,128,1024]{2,1,0:T(8,128)} %copy-done) | copy-start | bytes 4718596
  466.7 38.3 %all-to-all-start.7 = ((f32[2,128,1,1024]{3,2,0,1:T(1,128)}), f32[2,128,1,1024]{3,2,0,1:T(1,128)}, u32[]{:S(2)}, u32[]{:S(2)}) async-start(f32[2,128,1,1024]{3,2,0,1:T(1,128)} %copy.75), calls=%async_computation.8 | async-start | bytes 2097152 | tf_op jit(solution)/shard_map/all_to_all | solution.py:91
  480.9 4.1 copy-start.6
  480.9 30.9 %reduce-scatter.2.cloned.1.call-start = ((), (), s32[]{:S(2)}) async-start(), calls=%async_computation.9 | async-start | bytes 1572864 | tf_op jit(solution)/shard_map/reduce_scatter | solution.py:120
  508.1 5.5 %copy-start.10 = (f32[1,128,1,1024]{3,2,0,1:T(1,128)S(1)}, f32[1,128,1,1024]{3,2,0,1:T(1,128)}, u32[]{:S(2)}) copy-start(f32[1,128,1,1024]{3,2,0,1:T(1,128)} %get-tuple-element.35) | copy-start | bytes 1572868
  508.2 10.2 %collective-permute-start.1 = (bf16[3,6,1024]{2,1,0:T(8,128)(2,1)S(1)}, bf16[3,6,1024]{2,1,0:T(8,128)(2,1)S(1)}, u32[]{:S(2)}, u32[]{:S(2)}) collective-permute-start(bf16[3,6,1024]{2,1,0:T(8,128)(2,1)S(1)} %slice.332), channel_id=1, source_target_pairs={{2,0},{4,2},{6,4},{8,6},{10,8},{12,10},{14,12},{16,14},{18,16},{20... | collective-permute-start | bytes 110600 | tf_op jit(solution)/shard_map/ppermute | solution.py:14
Sparse Core Ops, SparseCore 0:
  485.0 15.1 reduce-scatter.1
where the time goes:
time: 536 us; the launch traced here: 528 us
  waiting for transfers between devices  289 us (54%)
  starting transfers between devices  98.3 us (18%)
  matrix products  61.9 us (12%)
  local copies, waits for them, and re-layouts  48.8 us (9%)
  between operations  15.2 us (3%)
  other arithmetic  13 us (2%)
    all_to_all x2, waiting for transfers between devices, spectra(): lax.all_to_all(jnp.stack(rotated), 'ctx', split_axis=2, concat_axis=3, ti...  116 us
    all_to_all x2, waiting for transfers between devices, inverse(): lax.all_to_all(jnp.stack(reverted), 'ctx', split_axis=3, concat_axis=2, t...  115 us
    dot_general x24, matrix products, product(): return jnp.einsum(form, left, right, precision=exact)  54.1 us
    all_to_all x2, waiting for transfers between devices, spectra(): lax.all_to_all(fields[:, None], 'ctx', split_axis=2, concat_axis=1, tiled...  33.1 us
    all_to_all x2, starting transfers between devices, spectra(): lax.all_to_all(fields[:, None], 'ctx', split_axis=2, concat_axis=1, tiled...  25.3 us
    all_to_all x2, starting transfers between devices, inverse(): lax.all_to_all(summed, 'ctx', split_axis=1, concat_axis=2, tiled=True)  23.9 us
    all_to_all x2, starting transfers between devices, spectra(): lax.all_to_all(jnp.stack(rotated), 'ctx', split_axis=2, concat_axis=3, ti...  21.4 us
    all_to_all x2, starting transfers between devices, inverse(): lax.all_to_all(jnp.stack(reverted), 'ctx', split_axis=3, concat_axis=2, t...  20.7 us
  transfers between devices with their start and end apart: 11, of which 8 were waited for; matrix products, arithmetic and copies ran while one was open for 17% of the time, Pallas kernels for 0%

commit v1 on v0

v1 whole, which is shorter than its diff:
```python
import math

import jax
import jax.numpy as jnp
import ml_dtypes
import numpy as np
from jax import lax
from jax.experimental import pallas as pl
from jax.experimental.pallas import tpu as pltpu
from jax.sharding import PartitionSpec as P

f32 = jnp.float32
bf16 = jnp.bfloat16
EDGE = 8
WIDE = 256
VMEM_LIMIT = 48 * 1024 * 1024


def shifted(value, axis, steps):
    count = lax.axis_size(axis)
    first, last = (max(0, -steps), min(count, count - steps))
    return lax.ppermute(value, axis, [(source, source + steps) for source in range(first, last)])


def halves(table):
    high = table.astype(ml_dtypes.bfloat16)
    low = (table - high.astype(np.float64)).astype(ml_dtypes.bfloat16)
    return high, low


def tables(parts, rows, gain):
    freqs = np.arange(parts) + 0.5
    blocks = np.arange(parts)
    inner = np.arange(rows)
    outer = np.outer(freqs, blocks) * (-2.0 * math.pi / (2 * parts))
    turn = np.outer(freqs, inner) * (-2.0 * math.pi / (2 * parts * rows))
    small = np.outer(inner, inner) % rows * (-2.0 * math.pi / rows)
    first = halves(np.concatenate([np.cos(outer), np.sin(outer)], 0))
    first = np.concatenate(first, 1)
    c, s = np.cos(small), np.sin(small)
    high, low = halves(np.block([[c, s], [-s, c]]))
    second = np.concatenate([high, high, low], 0)
    high, low = halves(np.block([[c, -s], [s, c]]))
    back = np.concatenate([high, high, low], 0)
    high, low = halves(np.concatenate([np.cos(outer).T, np.sin(outer).T], 1) * gain)
    last = np.concatenate([high, high, low], 1)
    twist = np.stack([np.cos(turn), np.sin(turn)]).astype(np.float32)
    return first, second, back, last, twist


def split(value):
    high = value.astype(bf16)
    low = (value - high.astype(f32)).astype(bf16)
    return high, low


def prepare_kernel(q, k, v, halo, taps, filt, mine, other, w_mine, w_other, send, qs, ks, vs, gg, pad):
    rows, width = q.shape

    def short(x, which):
        pad[0:EDGE, :] = halo[which].astype(f32)
        pad[EDGE : EDGE + rows, :] = x[...].astype(f32)
        total = taps[which, 0:1, :] * pad[EDGE : EDGE + rows, :]
        for shift in range(1, taps.shape[1]):
            total = total + taps[which, shift : shift + 1, :] * pad[EDGE - shift : EDGE - shift + rows, :]
        return total

    across = (((1,), (1,)), ((), ()))
    grad = lax.dot_general(mine[...], w_mine[...], across, preferred_element_type=f32)
    grad = grad + lax.dot_general(other[...], w_other[...], across, preferred_element_type=f32)
    gg[...] = grad
    q_short = short(q, 0)
    qs[...] = q_short
    k_short = short(k, 1)
    ks[...] = k_short
    v_short = short(v, 2)
    vs[...] = v_short
    fields = (k_short * v_short, filt[...], grad * q_short)
    turned = [field.T.reshape(width // 8, 8, rows) for field in fields]
    send[...] = jnp.concatenate(turned, axis=1).astype(bf16)


def spectral_kernel(x, first, second, back, last, twist, out, buf):
    parts, lines, rows = x.shape
    group = lines // 3
    buf[...] = x[...].astype(f32).reshape(parts * lines, rows)
    cos, sin = twist[0], twist[1]

    def dot(left, right):
        return jnp.dot(left, right, preferred_element_type=f32)

    def wide(value, table):
        high, low = split(value)
        return dot(jnp.concatenate([high, low, high], 1), table[...])

    for c in range(group):
        places = [pl.ds(f * group + c, parts, stride=lines) for f in range(3)]
        field = jnp.concatenate([buf[place, :] for place in places], 1).astype(bf16)
        half = dot(first[...], jnp.concatenate([field, field], 0))
        turned = []
        for f in range(3):
            re = half[:parts, f * rows : (f + 1) * rows]
            im = half[parts:, f * rows : (f + 1) * rows]
            turned.append(jnp.concatenate([re * cos - im * sin, re * sin + im * cos], 1))
        spec = wide(jnp.concatenate(turned, 0), second)
        (xr, xi), (kr, ki), (gr, gi) = [
            (spec[f * parts : (f + 1) * parts, :rows], spec[f * parts : (f + 1) * parts, rows:])
            for f in range(3)
        ]
        long_spec = jnp.concatenate([xr * kr - xi * ki, xr * ki + xi * kr], 1)
        mixed_spec = jnp.concatenate([kr * gr + ki * gi, kr * gi - ki * gr], 1)
        filter_spec = jnp.concatenate([xr * gr + xi * gi, xr * gi - xi * gr], 1)
        part = wide(jnp.concatenate([long_spec, mixed_spec, filter_spec], 0), back)
        turned = []
        for f in range(3):
            re = part[f * parts : (f + 1) * parts, :rows]
            im = part[f * parts : (f + 1) * parts, rows:]
            turned.append(jnp.concatenate([re * cos + im * sin, im * cos - re * sin], 0))
        high, low = split(jnp.concatenate(turned, 1))
        result = dot(last[...], jnp.concatenate([high, low, high], 0))
        for f in range(3):
            buf[places[f], :] = result[:, f * rows : (f + 1) * rows]
    out[...] = buf[...].reshape(parts, lines, rows).astype(bf16)


def finish_kernel(here, landed, qs, ks, vs, gg, w_mine, w_other, gq, gk, gv, gf, heads, mine, other, total):
    step = pl.program_id(0)
    count, lines, rows = landed.shape
    group = lines // 3
    values = landed[...].astype(f32)
    long_out, grad_mixed, grad_filter = [
        values[:, f * group : (f + 1) * group, :].reshape(count * group, rows).T for f in range(3)
    ]
    gated = (qs[...] * long_out).astype(bf16)
    mine_part = jnp.dot(gated, w_mine[...], preferred_element_type=f32)
    other_part = jnp.dot(gated, w_other[...], preferred_element_type=f32)

    @pl.when(step == 0)
    def _():
        mine[...] = mine_part
        total[...] = other_part

    @pl.when(step > 0)
    def _():
        mine[...] += mine_part
        total[...] += other_part

    other[...] = total[...].astype(bf16)
    gf[...] = grad_filter
    for which, (to, value) in enumerate(
        ((gq, gg[...] * long_out), (gk, grad_mixed * vs[...]), (gv, grad_mixed * ks[...]))
    ):
        to[...] = value
        heads[which] = value[:EDGE, :].astype(bf16)


def close_kernel(gq, gk, gv, after, taps, mine, other, block_out, oq, ok, ov, pad):
    rows, width = gq.shape
    for which, (value, to) in enumerate(((gq, oq), (gk, ok), (gv, ov))):
        pad[0:rows, :] = value[...]
        pad[rows : rows + EDGE, :] = after[which].astype(f32)
        total = taps[which, 0:1, :] * pad[0:rows, :]
        for shift in range(1, taps.shape[1]):
            total = total + taps[which, shift : shift + 1, :] * pad[shift : shift + rows, :]
        to[...] = total.astype(bf16)
    block_out[...] = (mine[...] + other[...].astype(f32)).astype(bf16)


def on_device(query_in, key_in, value_in, taps, long_filter, out_weight, out_grad):
    rows, width = query_in.shape
    parts = lax.axis_size("ctx")
    seq_total = parts * rows
    group = width // parts
    lines = 3 * group
    reach = taps.shape[1]
    outs = out_weight.shape[1]
    here = lax.axis_index("ch").astype(jnp.int32).reshape(1)
    gain = 1.0 / math.sqrt(seq_total) / seq_total
    swap = [(0, 1), (1, 0)]

    tails = jnp.stack([query_in[rows - EDGE :], key_in[rows - EDGE :], value_in[rows - EDGE :]])
    halo = shifted(tails, "ctx", 1)
    grad_other = lax.ppermute(out_grad, "ch", swap)

    steps = width // WIDE
    column = pl.BlockSpec((rows, WIDE), lambda i, me: (0, i))
    edge = pl.BlockSpec((3, EDGE, WIDE), lambda i, me: (0, 0, i))
    taps_spec = pl.BlockSpec((3, reach, WIDE), lambda i, me: (0, 0, i))
    whole = pl.BlockSpec((rows, width), lambda i, me: (0, 0))
    w_mine = pl.BlockSpec((WIDE, outs // 2), lambda i, me: (i, me[0]))
    w_other = pl.BlockSpec((WIDE, outs // 2), lambda i, me: (i, 1 - me[0]))
    chunk = pl.BlockSpec((WIDE // group, lines, rows), lambda i, me: (i, 0, 0))
    params = pltpu.CompilerParams(vmem_limit_bytes=VMEM_LIMIT)
    flat = jax.ShapeDtypeStruct((rows, width), f32)
    half = jax.ShapeDtypeStruct((rows, width), bf16)
    fields = jax.ShapeDtypeStruct((parts, lines, rows), bf16)

    with jax.named_scope("prepare"):
        send, qs, ks, vs, gg = pl.pallas_call(
            prepare_kernel_with_index,
            grid_spec=pltpu.PrefetchScalarGridSpec(
                num_scalar_prefetch=1,
                grid=(steps,),
                in_specs=[column] * 3 + [edge, taps_spec, column, whole, whole, w_mine, w_other],
                out_specs=[chunk] + [column] * 4,
                scratch_shapes=[pltpu.VMEM((rows + EDGE, WIDE), f32)],
            ),
            out_shape=[fields, flat, flat, flat, flat],
            compiler_params=params,
        )(here, query_in, key_in, value_in, halo, taps, long_filter, out_grad, grad_other, out_weight, out_weight)

    arrived = lax.all_to_all(send, "ctx", split_axis=0, concat_axis=0, tiled=True)

    with jax.named_scope("spectral"):
        solved = pl.pallas_call(
            spectral_kernel,
            out_shape=fields,
            scratch_shapes=[pltpu.VMEM((parts * lines, rows), f32)],
            compiler_params=params,
        )(arrived, *tables(parts, rows, gain))

    landed = lax.all_to_all(solved, "ctx", split_axis=0, concat_axis=0, tiled=True)

    with jax.named_scope("finish"):
        gq, gk, gv, grad_filter, heads, mine, other = pl.pallas_call(
            finish_kernel,
            grid_spec=pltpu.PrefetchScalarGridSpec(
                num_scalar_prefetch=1,
                grid=(steps,),
                in_specs=[chunk] + [column] * 4 + [w_mine, w_other],
                out_specs=[column] * 4 + [edge, whole, whole],
                scratch_shapes=[pltpu.VMEM((rows, width), f32)],
            ),
            out_shape=[flat] * 4 + [jax.ShapeDtypeStruct((3, EDGE, width), bf16), flat, half],
            compiler_params=params,
        )(here, landed, qs, ks, vs, gg, out_weight, out_weight)

    theirs = lax.ppermute(other, "ch", swap)
    after = shifted(heads, "ctx", -1)

    with jax.named_scope("close"):
        column = pl.BlockSpec((rows, WIDE), lambda i: (0, i))
        edge = pl.BlockSpec((3, EDGE, WIDE), lambda i: (0, 0, i))
        taps_spec = pl.BlockSpec((3, reach, WIDE), lambda i: (0, 0, i))
        block_out, grad_query, grad_key, grad_value = pl.pallas_call(
            close_kernel,
            grid=(steps,),
            in_specs=[column] * 3 + [edge, taps_spec, column, column],
            out_specs=[column] * 4,
            out_shape=[half] * 4,
            scratch_shapes=[pltpu.VMEM((rows + EDGE, WIDE), f32)],
            compiler_params=params,
        )(gq, gk, gv, after, taps, mine, theirs)
    return (block_out, grad_query, grad_key, grad_value, grad_filter)


def prepare_kernel_with_index(here, *refs):
    prepare_kernel(*refs)


def solution(mesh):
    return jax.shard_map(
        on_device,
        mesh=mesh,
        in_specs=(
            P("ctx", "ch"),
            P("ctx", "ch"),
            P("ctx", "ch"),
            P(None, None, "ch"),
            P("ctx", "ch"),
            P("ch", None),
            P("ctx", "ch"),
        ),
        out_specs=(P("ctx", "ch"), P("ctx", "ch"), P("ctx", "ch"), P("ctx", "ch"), P("ctx", "ch")),
        check_vma=False,
    )
```

time: 536 us -> 116 us (0.22); the launches traced: 528 us -> 114 us
  waiting for transfers between devices: 289 us -> 9.23 us
  starting transfers between devices: 98.3 us -> 7.14 us
  blocking collectives: 2.39 us -> 67.7 us
  matrix products: 61.9 us -> 0 us
  local copies, waits for them, and re-layouts: 48.8 us -> 7.22 us
  Pallas kernels: 0 us -> 22.1 us
  between operations: 15.2 us -> 0.72 us
  other arithmetic: 13 us -> 0.01 us
    all_to_all x8 -> x0, waiting for transfers between devices: 285 us -> none  [the longest x2 116 us: spectra(): lax.all_to_all(jnp.stack(rotated), 'ctx', split_axis=2, concat_axis=3, ti...]
    all_to_all x8 -> x0, starting transfers between devices: 91.3 us -> none  [the longest x2 25.3 us: spectra(): lax.all_to_all(fields[:, None], 'ctx', split_axis=2, concat_axis=1, tiled...]
    all_to_all x0 -> x2, blocking collectives: none -> 67.7 us  [the longest x1 36.9 us: on_device(): lax.all_to_all(send, 'ctx', split_axis=0, concat_axis=0, tiled=True)]
    dot_general x26 -> x0, matrix products: 61.9 us -> none  [the longest x24 54.1 us: product(): return jnp.einsum(form, left, right, precision=exact)]
    pallas_call x0 -> x4, Pallas kernels: none -> 22.1 us  [the longest x1 8.81 us: on_device(): pl.pallas_call(spectral_kernel, out_shape=fields, scratch_shapes=[pltpu.V...]
    another operation x7 -> x2, local copies, waits for them, and re-layouts: 22.2 us -> 1.46 us  [on_device(): jnp.stack([query_in[rows - EDGE:], key_in[rows - EDGE:], value_in[rows -...]
    slice x6 -> x0, local copies, waits for them, and re-layouts: 10.1 us -> none  [the longest x2 5.29 us: inverse(): moved[0]]
    all_to_all x3 -> x0, local copies, waits for them, and re-layouts: 7.31 us -> none  [the longest x2 5.84 us: spectra(): lax.all_to_all(jnp.stack(rotated), 'ctx', split_axis=2, concat_axis=3, ti...]
  transfers between devices with their start and end apart: 11 -> 4, of which waited for: 8 -> 2; matrix products, arithmetic and copies ran while one was open for 17% -> 1% of each run, Pallas kernels for 0% -> 0%
where the time goes in v1:
time: 116 us; the launch traced here: 114 us
  blocking collectives  67.7 us (58%)
  Pallas kernels  22.1 us (19%)
  waiting for transfers between devices  9.23 us (8%)
  local copies, waits for them, and re-layouts  7.22 us (6%)
  starting transfers between devices  7.14 us (6%)
    all_to_all x1, blocking collectives, on_device(): lax.all_to_all(send, 'ctx', split_axis=0, concat_axis=0, tiled=True)  36.9 us
    all_to_all x1, blocking collectives, on_device(): lax.all_to_all(solved, 'ctx', split_axis=0, concat_axis=0, tiled=True)  30.8 us
    ppermute x2, waiting for transfers between devices, shifted(): lax.ppermute(value, axis, [(source, source + steps) for source in range(f...  9.23 us
    pallas_call x1, Pallas kernels, on_device(): pl.pallas_call(spectral_kernel, out_shape=fields, scratch_shapes=[pltpu.V...  8.81 us
    ppermute x2, starting transfers between devices, shifted(): lax.ppermute(value, axis, [(source, source + steps) for source in range(f...  7.04 us
    unnamed x24, local copies, waits for them, and re-layouts  5.76 us
    pallas_call x1, Pallas kernels, on_device(): pl.pallas_call(prepare_kernel_with_index, grid_spec=pltpu.PrefetchScalarG...  5.5 us
    pallas_call x1, Pallas kernels, on_device(): pl.pallas_call(finish_kernel, grid_spec=pltpu.PrefetchScalarGridSpec(num_...  5.03 us
  transfers between devices with their start and end apart: 4, of which 2 were waited for; matrix products, arithmetic and copies ran while one was open for 1% of the time, Pallas kernels for 0%

profile of v1, /device:TPU:30, one launch (start us, length us, event | category | flops | bytes accessed | tf_op | source)
XLA Modules:
  0.0 114.1 jit_solution(2130029336029735412)
XLA Ops:
  0.6 0.1 collective-permute-start.1
  0.7 0.7 slice_bitcast_fusion
  1.5 0.7 slice_bitcast_fusion.2
  2.2 3.4 %collective-permute-start = (bf16[3,8,1024]{2,1,0:T(8,128)(2,1)S(1)}, bf16[3,8,1024]{2,1,0:T(8,128)(2,1)S(1)}, u32[]{:S(2)}, u32[]{:S(2)}) collective-permute-start(bf16[3,8,1024]{2,1,0:T(8,128)(2,1)S(1)} %pad_maximum_fusion), channel_id=1, source_target_pairs={{0,2},{2,4},{4,6},{6,8},{8,10},{10,12},{12,14},{14,16},{16,18},{18... | collective-permute-start | bytes 147464 | tf_op jit(solution)/shard_map/ppermute | solution.py:22
  5.6 2.6 %collective-permute-done.refs_3_ = bf16[3,8,1024]{2,1,0:T(8,128)(2,1)S(1)} collective-permute-done((bf16[3,8,1024]{2,1,0:T(8,128)(2,1)S(1)}, bf16[3,8,1024]{2,1,0:T(8,128)(2,1)S(1)}, u32[]{:S(2)}, u32[]{:S(2)}) %collective-permute-start) | collective-permute-done | bytes 49184 | tf_op jit(solution)/shard_map/ppermute | solution.py:22
  8.2 0.0 collective-permute-done.1.refs_7_
  8.2 0.0 copy-start
  8.2 1.0 copy-done
  9.3 0.0 copy-start.3
  9.3 0.9 copy-done.3
  10.2 0.0 copy-start.5
  10.2 0.9 copy-done.5
  11.1 0.0 copy-start.6
  11.1 0.9 copy-done.6
  12.1 0.0 copy-start.7
  12.1 0.9 copy-done.7
  13.0 0.0 copy-start.8
  13.0 0.9 copy-done.8
  14.0 0.0 copy-start.1
  14.0 0.0 copy-start.2
  14.0 0.0 copy-start.9
  14.0 0.0 copy-start.10
  14.0 0.0 copy-start.11
  14.0 5.5 %prepare.1 = (bf16[128,24,128]{2,1,0:T(8,128)(2,1)S(1)}, f32[128,1024]{1,0:T(8,128)S(1)}, f32[128,1024]{1,0:T(8,128)S(1)}, f32[128,1024]{1,0:T(8,128)S(1)}, f32[128,1024]{1,0:T(8,128)S(1)}) custom-call(s32[1]{0:T(128)} %bitcast.here, bf16[128,1024]{1,0:T(8,128)(2,1)S(1)} %copy-done.5, bf16[128,1024]{1,0:T(8,128)(2,1)S(1)} %copy-done.6, ...), custom_call_target="tpu_custom_call" | custom-call | tf_op jit(solution)/shard_map/prepare/pallas_call | solution.py:199
  19.5 36.9 %all_to_all.10.x = bf16[128,24,128]{2,1,0:T(8,128)(2,1)S(1)} all-to-all(bf16[128,24,128]{2,1,0:T(8,128)(2,1)S(1)} %get-tuple-element.21), channel_id=1, replica_groups=mesh['ctx'=128,'ch'=2] {'ctx'}, dimensions={0} | all-to-all | bytes 1572864 | tf_op jit(solution)/shard_map/all_to_all | solution.py:212
  56.4 0.0 copy-done.1
  56.4 0.0 copy-done.2
  56.4 0.0 copy-done.9
  56.4 0.0 copy-done.10
  56.4 0.0 copy-done.11
  56.5 8.8 %spectral.1 = bf16[128,24,128]{2,1,0:T(8,128)(2,1)S(1)} custom-call(bf16[128,24,128]{2,1,0:T(8,128)(2,1)S(1)} %all_to_all.10.x, bf16[256,256]{1,0:T(8,128)(2,1)S(1)} %copy-done.11, bf16[768,256]{1,0:T(8,128)(2,1)S(1)} %copy-done.2, bf16[768,256]{1,0:T(8,128)(2,1)S(1)} %copy-done.1, bf16[128,768]{1,0:T(8,128)(2,1)S(1)} %copy-done.9, f32[2,128,128]{2,1,0:T(8,128)S(1)} %copy-done.10), custom_call_target="tpu_custom_call" | custom-call | tf_op jit(solution)/shard_map/spectral/pallas_call | solution.py:215
  65.3 30.8 %all_to_all.11.landed = bf16[128,24,128]{2,1,0:T(8,128)(2,1)S(1)} all-to-all(bf16[128,24,128]{2,1,0:T(8,128)(2,1)S(1)} %spectral.1), channel_id=1, replica_groups=mesh['ctx'=128,'ch'=2] {'ctx'}, dimensions={0} | all-to-all | bytes 1572864 | tf_op jit(solution)/shard_map/all_to_all | solution.py:222
  96.1 0.0 copy-start.4
  96.1 5.0 %finish.1 = (f32[128,1024]{1,0:T(8,128)S(1)}, f32[128,1024]{1,0:T(8,128)S(1)}, f32[128,1024]{1,0:T(8,128)S(1)}, f32[128,1024]{1,0:T(8,128)}, bf16[3,8,1024]{2,1,...) custom-call(s32[1]{0:T(128)} %bitcast.here, bf16[128,24,128]{2,1,0:T(8,128)(2,1)S(1)} %all_to_all.11.landed, ...), custom_call_target="tpu_custom_call" | custom-call | tf_op jit(solution)/shard_map/finish/pallas_call | solution.py:225
  101.1 0.0 collective-permute-start.3
  101.1 3.6 %collective-permute-start.2 = (bf16[3,8,1024]{2,1,0:T(8,128)(2,1)S(1)}, bf16[3,8,1024]{2,1,0:T(8,128)(2,1)S(1)}, u32[]{:S(2)}, u32[]{:S(2)}) collective-permute-start(bf16[3,8,1024]{2,1,0:T(8,128)(2,1)S(1)} %get-tuple-element.29), channel_id=1, source_target_pairs={{2,0},{4,2},{6,4},{8,6},{10,8},{12,10},{14,12},{16,14},{18,16},{20... | collective-permute-start | bytes 147464 | tf_op jit(solution)/shard_map/ppermute | solution.py:22
  104.7 6.6 %collective-permute-done.2.after = bf16[3,8,1024]{2,1,0:T(8,128)(2,1)S(1)} collective-permute-done((bf16[3,8,1024]{2,1,0:T(8,128)(2,1)S(1)}, bf16[3,8,1024]{2,1,0:T(8,128)(2,1)S(1)}, u32[]{:S(2)}, u32[]{:S(2)}) %collective-permute-start.2) | collective-permute-done | bytes 49184 | tf_op jit(solution)/shard_map/ppermute | solution.py:22
  111.4 0.0 collective-permute-done.3.other
  111.4 0.0 copy-done.4
  111.4 2.8 %close.1 = (bf16[128,1024]{1,0:T(8,128)(2,1)}, bf16[128,1024]{1,0:T(8,128)(2,1)}, bf16[128,1024]{1,0:T(8,128)(2,1)}, bf16[128,1024]{1,0:T(8,128)(2,1)}) custom-call(f32[128,1024]{1,0:T(8,128)S(1)} %get-tuple-element.26.gq, f32[128,1024]{1,0:T(8,128)S(1)} %get-tuple-element.27.gk, f32[128,1024]{1,0:T(8,128)S(1)} %get-tuple-element.28.gv, ...), custom_call_target="tpu_custom_call" | custom-call | tf_op jit(solution)/shard_map/close/pallas_call | solution.py:245
  (1 shorter events, 0.0 us)
Async XLA Ops:
  0.6 7.6 %collective-permute-start.1 = (bf16[128,1024]{1,0:T(8,128)(2,1)}, bf16[128,1024]{1,0:T(8,128)(2,1)S(1)}, u32[]{:S(2)}, u32[]{:S(2)}) collective-permute-start(bf16[128,1024]{1,0:T(8,128)(2,1)} %refs_6_.1), channel_id=1, source_target_pairs={{0,1},{1,0},{2,3},{3,2},{4,5},{5,4},{6,7},{7,6},{8,9},{9,8},{10,11... | collective-permute-start | bytes 786440 | tf_op jit(solution)/shard_map/ppermute | solution.py:183
  2.2 6.0 %collective-permute-start = (bf16[3,8,1024]{2,1,0:T(8,128)(2,1)S(1)}, bf16[3,8,1024]{2,1,0:T(8,128)(2,1)S(1)}, u32[]{:S(2)}, u32[]{:S(2)}) collective-permute-start(bf16[3,8,1024]{2,1,0:T(8,128)(2,1)S(1)} %pad_maximum_fusion), channel_id=1, source_target_pairs={{0,2},{2,4},{4,6},{6,8},{8,10},{10,12},{12,14},{14,16},{16,18},{18... | collective-permute-start | bytes 147464 | tf_op jit(solution)/shard_map/ppermute | solution.py:22
  8.2 1.0 copy-start
  9.3 0.9 copy-start.3
  10.2 0.9 copy-start.5
  11.1 0.9 copy-start.6
  12.1 0.9 copy-start.7
  13.0 0.9 copy-start.8
  14.0 42.4 %copy-start.1 = (bf16[768,256]{1,0:T(8,128)(2,1)S(1)}, bf16[768,256]{1,0:T(8,128)(2,1)}, u32[]{:S(2)}) copy-start(bf16[768,256]{1,0:T(8,128)(2,1)} %constant.16.clone.back) | copy-start | bytes 1179652
  14.0 42.4 %copy-start.2 = (bf16[768,256]{1,0:T(8,128)(2,1)S(1)}, bf16[768,256]{1,0:T(8,128)(2,1)}, u32[]{:S(2)}) copy-start(bf16[768,256]{1,0:T(8,128)(2,1)} %constant.15.clone.second) | copy-start | bytes 1179652
  14.0 42.4 %copy-start.9 = (bf16[128,768]{1,0:T(8,128)(2,1)S(1)}, bf16[128,768]{1,0:T(8,128)(2,1)}, u32[]{:S(2)}) copy-start(bf16[128,768]{1,0:T(8,128)(2,1)} %constant.17.clone.last) | copy-start | bytes 589828
  14.0 42.4 %copy-start.10 = (f32[2,128,128]{2,1,0:T(8,128)S(1)}, f32[2,128,128]{2,1,0:T(8,128)}, u32[]{:S(2)}) copy-start(f32[2,128,128]{2,1,0:T(8,128)} %constant.18.clone.twist) | copy-start | bytes 393220
  14.0 42.5 %copy-start.11 = (bf16[256,256]{1,0:T(8,128)(2,1)S(1)}, bf16[256,256]{1,0:T(8,128)(2,1)}, u32[]{:S(2)}) copy-start(bf16[256,256]{1,0:T(8,128)(2,1)} %constant.14.clone.first) | copy-start | bytes 393220
  96.1 15.3 %copy-start.4 = (f32[3,7,1024]{2,1,0:T(8,128)S(1)}, f32[3,7,1024]{2,1,0:T(8,128)}, u32[]{:S(2)}) copy-start(f32[3,7,1024]{2,1,0:T(8,128)} %taps.1) | copy-start | bytes 258052
  101.1 10.3 %collective-permute-start.3 = (bf16[128,1024]{1,0:T(8,128)(2,1)S(1)}, bf16[128,1024]{1,0:T(8,128)(2,1)S(1)}, u32[]{:S(2)}, u32[]{:S(2)}) collective-permute-start(bf16[128,1024]{1,0:T(8,128)(2,1)S(1)} %get-tuple-element.31), channel_id=1, source_target_pairs={{0,1},{1,0},{2,3},{3,2},{4,5},{5,4},{6,7},{7,6},{8,9},{9,8},{10,11... | collective-permute-start | bytes 786440 | tf_op jit(solution)/shard_map/ppermute | solution.py:238
  101.1 10.3 %collective-permute-start.2 = (bf16[3,8,1024]{2,1,0:T(8,128)(2,1)S(1)}, bf16[3,8,1024]{2,1,0:T(8,128)(2,1)S(1)}, u32[]{:S(2)}, u32[]{:S(2)}) collective-permute-start(bf16[3,8,1024]{2,1,0:T(8,128)(2,1)S(1)} %get-tuple-element.29), channel_id=1, source_target_pairs={{2,0},{4,2},{6,4},{8,6},{10,8},{12,10},{14,12},{16,14},{18,16},{20... | collective-permute-start | bytes 147464 | tf_op jit(solution)/shard_map/ppermute | solution.py:22

commit v2 on v1

v2 whole, which is shorter than its diff:
```python
import math

import jax
import jax.numpy as jnp
import ml_dtypes
import numpy as np
from jax import lax
from jax.experimental import pallas as pl
from jax.experimental.pallas import tpu as pltpu
from jax.sharding import PartitionSpec as P

f32 = jnp.float32
bf16 = jnp.bfloat16
EDGE = 8
TAIL = 16
WIDE = 256
VMEM_LIMIT = 24 * 1024 * 1024


def shifted(value, axis, steps):
    count = lax.axis_size(axis)
    first, last = (max(0, -steps), min(count, count - steps))
    return lax.ppermute(value, axis, [(source, source + steps) for source in range(first, last)])


def halves(table):
    high = table.astype(ml_dtypes.bfloat16)
    low = (table - high.astype(np.float64)).astype(ml_dtypes.bfloat16)
    return high, low


def ring_order(parts):
    length = math.gcd(parts, 8)
    ring = [place for place in (3, 1, 2, 7, 6, 0, 5, 4) if place < length]
    plane = parts // length
    return [place * plane + spot for spot in range(plane) for place in ring]


def tables(parts, rows, gain, order):
    freqs = np.arange(parts) + 0.5
    blocks = np.asarray(order)
    inner = np.arange(rows)
    outer = np.outer(freqs, blocks) * (-2.0 * math.pi / (2 * parts))
    turn = np.outer(freqs, inner) * (-2.0 * math.pi / (2 * parts * rows))
    small = np.outer(inner, inner) % rows * (-2.0 * math.pi / rows)
    first = halves(np.concatenate([np.cos(outer), np.sin(outer)], 0))
    first = np.concatenate(first, 1)
    c, s = np.cos(small), np.sin(small)
    high, low = halves(np.block([[c, s], [-s, c]]))
    second = np.concatenate([high, high, low], 0)
    high, low = halves(np.block([[c, -s], [s, c]]))
    back = np.concatenate([high, high, low], 0)
    high, low = halves(np.concatenate([np.cos(outer).T, np.sin(outer).T], 1) * gain)
    last = np.concatenate([high, high, low], 1)
    twist = np.stack([np.cos(turn), np.sin(turn)]).astype(np.float32)
    return first, second, back, last, twist


def split(value):
    high = value.astype(bf16)
    low = (value - high.astype(f32)).astype(bf16)
    return high, low


def tails_kernel(q, k, v, out, sems):
    rows = q.shape[0]
    copies = [
        pltpu.make_async_copy(x.at[pl.ds(rows - TAIL, TAIL), :], out.at[which], sems.at[which])
        for which, x in enumerate((q, k, v))
    ]
    for copy in copies:
        copy.start()
    for copy in copies:
        copy.wait()


ACROSS = (((1,), (1,)), ((), ()))


def fetch_kernel(
    here, q, k, v, filt, mine, w, taps_in, qs, ks, vs, gg, ft, wm, wo, taps, qb, kb, vb, fb, mb, pad, sems
):
    rows, width = q.shape
    half = w.shape[1] // 2
    me = here[0]
    w_mine = w.at[:, pl.ds(pl.multiple_of(me * half, half), half)]
    w_other = w.at[:, pl.ds(pl.multiple_of((1 - me) * half, half), half)]
    pairs = ((taps_in, taps), (q, qb), (k, kb), (v, vb), (filt, fb), (mine, mb), (w_mine, wm), (w_other, wo))
    copies = [pltpu.make_async_copy(src, dst, sems.at[i]) for i, (src, dst) in enumerate(pairs)]
    for copy in copies:
        copy.start()
    pad[0:EDGE, :] = jnp.zeros((EDGE, WIDE), f32)
    copies[0].wait()
    for which, (buf, out) in enumerate(((qb, qs), (kb, ks), (vb, vs))):
        copies[1 + which].wait()
        for first in range(0, width, WIDE):
            columns = slice(first, first + WIDE)
            pad[EDGE : EDGE + rows, :] = buf[:, columns].astype(f32)
            total = taps[which, 0:1, columns] * pad[EDGE : EDGE + rows, :]
            for shift in range(1, taps.shape[1]):
                moved = pad[EDGE - shift : EDGE - shift + rows, :]
                total = total + taps[which, shift : shift + 1, columns] * moved
            out[:, columns] = total
    copies[4].wait()
    for first in range(0, width, WIDE):
        ft[first : first + WIDE, :] = fb[:, first : first + WIDE].T
    copies[5].wait()
    copies[6].wait()
    for first in range(0, width, WIDE):
        part = slice(first, first + WIDE)
        gg[:, part] = lax.dot_general(mb[...], wm[part, :], ACROSS, preferred_element_type=f32)
    copies[7].wait()


def prepare_kernel(halo, taps, qs_in, ks_in, vs_in, gg_in, ft, other, wo, send, qs, ks, vs, gg, pad):
    rows, width = gg.shape
    parts, lines, _ = send.shape
    group = lines // 3
    pad[EDGE : 2 * EDGE, :] = jnp.zeros((EDGE, WIDE), f32)
    for first in range(0, width, WIDE):
        part = slice(first, first + WIDE)
        grad = gg_in[:, part] + lax.dot_general(other[...], wo[part, :], ACROSS, preferred_element_type=f32)
        gg[:, part] = grad
        shorts = []
        for which, (before, after) in enumerate(((qs_in, qs), (ks_in, ks), (vs_in, vs))):
            pad[0:EDGE, :] = halo[which, :, part].astype(f32)[TAIL - EDGE :, :]
            top = before[0:EDGE, part]
            for shift in range(1, taps.shape[1]):
                top = top + taps[which, shift : shift + 1, part] * pad[EDGE - shift : 2 * EDGE - shift, :]
            value = jnp.concatenate([top, before[EDGE:, part]], 0)
            after[:, part] = value
            shorts.append(value)
        mixed = (shorts[1] * shorts[2]).T
        grad_long = (grad * shorts[0]).T
        turned = [field.reshape(WIDE // group, group, rows) for field in (mixed, ft[part, :], grad_long)]
        send[first // group : (first + WIDE) // group] = jnp.concatenate(turned, axis=1).astype(bf16)


def spectral_kernel(x, first, second, back, last, twist, out, buf):
    parts, lines, rows = x.shape
    group = lines // 3
    buf[...] = x[...].astype(f32).reshape(parts * lines, rows)
    cos, sin = twist[0], twist[1]

    def dot(left, right):
        return jnp.dot(left, right, preferred_element_type=f32)

    def wide(value, table):
        high, low = split(value)
        return dot(jnp.concatenate([high, low, high], 1), table[...])

    for c in range(group):
        places = [pl.ds(f * group + c, parts, stride=lines) for f in range(3)]
        field = jnp.concatenate([buf[place, :] for place in places], 1).astype(bf16)
        half = dot(first[...], jnp.concatenate([field, field], 0))
        turned = []
        for f in range(3):
            re = half[:parts, f * rows : (f + 1) * rows]
            im = half[parts:, f * rows : (f + 1) * rows]
            turned.append(jnp.concatenate([re * cos - im * sin, re * sin + im * cos], 1))
        spec = wide(jnp.concatenate(turned, 0), second)
        (xr, xi), (kr, ki), (gr, gi) = [
            (spec[f * parts : (f + 1) * parts, :rows], spec[f * parts : (f + 1) * parts, rows:])
            for f in range(3)
        ]
        long_spec = jnp.concatenate([xr * kr - xi * ki, xr * ki + xi * kr], 1)
        mixed_spec = jnp.concatenate([kr * gr + ki * gi, kr * gi - ki * gr], 1)
        filter_spec = jnp.concatenate([xr * gr + xi * gi, xr * gi - xi * gr], 1)
        part = wide(jnp.concatenate([long_spec, mixed_spec, filter_spec], 0), back)
        turned = []
        for f in range(3):
            re = part[f * parts : (f + 1) * parts, :rows]
            im = part[f * parts : (f + 1) * parts, rows:]
            turned.append(jnp.concatenate([re * cos + im * sin, im * cos - re * sin], 0))
        high, low = split(jnp.concatenate(turned, 1))
        result = dot(last[...], jnp.concatenate([high, low, high], 0))
        for f in range(3):
            buf[places[f], :] = result[:, f * rows : (f + 1) * rows]
    out[...] = buf[...].reshape(parts, lines, rows).astype(bf16)


def gate_kernel(landed, qs, ks, vs, gg, wo, gq, gk, gv, heads, gated, other):
    rows, width = qs.shape
    parts, lines, _ = landed.shape
    group = lines // 3
    for first in range(0, width, WIDE):
        part = slice(first, first + WIDE)
        values = landed[first // group : (first + WIDE) // group].astype(f32)
        long_out, grad_mixed = [
            values[:, f * group : (f + 1) * group, :].reshape(WIDE, rows).T for f in range(2)
        ]
        gated[:, part] = (qs[:, part] * long_out).astype(bf16)
        for which, (to, value) in enumerate(
            (
                (gq, gg[:, part] * long_out),
                (gk, grad_mixed * vs[:, part]),
                (gv, grad_mixed * ks[:, part]),
            )
        ):
            to[:, part] = value
            heads[which, :, part] = value[:TAIL, :].astype(bf16)
    for first in range(0, width, WIDE):
        part = slice(first, first + WIDE)
        other[:, part] = jnp.dot(gated[...], wo[:, part], preferred_element_type=f32)


def project_kernel(landed, gated, wm, gf, mine):
    rows, width = gated.shape
    parts, lines, _ = landed.shape
    group = lines // 3
    for first in range(0, width, WIDE):
        part = slice(first, first + WIDE)
        mine[:, part] = jnp.dot(gated[...], wm[:, part], preferred_element_type=f32)
        values = landed[first // group : (first + WIDE) // group].astype(f32)
        gf[:, part] = values[:, 2 * group :, :].reshape(WIDE, rows).T


def close_kernel(gq, gk, gv, after, taps, mine, other, block_out, oq, ok, ov, pad):
    rows, width = gq.shape
    for which, (value, to) in enumerate(((gq, oq), (gk, ok), (gv, ov))):
        pad[0:rows, :] = value[...]
        pad[rows : rows + EDGE, :] = after[which].astype(f32)[:EDGE, :]
        total = taps[which, 0:1, :] * pad[0:rows, :]
        for shift in range(1, taps.shape[1]):
            total = total + taps[which, shift : shift + 1, :] * pad[shift : shift + rows, :]
        to[...] = total.astype(bf16)
    block_out[...] = (mine[...] + other[...]).astype(bf16)


def on_device(query_in, key_in, value_in, taps, long_filter, out_weight, out_grad):
    rows, width = query_in.shape
    parts = lax.axis_size("ctx")
    seq_total = parts * rows
    group = width // parts
    lines = 3 * group
    reach = taps.shape[1]
    outs = out_weight.shape[1]
    here = lax.axis_index("ch").astype(jnp.int32).reshape(1)
    gain = 1.0 / math.sqrt(seq_total) / seq_total
    swap = [(0, 1), (1, 0)]
    order = ring_order(parts)

    params = pltpu.CompilerParams(vmem_limit_bytes=VMEM_LIMIT)
    vmem = pl.BlockSpec(memory_space=pltpu.VMEM)
    hbm = pl.BlockSpec(memory_space=pltpu.HBM)
    smem = pl.BlockSpec(memory_space=pltpu.SMEM)
    flat = jax.ShapeDtypeStruct((rows, width), f32)
    half = jax.ShapeDtypeStruct((rows, width), bf16)
    fields = jax.ShapeDtypeStruct((parts, lines, rows), bf16)
    edges = jax.ShapeDtypeStruct((3, TAIL, width), bf16)
    weights = jax.ShapeDtypeStruct((width, outs // 2), bf16)
    cost = pl.CostEstimate(flops=2 * rows * width * outs, bytes_accessed=8 * 2**20, transcendentals=0)

    grad_other = lax.ppermute(out_grad, "ch", swap)
    far = [
        pltpu.with_memory_space_constraint(x, pltpu.HBM)
        for x in (query_in, key_in, value_in, long_filter, out_grad, out_weight, taps)
    ]
    with jax.named_scope("tails"):
        tails = pl.pallas_call(
            tails_kernel,
            in_specs=[hbm] * 3,
            out_specs=vmem,
            out_shape=edges,
            scratch_shapes=[pltpu.SemaphoreType.DMA((3,))],
            compiler_params=params,
        )(*far[:3])
    halo = shifted(tails, "ctx", 1)

    with jax.named_scope("fetch"):
        qs, ks, vs, gg, ft, wm, wo, taps_near = pl.pallas_call(
            fetch_kernel,
            in_specs=[smem] + [hbm] * 7,
            out_specs=[vmem] * 8,
            out_shape=[
                flat,
                flat,
                flat,
                flat,
                jax.ShapeDtypeStruct((width, rows), f32),
                weights,
                weights,
                jax.ShapeDtypeStruct(taps.shape, f32),
            ],
            scratch_shapes=[
                pltpu.VMEM((rows, width), bf16),
                pltpu.VMEM((rows, width), bf16),
                pltpu.VMEM((rows, width), bf16),
                pltpu.VMEM((rows, width), f32),
                pltpu.VMEM((rows, width), bf16),
                pltpu.VMEM((rows + EDGE, WIDE), f32),
                pltpu.SemaphoreType.DMA((8,)),
            ],
            compiler_params=params,
            cost_estimate=cost,
        )(here, *far)

    with jax.named_scope("prepare"):
        send, qs, ks, vs, gg = pl.pallas_call(
            prepare_kernel,
            in_specs=[vmem] * 9,
            out_specs=[vmem] * 5,
            out_shape=[fields, flat, flat, flat, flat],
            scratch_shapes=[pltpu.VMEM((2 * EDGE, WIDE), f32)],
            compiler_params=params,
        )(halo, taps_near, qs, ks, vs, gg, ft, grad_other, wo)

    arrived = lax.all_to_all(
        send, "ctx", split_axis=0, concat_axis=0, tiled=True, axis_index_groups=[order]
    )

    with jax.named_scope("spectral"):
        solved = pl.pallas_call(
            spectral_kernel,
            out_shape=fields,
            scratch_shapes=[pltpu.VMEM((parts * lines, rows), f32)],
            compiler_params=params,
        )(arrived, *tables(parts, rows, gain, order))

    landed = lax.all_to_all(
        solved, "ctx", split_axis=0, concat_axis=0, tiled=True, axis_index_groups=[order]
    )

    with jax.named_scope("gate"):
        gq, gk, gv, heads, gated, other = pl.pallas_call(
            gate_kernel,
            in_specs=[vmem] * 6,
            out_specs=[vmem] * 6,
            out_shape=[flat, flat, flat, edges, half, flat],
            compiler_params=params,
        )(landed, qs, ks, vs, gg, wo)

    after = shifted(heads, "ctx", -1)
    theirs = lax.ppermute(other, "ch", swap)

    with jax.named_scope("project"):
        grad_filter, mine = pl.pallas_call(
            project_kernel,
            in_specs=[vmem] * 3,
            out_specs=[vmem] * 2,
            out_shape=[flat, flat],
            compiler_params=params,
            cost_estimate=cost,
        )(landed, gated, wm)

    with jax.named_scope("close"):
        column = pl.BlockSpec((rows, WIDE), lambda i: (0, i))
        edge = pl.BlockSpec((3, TAIL, WIDE), lambda i: (0, 0, i))
        taps_spec = pl.BlockSpec((3, reach, WIDE), lambda i: (0, 0, i))
        block_out, grad_query, grad_key, grad_value = pl.pallas_call(
            close_kernel,
            grid=(width // WIDE,),
            in_specs=[column] * 3 + [edge, taps_spec, column, column],
            out_specs=[column] * 4,
            out_shape=[half] * 4,
            scratch_shapes=[pltpu.VMEM((rows + EDGE, WIDE), f32)],
            compiler_params=params,
        )(gq, gk, gv, after, taps_near, mine, theirs)
    return (block_out, grad_query, grad_key, grad_value, grad_filter)


def solution(mesh):
    return jax.shard_map(
        on_device,
        mesh=mesh,
        in_specs=(
            P("ctx", "ch"),
            P("ctx", "ch"),
            P("ctx", "ch"),
            P(None, None, "ch"),
            P("ctx", "ch"),
            P("ch", None),
            P("ctx", "ch"),
        ),
        out_specs=(P("ctx", "ch"), P("ctx", "ch"), P("ctx", "ch"), P("ctx", "ch"), P("ctx", "ch")),
        check_vma=False,
    )
```

time: 116 us -> 101 us (0.87); the launches traced: 114 us -> 101 us
  local copies, waits for them, and re-layouts: 7.22 us -> 0.03 us
  Pallas kernels: 22.1 us -> 18.7 us
  waiting for transfers between devices: 9.23 us -> 7.47 us
    unnamed x24 -> x10, local copies, waits for them, and re-layouts: 5.76 us -> 0.03 us
    pallas_call x3 -> x6, Pallas kernels: 13.3 us -> 9.98 us  [the longest x1 3.67 us: on_device(): pl.pallas_call(fetch_kernel, in_specs=[smem] + [hbm] * 7, out_specs=[vmem...]
    ppermute x2, waiting for transfers between devices: 9.23 us -> 7.47 us  [shifted(): lax.ppermute(value, axis, [(source, source + steps) for source in range(f...]
    another operation x2 -> x0, local copies, waits for them, and re-layouts: 1.46 us -> none  [on_device(): jnp.stack([query_in[rows - EDGE:], key_in[rows - EDGE:], value_in[rows -...]
  transfers between devices with their start and end apart: 4 -> 4, of which waited for: 2 -> 1; matrix products, arithmetic and copies ran while one was open for 1% -> 0% of each run, Pallas kernels for 0% -> 6%
where the time goes in v2:
time: 101 us
  blocking collectives  67.3 us (67%)
  Pallas kernels  18.7 us (19%)
  waiting for transfers between devices  7.47 us (7%)
  starting transfers between devices  6.23 us (6%)
    all_to_all x1, blocking collectives, on_device(): lax.all_to_all(send, 'ctx', split_axis=0, concat_axis=0, tiled=True, axis...  36.8 us
    all_to_all x1, blocking collectives, on_device(): lax.all_to_all(solved, 'ctx', split_axis=0, concat_axis=0, tiled=True, ax...  30.5 us
    pallas_call x1, Pallas kernels, on_device(): pl.pallas_call(spectral_kernel, out_shape=fields, scratch_shapes=[pltpu.V...  8.77 us
    ppermute x2, waiting for transfers between devices, shifted(): lax.ppermute(value, axis, [(source, source + steps) for source in range(f...  7.47 us
    ppermute x2, starting transfers between devices, shifted(): lax.ppermute(value, axis, [(source, source + steps) for source in range(f...  6.04 us
    pallas_call x1, Pallas kernels, on_device(): pl.pallas_call(fetch_kernel, in_specs=[smem] + [hbm] * 7, out_specs=[vmem...  3.67 us
    pallas_call x1, Pallas kernels, on_device(): pl.pallas_call(close_kernel, grid=(width // WIDE,), in_specs=[column] * 3...  2.77 us
  transfers between devices with their start and end apart: 4, of which 1 were waited for; matrix products, arithmetic and copies ran while one was open for 0% of the time, Pallas kernels for 6%

profile of v2, /device:TPU:30, one launch (start us, length us, event | category | flops | bytes accessed | tf_op | source)
XLA Modules:
  0.0 100.5 jit_solution(14843036887569559605)
XLA Ops:
  0.6 0.1 collective-permute-start.1
  0.7 0.8 tails.1
  1.6 3.4 %collective-permute-start = (bf16[3,16,1024]{2,1,0:T(8,128)(2,1)S(1)}, bf16[3,16,1024]{2,1,0:T(8,128)(2,1)S(1)}, u32[]{:S(2)}, u32[]{:S(2)}) collective-permute-start(bf16[3,16,1024]{2,1,0:T(8,128)(2,1)S(1)} %tails.1), channel_id=1, source_target_pairs={{0,2},{2,4},{4,6},{6,8},{8,10},{10,12},{12,14},{14,16},{16,18},{18... | collective-permute-start | bytes 294920 | tf_op jit(solution)/shard_map/ppermute | solution.py:23
  5.0 3.7 %fetch.1 = (f32[128,1024]{1,0:T(8,128)S(1)}, f32[128,1024]{1,0:T(8,128)S(1)}, f32[128,1024]{1,0:T(8,128)S(1)}, f32[128,1024]{1,0:T(8,128)S(1)}, f32[1024,128]{1,...) custom-call(s32[1]{0:T(128)} %bitcast.here, ...), custom_call_target="tpu_custom_call" | custom-call | flops 536870912 | bytes 8388608 | tf_op jit(solution)/shard_map/fetch/pallas_call | solution.py:271
  8.7 0.0 collective-permute-done.halo
  8.7 0.0 collective-permute-done.1.other
  8.7 0.0 copy-start
  8.7 0.0 copy-start.1
  8.7 0.0 copy-start.2
  8.7 0.0 copy-start.3
  8.7 0.0 copy-start.4
  8.7 1.0 %prepare.1 = (bf16[128,24,128]{2,1,0:T(8,128)(2,1)S(1)}, f32[128,1024]{1,0:T(8,128)S(1)}, f32[128,1024]{1,0:T(8,128)S(1)}, f32[128,1024]{1,0:T(8,128)S(1)}, f32[128,1024]{1,0:T(8,128)S(1)}) custom-call(bf16[3,16,1024]{2,1,0:T(8,128)(2,1)S(1)} %collective-permute-done.halo, f32[3,7,1024]{2,1,0:T(8,128)S(1)} %get-tuple-element.30.taps, ...), custom_call_target="tpu_custom_call" | custom-call | tf_op jit(solution)/shard_map/prepare/pallas_call | solution.py:299
  9.8 36.8 %all_to_all.10.x = bf16[128,24,128]{2,1,0:T(8,128)(2,1)S(1)} all-to-all(bf16[128,24,128]{2,1,0:T(8,128)(2,1)S(1)} %get-tuple-element.37), channel_id=1, replica_groups={{96,32,64,224,192,0,160,128,98,34,66,226,194,2,162,130,100,36,68,228,19..., dimensions={0} | all-to-all | bytes 1572864 | tf_op jit(solution)/shard_map/all_to_all | solution.py:308
  46.6 0.0 copy-done
  46.6 0.0 copy-done.1
  46.6 0.0 copy-done.2
  46.6 0.0 copy-done.3
  46.6 0.0 copy-done.4
  46.6 8.8 %spectral.1 = bf16[128,24,128]{2,1,0:T(8,128)(2,1)S(1)} custom-call(bf16[128,24,128]{2,1,0:T(8,128)(2,1)S(1)} %all_to_all.10.x, bf16[256,256]{1,0:T(8,128)(2,1)S(1)} %copy-done.4, bf16[768,256]{1,0:T(8,128)(2,1)S(1)} %copy-done.1, bf16[768,256]{1,0:T(8,128)(2,1)S(1)} %copy-done, bf16[128,768]{1,0:T(8,128)(2,1)S(1)} %copy-done.2, f32[2,128,128]{2,1,0:T(8,128)S(1)} %copy-done.3), custom_call_target="tpu_custom_call" | custom-call | tf_op jit(solution)/shard_map/spectral/pallas_call | solution.py:313
  55.4 30.5 %all_to_all.11.landed = bf16[128,24,128]{2,1,0:T(8,128)(2,1)S(1)} all-to-all(bf16[128,24,128]{2,1,0:T(8,128)(2,1)S(1)} %spectral.1), channel_id=1, replica_groups={{96,32,64,224,192,0,160,128,98,34,66,226,194,2,162,130,100,36,68,228,19..., dimensions={0} | all-to-all | bytes 1572864 | tf_op jit(solution)/shard_map/all_to_all | solution.py:320
  85.9 0.5 gate.1
  86.4 0.1 collective-permute-start.3
  86.5 2.6 %collective-permute-start.2 = (bf16[3,16,1024]{2,1,0:T(8,128)(2,1)S(1)}, bf16[3,16,1024]{2,1,0:T(8,128)(2,1)S(1)}, u32[]{:S(2)}, u32[]{:S(2)}) collective-permute-start(bf16[3,16,1024]{2,1,0:T(8,128)(2,1)S(1)} %get-tuple-element.45), channel_id=1, source_target_pairs={{2,0},{4,2},{6,4},{8,6},{10,8},{12,10},{14,12},{16,14},{18,16},{20... | collective-permute-start | bytes 294920 | tf_op jit(solution)/shard_map/ppermute | solution.py:23
  89.1 1.2 %project.1 = (f32[128,1024]{1,0:T(8,128)}, f32[128,1024]{1,0:T(8,128)S(1)}) custom-call(bf16[128,24,128]{2,1,0:T(8,128)(2,1)S(1)} %all_to_all.11.landed, bf16[128,1024]{1,0:T(8,128)(2,1)S(1)} %get-tuple-element.46.gated, bf16[1024,1024]{1,0:T(8,128)(2,1)S(1)} %get-tuple-element.47.wm), custom_call_target="tpu_custom_call" | custom-call | flops 536870912 | bytes 8388608 | tf_op jit(solution)/shard_map/project/pallas_call | solution.py:337
  90.3 7.5 %collective-permute-done.2.after = bf16[3,16,1024]{2,1,0:T(8,128)(2,1)S(1)} collective-permute-done((bf16[3,16,1024]{2,1,0:T(8,128)(2,1)S(1)}, bf16[3,16,1024]{2,1,0:T(8,128)(2,1)S(1)}, u32[]{:S(2)}, u32[]{:S(2)}) %collective-permute-start.2) | collective-permute-done | bytes 98336 | tf_op jit(solution)/shard_map/ppermute | solution.py:23
  97.8 0.0 collective-permute-done.3.other
  97.8 2.8 %close.1 = (bf16[128,1024]{1,0:T(8,128)(2,1)}, bf16[128,1024]{1,0:T(8,128)(2,1)}, bf16[128,1024]{1,0:T(8,128)(2,1)}, bf16[128,1024]{1,0:T(8,128)(2,1)}) custom-call(f32[128,1024]{1,0:T(8,128)S(1)} %get-tuple-element.42.gq, f32[128,1024]{1,0:T(8,128)S(1)} %get-tuple-element.43.gk, f32[128,1024]{1,0:T(8,128)S(1)} %get-tuple-element.44.gv, ...), custom_call_target="tpu_custom_call" | custom-call | tf_op jit(solution)/shard_map/close/pallas_call | solution.py:350
Async XLA Ops:
  0.6 8.0 %collective-permute-start.1 = (bf16[128,1024]{1,0:T(8,128)(2,1)}, bf16[128,1024]{1,0:T(8,128)(2,1)S(1)}, u32[]{:S(2)}, u32[]{:S(2)}) collective-permute-start(bf16[128,1024]{1,0:T(8,128)(2,1)} %mine.1), channel_id=1, source_target_pairs={{0,1},{1,0},{2,3},{3,2},{4,5},{5,4},{6,7},{7,6},{8,9},{9,8},{10,11... | collective-permute-start | bytes 786440 | tf_op jit(solution)/shard_map/ppermute | solution.py:254
  1.6 7.1 %collective-permute-start = (bf16[3,16,1024]{2,1,0:T(8,128)(2,1)S(1)}, bf16[3,16,1024]{2,1,0:T(8,128)(2,1)S(1)}, u32[]{:S(2)}, u32[]{:S(2)}) collective-permute-start(bf16[3,16,1024]{2,1,0:T(8,128)(2,1)S(1)} %tails.1), channel_id=1, source_target_pairs={{0,2},{2,4},{4,6},{6,8},{8,10},{10,12},{12,14},{14,16},{16,18},{18... | collective-permute-start | bytes 294920 | tf_op jit(solution)/shard_map/ppermute | solution.py:23
  8.7 37.9 %copy-start = (bf16[768,256]{1,0:T(8,128)(2,1)S(1)}, bf16[768,256]{1,0:T(8,128)(2,1)}, u32[]{:S(2)}) copy-start(bf16[768,256]{1,0:T(8,128)(2,1)} %constant.16.clone.back) | copy-start | bytes 1179652
  8.7 37.9 %copy-start.1 = (bf16[768,256]{1,0:T(8,128)(2,1)S(1)}, bf16[768,256]{1,0:T(8,128)(2,1)}, u32[]{:S(2)}) copy-start(bf16[768,256]{1,0:T(8,128)(2,1)} %constant.15.clone.second) | copy-start | bytes 1179652
  8.7 37.9 %copy-start.2 = (bf16[128,768]{1,0:T(8,128)(2,1)S(1)}, bf16[128,768]{1,0:T(8,128)(2,1)}, u32[]{:S(2)}) copy-start(bf16[128,768]{1,0:T(8,128)(2,1)} %constant.17.clone.last) | copy-start | bytes 589828
  8.7 37.9 %copy-start.3 = (f32[2,128,128]{2,1,0:T(8,128)S(1)}, f32[2,128,128]{2,1,0:T(8,128)}, u32[]{:S(2)}) copy-start(f32[2,128,128]{2,1,0:T(8,128)} %constant.18.clone.twist) | copy-start | bytes 393220
  8.7 37.9 %copy-start.4 = (bf16[256,256]{1,0:T(8,128)(2,1)S(1)}, bf16[256,256]{1,0:T(8,128)(2,1)}, u32[]{:S(2)}) copy-start(bf16[256,256]{1,0:T(8,128)(2,1)} %constant.14.clone.first) | copy-start | bytes 393220
  86.4 11.4 %collective-permute-start.3 = (f32[128,1024]{1,0:T(8,128)S(1)}, f32[128,1024]{1,0:T(8,128)S(1)}, u32[]{:S(2)}, u32[]{:S(2)}) collective-permute-start(f32[128,1024]{1,0:T(8,128)S(1)} %get-tuple-element.49), channel_id=1, source_target_pairs={{0,1},{1,0},{2,3},{3,2},{4,5},{5,4},{6,7},{7,6},{8,9},{9,8},{10,11... | collective-permute-start | bytes 1572872 | tf_op jit(solution)/shard_map/ppermute | solution.py:334
  86.5 11.3 %collective-permute-start.2 = (bf16[3,16,1024]{2,1,0:T(8,128)(2,1)S(1)}, bf16[3,16,1024]{2,1,0:T(8,128)(2,1)S(1)}, u32[]{:S(2)}, u32[]{:S(2)}) collective-permute-start(bf16[3,16,1024]{2,1,0:T(8,128)(2,1)S(1)} %get-tuple-element.45), channel_id=1, source_target_pairs={{2,0},{4,2},{6,4},{8,6},{10,8},{12,10},{14,12},{16,14},{18,16},{20... | collective-permute-start | bytes 294920 | tf_op jit(solution)/shard_map/ppermute | solution.py:23

commit v3 on v2

--- a/solution.py
+++ b/solution.py
@@ -31,7 +31,7 @@
 
 def ring_order(parts):
     length = math.gcd(parts, 8)
-    ring = [place for place in (3, 1, 2, 7, 6, 0, 5, 4) if place < length]
+    ring = [place for place in (0, 4, 2, 6, 1, 5, 3, 7) if place < length]
     plane = parts // length
     return [place * plane + spot for spot in range(plane) for place in ring]
 
@@ -47,11 +47,11 @@
     first = np.concatenate(first, 1)
     c, s = np.cos(small), np.sin(small)
     high, low = halves(np.block([[c, s], [-s, c]]))
-    second = np.concatenate([high, high, low], 0)
+    second = np.stack([high, low])
     high, low = halves(np.block([[c, -s], [s, c]]))
-    back = np.concatenate([high, high, low], 0)
+    back = np.stack([high, low])
     high, low = halves(np.concatenate([np.cos(outer).T, np.sin(outer).T], 1) * gain)
-    last = np.concatenate([high, high, low], 1)
+    last = np.concatenate([high, low], 0)
     twist = np.stack([np.cos(turn), np.sin(turn)]).astype(np.float32)
     return first, second, back, last, twist
 
@@ -136,6 +136,9 @@
         send[first // group : (first + WIDE) // group] = jnp.concatenate(turned, axis=1).astype(bf16)
 
 
+BATCH = 4
+
+
 def spectral_kernel(x, first, second, back, last, twist, out, buf):
     parts, lines, rows = x.shape
     group = lines // 3
@@ -147,35 +150,46 @@
 
     def wide(value, table):
         high, low = split(value)
-        return dot(jnp.concatenate([high, low, high], 1), table[...])
-
-    for c in range(group):
-        places = [pl.ds(f * group + c, parts, stride=lines) for f in range(3)]
-        field = jnp.concatenate([buf[place, :] for place in places], 1).astype(bf16)
-        half = dot(first[...], jnp.concatenate([field, field], 0))
+        count = value.shape[0]
+        both = dot(jnp.concatenate([high, low], 0), table[0])
+        return both[:count] + both[count:] + dot(high, table[1])
+
+    def spot(f, c):
+        return pl.ds(f * group + c, parts, stride=lines)
+
+    for base in range(0, group, BATCH):
+        lanes = range(base, min(base + BATCH, group))
         turned = []
-        for f in range(3):
-            re = half[:parts, f * rows : (f + 1) * rows]
-            im = half[parts:, f * rows : (f + 1) * rows]
-            turned.append(jnp.concatenate([re * cos - im * sin, re * sin + im * cos], 1))
+        for c in lanes:
+            field = jnp.concatenate([buf[spot(f, c), :] for f in range(3)], 1).astype(bf16)
+            half = dot(first[...], jnp.concatenate([field, field], 0))
+            for f in range(3):
+                re = half[:parts, f * rows : (f + 1) * rows]
+                im = half[parts:, f * rows : (f + 1) * rows]
+                turned.append(jnp.concatenate([re * cos - im * sin, re * sin + im * cos], 1))
         spec = wide(jnp.concatenate(turned, 0), second)
-        (xr, xi), (kr, ki), (gr, gi) = [
-            (spec[f * parts : (f + 1) * parts, :rows], spec[f * parts : (f + 1) * parts, rows:])
-            for f in range(3)
-        ]
-        long_spec = jnp.concatenate([xr * kr - xi * ki, xr * ki + xi * kr], 1)
-        mixed_spec = jnp.concatenate([kr * gr + ki * gi, kr * gi - ki * gr], 1)
-        filter_spec = jnp.concatenate([xr * gr + xi * gi, xr * gi - xi * gr], 1)
-        part = wide(jnp.concatenate([long_spec, mixed_spec, filter_spec], 0), back)
+        solved = []
+        for i in range(len(lanes)):
+            (xr, xi), (kr, ki), (gr, gi) = [
+                (spec[f * parts : (f + 1) * parts, :rows], spec[f * parts : (f + 1) * parts, rows:])
+                for f in range(3 * i, 3 * i + 3)
+            ]
+            solved.append(jnp.concatenate([xr * kr - xi * ki, xr * ki + xi * kr], 1))
+            solved.append(jnp.concatenate([kr * gr + ki * gi, kr * gi - ki * gr], 1))
+            solved.append(jnp.concatenate([xr * gr + xi * gi, xr * gi - xi * gr], 1))
+        part = wide(jnp.concatenate(solved, 0), back)
         turned = []
-        for f in range(3):
+        for f in range(3 * len(lanes)):
             re = part[f * parts : (f + 1) * parts, :rows]
             im = part[f * parts : (f + 1) * parts, rows:]
             turned.append(jnp.concatenate([re * cos + im * sin, im * cos - re * sin], 0))
         high, low = split(jnp.concatenate(turned, 1))
-        result = dot(last[...], jnp.concatenate([high, low, high], 0))
-        for f in range(3):
-            buf[places[f], :] = result[:, f * rows : (f + 1) * rows]
+        both = dot(last[...], high)
+        result = both[:parts] + both[parts:] + dot(last[:parts, :], low)
+        for i, c in enumerate(lanes):
+            for f in range(3):
+                place = (3 * i + f) * rows
+                buf[spot(f, c), :] = result[:, place : place + rows]
     out[...] = buf[...].reshape(parts, lines, rows).astype(bf16)
 
 
@@ -204,26 +218,33 @@
         other[:, part] = jnp.dot(gated[...], wo[:, part], preferred_element_type=f32)
 
 
-def project_kernel(landed, gated, wm, gf, mine):
+def project_kernel(landed, gated, wm, gq, gk, gv, taps, gf, mine, tq, tk, tv, pad):
     rows, width = gated.shape
     parts, lines, _ = landed.shape
     group = lines // 3
+    pad[rows : rows + EDGE, :] = jnp.zeros((EDGE, WIDE), f32)
     for first in range(0, width, WIDE):
         part = slice(first, first + WIDE)
         mine[:, part] = jnp.dot(gated[...], wm[:, part], preferred_element_type=f32)
         values = landed[first // group : (first + WIDE) // group].astype(f32)
         gf[:, part] = values[:, 2 * group :, :].reshape(WIDE, rows).T
-
-
-def close_kernel(gq, gk, gv, after, taps, mine, other, block_out, oq, ok, ov, pad):
-    rows, width = gq.shape
-    for which, (value, to) in enumerate(((gq, oq), (gk, ok), (gv, ov))):
-        pad[0:rows, :] = value[...]
-        pad[rows : rows + EDGE, :] = after[which].astype(f32)[:EDGE, :]
-        total = taps[which, 0:1, :] * pad[0:rows, :]
+        for which, (value, to) in enumerate(((gq, tq), (gk, tk), (gv, tv))):
+            pad[0:rows, :] = value[:, part]
+            total = taps[which, 0:1, part] * value[:, part]
+            for shift in range(1, taps.shape[1]):
+                total = total + taps[which, shift : shift + 1, part] * pad[shift : shift + rows, :]
+            to[:, part] = total
+
+
+def close_kernel(tq, tk, tv, after, taps, mine, other, block_out, oq, ok, ov, pad):
+    rows, width = tq.shape
+    pad[0:EDGE, :] = jnp.zeros((EDGE, width), f32)
+    for which, (value, to) in enumerate(((tq, oq), (tk, ok), (tv, ov))):
+        pad[EDGE : 2 * EDGE, :] = after[which].astype(f32)[:EDGE, :]
+        end = value[rows - EDGE :, :]
         for shift in range(1, taps.shape[1]):
-            total = total + taps[which, shift : shift + 1, :] * pad[shift : shift + rows, :]
-        to[...] = total.astype(bf16)
+            end = end + taps[which, shift : shift + 1, :] * pad[shift : shift + EDGE, :]
+        to[...] = jnp.concatenate([value[: rows - EDGE, :], end], 0).astype(bf16)
     block_out[...] = (mine[...] + other[...]).astype(bf16)
 
 
@@ -334,14 +355,15 @@
     theirs = lax.ppermute(other, "ch", swap)
 
     with jax.named_scope("project"):
-        grad_filter, mine = pl.pallas_call(
+        grad_filter, mine, tq, tk, tv = pl.pallas_call(
             project_kernel,
-            in_specs=[vmem] * 3,
-            out_specs=[vmem] * 2,
-            out_shape=[flat, flat],
+            in_specs=[vmem] * 7,
+            out_specs=[vmem] * 5,
+            out_shape=[flat] * 5,
+            scratch_shapes=[pltpu.VMEM((rows + EDGE, WIDE), f32)],
             compiler_params=params,
             cost_estimate=cost,
-        )(landed, gated, wm)
+        )(landed, gated, wm, gq, gk, gv, taps_near)
 
     with jax.named_scope("close"):
         column = pl.BlockSpec((rows, WIDE), lambda i: (0, i))
@@ -353,9 +375,9 @@
             in_specs=[column] * 3 + [edge, taps_spec, column, column],
             out_specs=[column] * 4,
             out_shape=[half] * 4,
-            scratch_shapes=[pltpu.VMEM((rows + EDGE, WIDE), f32)],
-            compiler_params=params,
-        )(gq, gk, gv, after, taps_near, mine, theirs)
+            scratch_shapes=[pltpu.VMEM((2 * EDGE, WIDE), f32)],
+            compiler_params=params,
+        )(tq, tk, tv, after, taps_near, mine, theirs)
     return (block_out, grad_query, grad_key, grad_value, grad_filter)
 
 

time: 101 us -> 98.3 us (0.973)
  Pallas kernels: 18.7 us -> 16.3 us
    pallas_call x1, Pallas kernels: 8.77 us -> 6.13 us  [on_device(): pl.pallas_call(spectral_kernel, out_shape=fields, scratch_shapes=[pltpu.V...]
    pallas_call x1, Pallas kernels: 1.18 us -> 2.37 us  [on_device(): pl.pallas_call(project_kernel, in_specs=[vmem] * 7, out_specs=[vmem] * 5,...]
  transfers between devices with their start and end apart: 4 -> 4, of which waited for: 1 -> 1; matrix products, arithmetic and copies ran while one was open for 0% -> 0% of each run, Pallas kernels for 6% -> 7%
where the time goes in v3:
time: 98.3 us; the launch traced here: 98 us
  blocking collectives  68.3 us (69%)
  Pallas kernels  16.3 us (17%)
  waiting for transfers between devices  7.01 us (7%)
  starting transfers between devices  5.51 us (6%)
    all_to_all x1, blocking collectives, on_device(): lax.all_to_all(send, 'ctx', split_axis=0, concat_axis=0, tiled=True, axis...  37.8 us
    all_to_all x1, blocking collectives, on_device(): lax.all_to_all(solved, 'ctx', split_axis=0, concat_axis=0, tiled=True, ax...  30.5 us
    ppermute x2, waiting for transfers between devices, shifted(): lax.ppermute(value, axis, [(source, source + steps) for source in range(f...  7 us
    pallas_call x1, Pallas kernels, on_device(): pl.pallas_call(spectral_kernel, out_shape=fields, scratch_shapes=[pltpu.V...  6.13 us
    ppermute x2, starting transfers between devices, shifted(): lax.ppermute(value, axis, [(source, source + steps) for source in range(f...  5.32 us
    pallas_call x1, Pallas kernels, on_device(): pl.pallas_call(fetch_kernel, in_specs=[smem] + [hbm] * 7, out_specs=[vmem...  3.67 us
    pallas_call x1, Pallas kernels, on_device(): pl.pallas_call(project_kernel, in_specs=[vmem] * 7, out_specs=[vmem] * 5,...  2.37 us
  transfers between devices with their start and end apart: 4, of which 1 were waited for; matrix products, arithmetic and copies ran while one was open for 0% of the time, Pallas kernels for 7%

profile of v3, /device:TPU:30, one launch (start us, length us, event | category | flops | bytes accessed | tf_op | source)
XLA Modules:
  0.0 98.0 jit_solution(18108820487946563648)
XLA Ops:
  0.6 0.1 collective-permute-start.1
  0.7 0.8 tails.1
  1.6 3.4 %collective-permute-start = (bf16[3,16,1024]{2,1,0:T(8,128)(2,1)S(1)}, bf16[3,16,1024]{2,1,0:T(8,128)(2,1)S(1)}, u32[]{:S(2)}, u32[]{:S(2)}) collective-permute-start(bf16[3,16,1024]{2,1,0:T(8,128)(2,1)S(1)} %tails.1), channel_id=1, source_target_pairs={{0,2},{2,4},{4,6},{6,8},{8,10},{10,12},{12,14},{14,16},{16,18},{18... | collective-permute-start | bytes 294920 | tf_op jit(solution)/shard_map/ppermute | solution.py:23
  5.0 3.7 %fetch.1 = (f32[128,1024]{1,0:T(8,128)S(1)}, f32[128,1024]{1,0:T(8,128)S(1)}, f32[128,1024]{1,0:T(8,128)S(1)}, f32[128,1024]{1,0:T(8,128)S(1)}, f32[1024,128]{1,...) custom-call(s32[1]{0:T(128)} %bitcast.here, ...), custom_call_target="tpu_custom_call" | custom-call | flops 536870912 | bytes 8388608 | tf_op jit(solution)/shard_map/fetch/pallas_call | solution.py:292
  8.7 0.0 collective-permute-done.halo
  8.7 0.0 collective-permute-done.1.other
  8.7 0.0 copy-start
  8.7 0.0 copy-start.1
  8.7 0.0 copy-start.2
  8.7 0.0 copy-start.3
  8.7 0.0 copy-start.4
  8.7 1.0 %prepare.1 = (bf16[128,24,128]{2,1,0:T(8,128)(2,1)S(1)}, f32[128,1024]{1,0:T(8,128)S(1)}, f32[128,1024]{1,0:T(8,128)S(1)}, f32[128,1024]{1,0:T(8,128)S(1)}, f32[128,1024]{1,0:T(8,128)S(1)}) custom-call(bf16[3,16,1024]{2,1,0:T(8,128)(2,1)S(1)} %collective-permute-done.halo, f32[3,7,1024]{2,1,0:T(8,128)S(1)} %get-tuple-element.33.taps, ...), custom_call_target="tpu_custom_call" | custom-call | tf_op jit(solution)/shard_map/prepare/pallas_call | solution.py:320
  9.8 37.8 %all_to_all.10.x = bf16[128,24,128]{2,1,0:T(8,128)(2,1)S(1)} all-to-all(bf16[128,24,128]{2,1,0:T(8,128)(2,1)S(1)} %get-tuple-element.40), channel_id=1, replica_groups={{0,128,64,192,32,160,96,224,2,130,66,194,34,162,98,226,4,132,68,196,36,..., dimensions={0} | all-to-all | bytes 1572864 | tf_op jit(solution)/shard_map/all_to_all | solution.py:329
  47.6 0.0 copy-done
  47.6 0.0 copy-done.1
  47.6 0.0 copy-done.2
  47.6 0.0 copy-done.3
  47.6 0.0 copy-done.4
  47.6 6.1 %spectral.1 = bf16[128,24,128]{2,1,0:T(8,128)(2,1)S(1)} custom-call(bf16[128,24,128]{2,1,0:T(8,128)(2,1)S(1)} %all_to_all.10.x, bf16[256,256]{1,0:T(8,128)(2,1)S(1)} %copy-done.4, bf16[2,256,256]{2,1,0:T(8,128)(2,1)S(1)} %copy-done.1, bf16[2,256,256]{2,1,0:T(8,128)(2,1)S(1)} %copy-done, bf16[256,256]{1,0:T(8,128)(2,1)S(1)} %copy-done.3, ...), custom_call_target="tpu_custom_call" | custom-call | tf_op jit(solution)/shard_map/spectral/pallas_call | solution.py:334
  53.8 30.5 %all_to_all.11.landed = bf16[128,24,128]{2,1,0:T(8,128)(2,1)S(1)} all-to-all(bf16[128,24,128]{2,1,0:T(8,128)(2,1)S(1)} %spectral.1), channel_id=1, replica_groups={{0,128,64,192,32,160,96,224,2,130,66,194,34,162,98,226,4,132,68,196,36,..., dimensions={0} | all-to-all | bytes 1572864 | tf_op jit(solution)/shard_map/all_to_all | solution.py:341
  84.2 0.5 gate.1
  84.7 0.1 collective-permute-start.3
  84.8 1.9 %collective-permute-start.2 = (bf16[3,16,1024]{2,1,0:T(8,128)(2,1)S(1)}, bf16[3,16,1024]{2,1,0:T(8,128)(2,1)S(1)}, u32[]{:S(2)}, u32[]{:S(2)}) collective-permute-start(bf16[3,16,1024]{2,1,0:T(8,128)(2,1)S(1)} %get-tuple-element.53), channel_id=1, source_target_pairs={{2,0},{4,2},{6,4},{8,6},{10,8},{12,10},{14,12},{16,14},{18,16},{20... | collective-permute-start | bytes 294920 | tf_op jit(solution)/shard_map/ppermute | solution.py:23
  86.8 2.4 %project.1 = (f32[128,1024]{1,0:T(8,128)}, f32[128,1024]{1,0:T(8,128)S(1)}, f32[128,1024]{1,0:T(8,128)S(1)}, f32[128,1024]{1,0:T(8,128)S(1)}, f32[128,1024]{1,0:T(8,128)S(1)}) custom-call(bf16[128,24,128]{2,1,0:T(8,128)(2,1)S(1)} %all_to_all.11.landed, bf16[128,1024]{1,0:T(8,128)(2,1)S(1)} %get-tuple-element.45.gated, ...), custom_call_target="tpu_custom_call" | custom-call | flops 536870912 | bytes 8388608 | tf_op jit(solution)/shard_map/project/pallas_call | solution.py:358
  89.1 7.0 %collective-permute-done.2.after = bf16[3,16,1024]{2,1,0:T(8,128)(2,1)S(1)} collective-permute-done((bf16[3,16,1024]{2,1,0:T(8,128)(2,1)S(1)}, bf16[3,16,1024]{2,1,0:T(8,128)(2,1)S(1)}, u32[]{:S(2)}, u32[]{:S(2)}) %collective-permute-start.2) | collective-permute-done | bytes 98336 | tf_op jit(solution)/shard_map/ppermute | solution.py:23
  96.1 0.0 collective-permute-done.3.other
  96.1 1.8 %close.1 = (bf16[128,1024]{1,0:T(8,128)(2,1)}, bf16[128,1024]{1,0:T(8,128)(2,1)}, bf16[128,1024]{1,0:T(8,128)(2,1)}, bf16[128,1024]{1,0:T(8,128)(2,1)}) custom-call(f32[128,1024]{1,0:T(8,128)S(1)} %get-tuple-element.50.tq, f32[128,1024]{1,0:T(8,128)S(1)} %get-tuple-element.51.tk, f32[128,1024]{1,0:T(8,128)S(1)} %get-tuple-element.52.tv, ...), custom_call_target="tpu_custom_call" | custom-call | tf_op jit(solution)/shard_map/close/pallas_call | solution.py:372
Async XLA Ops:
  0.6 8.0 %collective-permute-start.1 = (bf16[128,1024]{1,0:T(8,128)(2,1)}, bf16[128,1024]{1,0:T(8,128)(2,1)S(1)}, u32[]{:S(2)}, u32[]{:S(2)}) collective-permute-start(bf16[128,1024]{1,0:T(8,128)(2,1)} %mine.1), channel_id=1, source_target_pairs={{0,1},{1,0},{2,3},{3,2},{4,5},{5,4},{6,7},{7,6},{8,9},{9,8},{10,11... | collective-permute-start | bytes 786440 | tf_op jit(solution)/shard_map/ppermute | solution.py:275
  1.6 7.1 %collective-permute-start = (bf16[3,16,1024]{2,1,0:T(8,128)(2,1)S(1)}, bf16[3,16,1024]{2,1,0:T(8,128)(2,1)S(1)}, u32[]{:S(2)}, u32[]{:S(2)}) collective-permute-start(bf16[3,16,1024]{2,1,0:T(8,128)(2,1)S(1)} %tails.1), channel_id=1, source_target_pairs={{0,2},{2,4},{4,6},{6,8},{8,10},{10,12},{12,14},{14,16},{16,18},{18... | collective-permute-start | bytes 294920 | tf_op jit(solution)/shard_map/ppermute | solution.py:23
  8.7 38.9 %copy-start = (bf16[2,256,256]{2,1,0:T(8,128)(2,1)S(1)}, bf16[2,256,256]{2,1,0:T(8,128)(2,1)}, u32[]{:S(2)}) copy-start(bf16[2,256,256]{2,1,0:T(8,128)(2,1)} %constant.16.clone.back) | copy-start | bytes 786436
  8.7 38.9 %copy-start.1 = (bf16[2,256,256]{2,1,0:T(8,128)(2,1)S(1)}, bf16[2,256,256]{2,1,0:T(8,128)(2,1)}, u32[]{:S(2)}) copy-start(bf16[2,256,256]{2,1,0:T(8,128)(2,1)} %constant.15.clone.second) | copy-start | bytes 786436
  8.7 38.9 %copy-start.2 = (f32[2,128,128]{2,1,0:T(8,128)S(1)}, f32[2,128,128]{2,1,0:T(8,128)}, u32[]{:S(2)}) copy-start(f32[2,128,128]{2,1,0:T(8,128)} %constant.18.clone.twist) | copy-start | bytes 393220
  8.7 38.9 %copy-start.3 = (bf16[256,256]{1,0:T(8,128)(2,1)S(1)}, bf16[256,256]{1,0:T(8,128)(2,1)}, u32[]{:S(2)}) copy-start(bf16[256,256]{1,0:T(8,128)(2,1)} %constant.17.clone.last) | copy-start | bytes 393220
  8.7 38.9 %copy-start.4 = (bf16[256,256]{1,0:T(8,128)(2,1)S(1)}, bf16[256,256]{1,0:T(8,128)(2,1)}, u32[]{:S(2)}) copy-start(bf16[256,256]{1,0:T(8,128)(2,1)} %constant.14.clone.first) | copy-start | bytes 393220
  84.7 11.4 %collective-permute-start.3 = (f32[128,1024]{1,0:T(8,128)S(1)}, f32[128,1024]{1,0:T(8,128)S(1)}, u32[]{:S(2)}, u32[]{:S(2)}) collective-permute-start(f32[128,1024]{1,0:T(8,128)S(1)} %get-tuple-element.55), channel_id=1, source_target_pairs={{0,1},{1,0},{2,3},{3,2},{4,5},{5,4},{6,7},{7,6},{8,9},{9,8},{10,11... | collective-permute-start | bytes 1572872 | tf_op jit(solution)/shard_map/ppermute | solution.py:355
  84.8 11.3 %collective-permute-start.2 = (bf16[3,16,1024]{2,1,0:T(8,128)(2,1)S(1)}, bf16[3,16,1024]{2,1,0:T(8,128)(2,1)S(1)}, u32[]{:S(2)}, u32[]{:S(2)}) collective-permute-start(bf16[3,16,1024]{2,1,0:T(8,128)(2,1)S(1)} %get-tuple-element.53), channel_id=1, source_target_pairs={{2,0},{4,2},{6,4},{8,6},{10,8},{12,10},{14,12},{16,14},{18,16},{20... | collective-permute-start | bytes 294920 | tf_op jit(solution)/shard_map/ppermute | solution.py:23

commit v4 on v3

--- a/solution.py
+++ b/solution.py
@@ -14,6 +14,7 @@
 EDGE = 8
 TAIL = 16
 WIDE = 256
+LANES = 128
 VMEM_LIMIT = 24 * 1024 * 1024
 
 
@@ -89,12 +90,12 @@
     copies = [pltpu.make_async_copy(src, dst, sems.at[i]) for i, (src, dst) in enumerate(pairs)]
     for copy in copies:
         copy.start()
-    pad[0:EDGE, :] = jnp.zeros((EDGE, WIDE), f32)
+    pad[0:EDGE, :] = jnp.zeros((EDGE, LANES), f32)
     copies[0].wait()
     for which, (buf, out) in enumerate(((qb, qs), (kb, ks), (vb, vs))):
         copies[1 + which].wait()
-        for first in range(0, width, WIDE):
-            columns = slice(first, first + WIDE)
+        for first in range(0, width, LANES):
+            columns = slice(first, first + LANES)
             pad[EDGE : EDGE + rows, :] = buf[:, columns].astype(f32)
             total = taps[which, 0:1, columns] * pad[EDGE : EDGE + rows, :]
             for shift in range(1, taps.shape[1]):
@@ -193,59 +194,74 @@
     out[...] = buf[...].reshape(parts, lines, rows).astype(bf16)
 
 
-def gate_kernel(landed, qs, ks, vs, gg, wo, gq, gk, gv, heads, gated, other):
+def gate_kernel(landed, qs, gg, wo, gq, gated, other):
     rows, width = qs.shape
     parts, lines, _ = landed.shape
     group = lines // 3
     for first in range(0, width, WIDE):
         part = slice(first, first + WIDE)
         values = landed[first // group : (first + WIDE) // group].astype(f32)
-        long_out, grad_mixed = [
-            values[:, f * group : (f + 1) * group, :].reshape(WIDE, rows).T for f in range(2)
-        ]
+        long_out = values[:, :group, :].reshape(WIDE, rows).T
         gated[:, part] = (qs[:, part] * long_out).astype(bf16)
-        for which, (to, value) in enumerate(
-            (
-                (gq, gg[:, part] * long_out),
-                (gk, grad_mixed * vs[:, part]),
-                (gv, grad_mixed * ks[:, part]),
-            )
-        ):
-            to[:, part] = value
-            heads[which, :, part] = value[:TAIL, :].astype(bf16)
+        gq[:, part] = gg[:, part] * long_out
     for first in range(0, width, WIDE):
         part = slice(first, first + WIDE)
         other[:, part] = jnp.dot(gated[...], wo[:, part], preferred_element_type=f32)
 
 
-def project_kernel(landed, gated, wm, gq, gk, gv, taps, gf, mine, tq, tk, tv, pad):
-    rows, width = gated.shape
+def grads_kernel(landed, ks, vs, gq, gk, gv, gf, heads):
+    rows, width = ks.shape
     parts, lines, _ = landed.shape
     group = lines // 3
-    pad[rows : rows + EDGE, :] = jnp.zeros((EDGE, WIDE), f32)
+    for first in range(0, width, WIDE):
+        part = slice(first, first + WIDE)
+        values = landed[first // group : (first + WIDE) // group].astype(f32)
+        grad_mixed, grad_filter = [
+            values[:, f * group : (f + 1) * group, :].reshape(WIDE, rows).T for f in (1, 2)
+        ]
+        grad_k = grad_mixed * vs[:, part]
+        grad_v = grad_mixed * ks[:, part]
+        gk[:, part] = grad_k
+        gv[:, part] = grad_v
+        gf[:, part] = grad_filter
+        heads[0, :, part] = gq[:TAIL, part].astype(bf16)
+        heads[1, :, part] = grad_k[:TAIL].astype(bf16)
+        heads[2, :, part] = grad_v[:TAIL].astype(bf16)
+
+
+def project_kernel(gated, wm, gq, gk, gv, taps, mine, ends, oq, ok, ov, pad):
+    rows, width = gated.shape
     for first in range(0, width, WIDE):
         part = slice(first, first + WIDE)
         mine[:, part] = jnp.dot(gated[...], wm[:, part], preferred_element_type=f32)
-        values = landed[first // group : (first + WIDE) // group].astype(f32)
-        gf[:, part] = values[:, 2 * group :, :].reshape(WIDE, rows).T
-        for which, (value, to) in enumerate(((gq, tq), (gk, tk), (gv, tv))):
+    pad[rows : rows + EDGE, :] = jnp.zeros((EDGE, LANES), f32)
+    for which, (value, to) in enumerate(((gq, oq), (gk, ok), (gv, ov))):
+        for first in range(0, width, LANES):
+            part = slice(first, first + LANES)
             pad[0:rows, :] = value[:, part]
             total = taps[which, 0:1, part] * value[:, part]
             for shift in range(1, taps.shape[1]):
                 total = total + taps[which, shift : shift + 1, part] * pad[shift : shift + rows, :]
-            to[:, part] = total
-
-
-def close_kernel(tq, tk, tv, after, taps, mine, other, block_out, oq, ok, ov, pad):
-    rows, width = tq.shape
+            to[:, part] = total.astype(bf16)
+            ends[which, :, part] = total[rows - TAIL :, :]
+
+
+def close_kernel(ends, after, taps, mine, other, near_q, near_k, near_v, block_out, oq, ok, ov, pad, tail, sems):
+    rows, width = mine.shape
     pad[0:EDGE, :] = jnp.zeros((EDGE, width), f32)
-    for which, (value, to) in enumerate(((tq, oq), (tk, ok), (tv, ov))):
+    copies = []
+    for which, to in enumerate((oq, ok, ov)):
         pad[EDGE : 2 * EDGE, :] = after[which].astype(f32)[:EDGE, :]
-        end = value[rows - EDGE :, :]
+        end = ends[which, TAIL - EDGE :, :]
         for shift in range(1, taps.shape[1]):
             end = end + taps[which, shift : shift + 1, :] * pad[shift : shift + EDGE, :]
-        to[...] = jnp.concatenate([value[: rows - EDGE, :], end], 0).astype(bf16)
+        tail[which] = jnp.concatenate([ends[which, : TAIL - EDGE, :], end], 0).astype(bf16)
+        copy = pltpu.make_async_copy(tail.at[which], to.at[pl.ds(rows - TAIL, TAIL), :], sems.at[which])
+        copy.start()
+        copies.append(copy)
     block_out[...] = (mine[...] + other[...]).astype(bf16)
+    for copy in copies:
+        copy.wait()
 
 
 def on_device(query_in, key_in, value_in, taps, long_filter, out_weight, out_grad):
@@ -254,7 +270,6 @@
     seq_total = parts * rows
     group = width // parts
     lines = 3 * group
-    reach = taps.shape[1]
     outs = out_weight.shape[1]
     here = lax.axis_index("ch").astype(jnp.int32).reshape(1)
     gain = 1.0 / math.sqrt(seq_total) / seq_total
@@ -309,7 +324,7 @@
                 pltpu.VMEM((rows, width), bf16),
                 pltpu.VMEM((rows, width), f32),
                 pltpu.VMEM((rows, width), bf16),
-                pltpu.VMEM((rows + EDGE, WIDE), f32),
+                pltpu.VMEM((rows + EDGE, LANES), f32),
                 pltpu.SemaphoreType.DMA((8,)),
             ],
             compiler_params=params,
@@ -343,41 +358,51 @@
     )
 
     with jax.named_scope("gate"):
-        gq, gk, gv, heads, gated, other = pl.pallas_call(
+        gq, gated, other = pl.pallas_call(
             gate_kernel,
+            in_specs=[vmem] * 4,
+            out_specs=[vmem] * 3,
+            out_shape=[flat, half, flat],
+            compiler_params=params,
+        )(landed, qs, gg, wo)
+    theirs = lax.ppermute(other, "ch", swap)
+
+    with jax.named_scope("grads"):
+        gk, gv, grad_filter, heads = pl.pallas_call(
+            grads_kernel,
+            in_specs=[vmem] * 4,
+            out_specs=[vmem] * 4,
+            out_shape=[flat, flat, flat, edges],
+            compiler_params=params,
+        )(landed, ks, vs, gq)
+    after = shifted(heads, "ctx", -1)
+
+    with jax.named_scope("project"):
+        mine, ends, oq, ok, ov = pl.pallas_call(
+            project_kernel,
             in_specs=[vmem] * 6,
-            out_specs=[vmem] * 6,
-            out_shape=[flat, flat, flat, edges, half, flat],
-            compiler_params=params,
-        )(landed, qs, ks, vs, gg, wo)
-
-    after = shifted(heads, "ctx", -1)
-    theirs = lax.ppermute(other, "ch", swap)
-
-    with jax.named_scope("project"):
-        grad_filter, mine, tq, tk, tv = pl.pallas_call(
-            project_kernel,
-            in_specs=[vmem] * 7,
             out_specs=[vmem] * 5,
-            out_shape=[flat] * 5,
-            scratch_shapes=[pltpu.VMEM((rows + EDGE, WIDE), f32)],
+            out_shape=[flat, jax.ShapeDtypeStruct((3, TAIL, width), f32), half, half, half],
+            scratch_shapes=[pltpu.VMEM((rows + EDGE, LANES), f32)],
             compiler_params=params,
             cost_estimate=cost,
-        )(landed, gated, wm, gq, gk, gv, taps_near)
+        )(gated, wm, gq, gk, gv, taps_near)
 
     with jax.named_scope("close"):
-        column = pl.BlockSpec((rows, WIDE), lambda i: (0, i))
-        edge = pl.BlockSpec((3, TAIL, WIDE), lambda i: (0, 0, i))
-        taps_spec = pl.BlockSpec((3, reach, WIDE), lambda i: (0, 0, i))
+        begun = [pltpu.with_memory_space_constraint(x, pltpu.HBM) for x in (oq, ok, ov)]
         block_out, grad_query, grad_key, grad_value = pl.pallas_call(
             close_kernel,
-            grid=(width // WIDE,),
-            in_specs=[column] * 3 + [edge, taps_spec, column, column],
-            out_specs=[column] * 4,
+            in_specs=[vmem] * 5 + [hbm] * 3,
+            out_specs=[vmem] + [hbm] * 3,
             out_shape=[half] * 4,
-            scratch_shapes=[pltpu.VMEM((2 * EDGE, WIDE), f32)],
-            compiler_params=params,
-        )(tq, tk, tv, after, taps_near, mine, theirs)
+            input_output_aliases={5: 1, 6: 2, 7: 3},
+            scratch_shapes=[
+                pltpu.VMEM((2 * EDGE, width), f32),
+                pltpu.VMEM((3, TAIL, width), bf16),
+                pltpu.SemaphoreType.DMA((3,)),
+            ],
+            compiler_params=params,
+        )(ends, after, taps_near, mine, theirs, *begun)
     return (block_out, grad_query, grad_key, grad_value, grad_filter)
 
 

time: 98.3 us -> 99.1 us (level)
    pallas_call x3 -> x4, Pallas kernels: 4.64 us -> 5.44 us  [the longest x1 2.43 us: on_device(): pl.pallas_call(project_kernel, in_specs=[vmem] * 6, out_specs=[vmem] * 5,...]
  transfers between devices with their start and end apart: 4 -> 4, of which waited for: 1 -> 2; matrix products, arithmetic and copies ran while one was open for 0% -> 0% of each run, Pallas kernels for 7% -> 7%
where the time goes in v4:
time: 99.1 us; the launch traced here: 98.8 us
  blocking collectives  68.3 us (69%)
  Pallas kernels  16.5 us (17%)
  waiting for transfers between devices  7.55 us (8%)
  starting transfers between devices  5.5 us (6%)
    all_to_all x1, blocking collectives, on_device(): lax.all_to_all(send, 'ctx', split_axis=0, concat_axis=0, tiled=True, axis...  37.9 us
    all_to_all x1, blocking collectives, on_device(): lax.all_to_all(solved, 'ctx', split_axis=0, concat_axis=0, tiled=True, ax...  30.5 us
    ppermute x2, waiting for transfers between devices, shifted(): lax.ppermute(value, axis, [(source, source + steps) for source in range(f...  7.54 us
    pallas_call x1, Pallas kernels, on_device(): pl.pallas_call(spectral_kernel, out_shape=fields, scratch_shapes=[pltpu.V...  6.13 us
    ppermute x2, starting transfers between devices, shifted(): lax.ppermute(value, axis, [(source, source + steps) for source in range(f...  5.31 us
    pallas_call x1, Pallas kernels, on_device(): pl.pallas_call(fetch_kernel, in_specs=[smem] + [hbm] * 7, out_specs=[vmem...  3.07 us
    pallas_call x1, Pallas kernels, on_device(): pl.pallas_call(project_kernel, in_specs=[vmem] * 6, out_specs=[vmem] * 5,...  2.43 us
  transfers between devices with their start and end apart: 4, of which 2 were waited for; matrix products, arithmetic and copies ran while one was open for 0% of the time, Pallas kernels for 7%

profile of v4, /device:TPU:30, one launch (start us, length us, event | category | flops | bytes accessed | tf_op | source)
XLA Modules:
  0.0 98.8 jit_solution(6194542766859954711)
XLA Ops:
  0.6 0.1 collective-permute-start.1
  0.7 0.8 tails.1
  1.6 3.4 %collective-permute-start = (bf16[3,16,1024]{2,1,0:T(8,128)(2,1)S(1)}, bf16[3,16,1024]{2,1,0:T(8,128)(2,1)S(1)}, u32[]{:S(2)}, u32[]{:S(2)}) collective-permute-start(bf16[3,16,1024]{2,1,0:T(8,128)(2,1)S(1)} %tails.1), channel_id=1, source_target_pairs={{0,2},{2,4},{4,6},{6,8},{8,10},{10,12},{12,14},{14,16},{16,18},{18... | collective-permute-start | bytes 294920 | tf_op jit(solution)/shard_map/ppermute | solution.py:24
  5.0 3.1 %fetch.1 = (f32[128,1024]{1,0:T(8,128)S(1)}, f32[128,1024]{1,0:T(8,128)S(1)}, f32[128,1024]{1,0:T(8,128)S(1)}, f32[128,1024]{1,0:T(8,128)S(1)}, f32[1024,128]{1,...) custom-call(s32[1]{0:T(128)} %bitcast.here, ...), custom_call_target="tpu_custom_call" | custom-call | flops 536870912 | bytes 8388608 | tf_op jit(solution)/shard_map/fetch/pallas_call | solution.py:307
  8.0 0.6 collective-permute-done.halo
  8.6 0.0 collective-permute-done.1.other
  8.6 0.0 copy-start
  8.6 0.0 copy-start.1
  8.7 0.0 copy-start.2
  8.7 0.0 copy-start.3
  8.7 0.0 copy-start.4
  8.7 1.0 %prepare.1 = (bf16[128,24,128]{2,1,0:T(8,128)(2,1)S(1)}, f32[128,1024]{1,0:T(8,128)S(1)}, f32[128,1024]{1,0:T(8,128)S(1)}, f32[128,1024]{1,0:T(8,128)S(1)}, f32[128,1024]{1,0:T(8,128)S(1)}) custom-call(bf16[3,16,1024]{2,1,0:T(8,128)(2,1)S(1)} %collective-permute-done.halo, f32[3,7,1024]{2,1,0:T(8,128)S(1)} %get-tuple-element.34.taps, ...), custom_call_target="tpu_custom_call" | custom-call | tf_op jit(solution)/shard_map/prepare/pallas_call | solution.py:335
  9.7 37.9 %all_to_all.10.x = bf16[128,24,128]{2,1,0:T(8,128)(2,1)S(1)} all-to-all(bf16[128,24,128]{2,1,0:T(8,128)(2,1)S(1)} %get-tuple-element.41), channel_id=1, replica_groups={{0,128,64,192,32,160,96,224,2,130,66,194,34,162,98,226,4,132,68,196,36,..., dimensions={0} | all-to-all | bytes 1572864 | tf_op jit(solution)/shard_map/all_to_all | solution.py:344
  47.6 0.0 copy-done
  47.6 0.0 copy-done.1
  47.6 0.0 copy-done.2
  47.6 0.0 copy-done.3
  47.6 0.0 copy-done.4
  47.6 6.1 %spectral.1 = bf16[128,24,128]{2,1,0:T(8,128)(2,1)S(1)} custom-call(bf16[128,24,128]{2,1,0:T(8,128)(2,1)S(1)} %all_to_all.10.x, bf16[256,256]{1,0:T(8,128)(2,1)S(1)} %copy-done.4, bf16[2,256,256]{2,1,0:T(8,128)(2,1)S(1)} %copy-done.1, bf16[2,256,256]{2,1,0:T(8,128)(2,1)S(1)} %copy-done, bf16[256,256]{1,0:T(8,128)(2,1)S(1)} %copy-done.3, ...), custom_call_target="tpu_custom_call" | custom-call | tf_op jit(solution)/shard_map/spectral/pallas_call | solution.py:349
  53.7 30.5 %all_to_all.11.landed = bf16[128,24,128]{2,1,0:T(8,128)(2,1)S(1)} all-to-all(bf16[128,24,128]{2,1,0:T(8,128)(2,1)S(1)} %spectral.1), channel_id=1, replica_groups={{0,128,64,192,32,160,96,224,2,130,66,194,34,162,98,226,4,132,68,196,36,..., dimensions={0} | all-to-all | bytes 1572864 | tf_op jit(solution)/shard_map/all_to_all | solution.py:356
  84.2 0.5 gate.1
  84.7 0.1 collective-permute-start.3
  84.8 1.0 %grads.1 = (f32[128,1024]{1,0:T(8,128)S(1)}, f32[128,1024]{1,0:T(8,128)S(1)}, f32[128,1024]{1,0:T(8,128)}, bf16[3,16,1024]{2,1,0:T(8,128)(2,1)S(1)}) custom-call(bf16[128,24,128]{2,1,0:T(8,128)(2,1)S(1)} %all_to_all.11.landed, f32[128,1024]{1,0:T(8,128)S(1)} %get-tuple-element.47.ks, f32[128,1024]{1,0:T(8,128)S(1)} %get-tuple-element.48.vs, ...), custom_call_target="tpu_custom_call" | custom-call | tf_op jit(solution)/shard_map/grads/pallas_call | solution.py:371
  85.8 1.9 %collective-permute-start.2 = (bf16[3,16,1024]{2,1,0:T(8,128)(2,1)S(1)}, bf16[3,16,1024]{2,1,0:T(8,128)(2,1)S(1)}, u32[]{:S(2)}, u32[]{:S(2)}) collective-permute-start(bf16[3,16,1024]{2,1,0:T(8,128)(2,1)S(1)} %get-tuple-element.52), channel_id=1, source_target_pairs={{2,0},{4,2},{6,4},{8,6},{10,8},{12,10},{14,12},{16,14},{18,16},{20... | collective-permute-start | bytes 294920 | tf_op jit(solution)/shard_map/ppermute | solution.py:24
  87.8 2.4 %project.1 = (f32[128,1024]{1,0:T(8,128)S(1)}, f32[3,16,1024]{2,1,0:T(8,128)S(1)}, bf16[128,1024]{1,0:T(8,128)(2,1)}, bf16[128,1024]{1,0:T(8,128)(2,1)}, bf16[128,1024]{1,0:T(8,128)(2,1)}) custom-call(bf16[128,1024]{1,0:T(8,128)(2,1)S(1)} %get-tuple-element.44.gated, bf16[1024,1024]{1,0:T(8,128)(2,1)S(1)} %get-tuple-element.45.wm, ...), custom_call_target="tpu_custom_call" | custom-call | flops 536870912 | bytes 8388608 | tf_op jit(solution)/shard_map/project/pallas_call | solution.py:381
  90.2 6.9 %collective-permute-done.2.after = bf16[3,16,1024]{2,1,0:T(8,128)(2,1)S(1)} collective-permute-done((bf16[3,16,1024]{2,1,0:T(8,128)(2,1)S(1)}, bf16[3,16,1024]{2,1,0:T(8,128)(2,1)S(1)}, u32[]{:S(2)}, u32[]{:S(2)}) %collective-permute-start.2) | collective-permute-done | bytes 98336 | tf_op jit(solution)/shard_map/ppermute | solution.py:24
  97.1 0.0 collective-permute-done.3.other
  97.1 1.5 %close.1 = (bf16[128,1024]{1,0:T(8,128)(2,1)}, bf16[128,1024]{1,0:T(8,128)(2,1)}, bf16[128,1024]{1,0:T(8,128)(2,1)}, bf16[128,1024]{1,0:T(8,128)(2,1)}) custom-call(f32[3,16,1024]{2,1,0:T(8,128)S(1)} %get-tuple-element.51.ends, bf16[3,16,1024]{2,1,0:T(8,128)(2,1)S(1)} %collective-permute-done.2.after, ...), custom_call_target="tpu_custom_call", output_to_operand_aliasing={{1}: (5, {}), {2}: (6, {}), {3}: (7, {})} | custom-call | tf_op jit(solution)/shard_map/close/pallas_call | solution.py:393
Async XLA Ops:
  0.6 8.0 %collective-permute-start.1 = (bf16[128,1024]{1,0:T(8,128)(2,1)}, bf16[128,1024]{1,0:T(8,128)(2,1)S(1)}, u32[]{:S(2)}, u32[]{:S(2)}) collective-permute-start(bf16[128,1024]{1,0:T(8,128)(2,1)} %mine.1), channel_id=1, source_target_pairs={{0,1},{1,0},{2,3},{3,2},{4,5},{5,4},{6,7},{7,6},{8,9},{9,8},{10,11... | collective-permute-start | bytes 786440 | tf_op jit(solution)/shard_map/ppermute | solution.py:290
  1.6 7.1 %collective-permute-start = (bf16[3,16,1024]{2,1,0:T(8,128)(2,1)S(1)}, bf16[3,16,1024]{2,1,0:T(8,128)(2,1)S(1)}, u32[]{:S(2)}, u32[]{:S(2)}) collective-permute-start(bf16[3,16,1024]{2,1,0:T(8,128)(2,1)S(1)} %tails.1), channel_id=1, source_target_pairs={{0,2},{2,4},{4,6},{6,8},{8,10},{10,12},{12,14},{14,16},{16,18},{18... | collective-permute-start | bytes 294920 | tf_op jit(solution)/shard_map/ppermute | solution.py:24
  8.6 38.9 %copy-start = (bf16[2,256,256]{2,1,0:T(8,128)(2,1)S(1)}, bf16[2,256,256]{2,1,0:T(8,128)(2,1)}, u32[]{:S(2)}) copy-start(bf16[2,256,256]{2,1,0:T(8,128)(2,1)} %constant.16.clone.back) | copy-start | bytes 786436
  8.6 38.9 %copy-start.1 = (bf16[2,256,256]{2,1,0:T(8,128)(2,1)S(1)}, bf16[2,256,256]{2,1,0:T(8,128)(2,1)}, u32[]{:S(2)}) copy-start(bf16[2,256,256]{2,1,0:T(8,128)(2,1)} %constant.15.clone.second) | copy-start | bytes 786436
  8.7 38.9 %copy-start.2 = (f32[2,128,128]{2,1,0:T(8,128)S(1)}, f32[2,128,128]{2,1,0:T(8,128)}, u32[]{:S(2)}) copy-start(f32[2,128,128]{2,1,0:T(8,128)} %constant.18.clone.twist) | copy-start | bytes 393220
  8.7 38.9 %copy-start.3 = (bf16[256,256]{1,0:T(8,128)(2,1)S(1)}, bf16[256,256]{1,0:T(8,128)(2,1)}, u32[]{:S(2)}) copy-start(bf16[256,256]{1,0:T(8,128)(2,1)} %constant.17.clone.last) | copy-start | bytes 393220
  8.7 38.9 %copy-start.4 = (bf16[256,256]{1,0:T(8,128)(2,1)S(1)}, bf16[256,256]{1,0:T(8,128)(2,1)}, u32[]{:S(2)}) copy-start(bf16[256,256]{1,0:T(8,128)(2,1)} %constant.14.clone.first) | copy-start | bytes 393220
  84.7 12.4 %collective-permute-start.3 = (f32[128,1024]{1,0:T(8,128)S(1)}, f32[128,1024]{1,0:T(8,128)S(1)}, u32[]{:S(2)}, u32[]{:S(2)}) collective-permute-start(f32[128,1024]{1,0:T(8,128)S(1)} %get-tuple-element.54), channel_id=1, source_target_pairs={{0,1},{1,0},{2,3},{3,2},{4,5},{5,4},{6,7},{7,6},{8,9},{9,8},{10,11... | collective-permute-start | bytes 1572872 | tf_op jit(solution)/shard_map/ppermute | solution.py:368
  85.8 11.3 %collective-permute-start.2 = (bf16[3,16,1024]{2,1,0:T(8,128)(2,1)S(1)}, bf16[3,16,1024]{2,1,0:T(8,128)(2,1)S(1)}, u32[]{:S(2)}, u32[]{:S(2)}) collective-permute-start(bf16[3,16,1024]{2,1,0:T(8,128)(2,1)S(1)} %get-tuple-element.52), channel_id=1, source_target_pairs={{2,0},{4,2},{6,4},{8,6},{10,8},{12,10},{14,12},{16,14},{18,16},{20... | collective-permute-start | bytes 294920 | tf_op jit(solution)/shard_map/ppermute | solution.py:24

commit v5 on v3

--- a/solution.py
+++ b/solution.py
@@ -14,6 +14,7 @@
 EDGE = 8
 TAIL = 16
 WIDE = 256
+LANES = 128
 VMEM_LIMIT = 24 * 1024 * 1024
 
 
@@ -89,12 +90,12 @@
     copies = [pltpu.make_async_copy(src, dst, sems.at[i]) for i, (src, dst) in enumerate(pairs)]
     for copy in copies:
         copy.start()
-    pad[0:EDGE, :] = jnp.zeros((EDGE, WIDE), f32)
+    pad[0:EDGE, :] = jnp.zeros((EDGE, LANES), f32)
     copies[0].wait()
     for which, (buf, out) in enumerate(((qb, qs), (kb, ks), (vb, vs))):
         copies[1 + which].wait()
-        for first in range(0, width, WIDE):
-            columns = slice(first, first + WIDE)
+        for first in range(0, width, LANES):
+            columns = slice(first, first + LANES)
             pad[EDGE : EDGE + rows, :] = buf[:, columns].astype(f32)
             total = taps[which, 0:1, columns] * pad[EDGE : EDGE + rows, :]
             for shift in range(1, taps.shape[1]):
@@ -218,34 +219,57 @@
         other[:, part] = jnp.dot(gated[...], wo[:, part], preferred_element_type=f32)
 
 
-def project_kernel(landed, gated, wm, gq, gk, gv, taps, gf, mine, tq, tk, tv, pad):
+def project_kernel(
+    landed, gated, wm, gq, gk, gv, taps, gf, mine, ends, oq, ok, ov, pad, turned, rounded, sems
+):
     rows, width = gated.shape
     parts, lines, _ = landed.shape
     group = lines // 3
-    pad[rows : rows + EDGE, :] = jnp.zeros((EDGE, WIDE), f32)
-    for first in range(0, width, WIDE):
-        part = slice(first, first + WIDE)
-        mine[:, part] = jnp.dot(gated[...], wm[:, part], preferred_element_type=f32)
+    for first in range(0, width, WIDE):
+        part = slice(first, first + WIDE)
         values = landed[first // group : (first + WIDE) // group].astype(f32)
-        gf[:, part] = values[:, 2 * group :, :].reshape(WIDE, rows).T
-        for which, (value, to) in enumerate(((gq, tq), (gk, tk), (gv, tv))):
+        turned[:, part] = values[:, 2 * group :, :].reshape(WIDE, rows).T
+    copies = [pltpu.make_async_copy(turned, gf, sems.at[3])]
+    copies[0].start()
+    pad[rows : rows + EDGE, :] = jnp.zeros((EDGE, LANES), f32)
+    for which, (value, to) in enumerate(((gq, oq), (gk, ok), (gv, ov))):
+        for first in range(0, width, LANES):
+            part = slice(first, first + LANES)
             pad[0:rows, :] = value[:, part]
             total = taps[which, 0:1, part] * value[:, part]
             for shift in range(1, taps.shape[1]):
                 total = total + taps[which, shift : shift + 1, part] * pad[shift : shift + rows, :]
-            to[:, part] = total
-
-
-def close_kernel(tq, tk, tv, after, taps, mine, other, block_out, oq, ok, ov, pad):
-    rows, width = tq.shape
+            rounded[which, :, part] = total.astype(bf16)
+            ends[which, :, part] = total[rows - TAIL :, :]
+        copy = pltpu.make_async_copy(rounded.at[which], to, sems.at[which])
+        copy.start()
+        copies.append(copy)
+    for first in range(0, width, WIDE):
+        part = slice(first, first + WIDE)
+        mine[:, part] = jnp.dot(gated[...], wm[:, part], preferred_element_type=f32)
+    for copy in copies:
+        copy.wait()
+
+
+def close_kernel(
+    ends, after, taps, mine, other, near_q, near_k, near_v, block_out, oq, ok, ov, pad, tail, total, sems
+):
+    rows, width = mine.shape
+    total[...] = (mine[...] + other[...]).astype(bf16)
+    copies = [pltpu.make_async_copy(total, block_out, sems.at[3])]
+    copies[0].start()
     pad[0:EDGE, :] = jnp.zeros((EDGE, width), f32)
-    for which, (value, to) in enumerate(((tq, oq), (tk, ok), (tv, ov))):
+    for which, to in enumerate((oq, ok, ov)):
         pad[EDGE : 2 * EDGE, :] = after[which].astype(f32)[:EDGE, :]
-        end = value[rows - EDGE :, :]
+        end = ends[which, TAIL - EDGE :, :]
         for shift in range(1, taps.shape[1]):
             end = end + taps[which, shift : shift + 1, :] * pad[shift : shift + EDGE, :]
-        to[...] = jnp.concatenate([value[: rows - EDGE, :], end], 0).astype(bf16)
-    block_out[...] = (mine[...] + other[...]).astype(bf16)
+        tail[which] = jnp.concatenate([ends[which, : TAIL - EDGE, :], end], 0).astype(bf16)
+        copy = pltpu.make_async_copy(tail.at[which], to.at[pl.ds(rows - TAIL, TAIL), :], sems.at[which])
+        copy.start()
+        copies.append(copy)
+    for copy in copies:
+        copy.wait()
 
 
 def on_device(query_in, key_in, value_in, taps, long_filter, out_weight, out_grad):
@@ -254,7 +278,6 @@
     seq_total = parts * rows
     group = width // parts
     lines = 3 * group
-    reach = taps.shape[1]
     outs = out_weight.shape[1]
     here = lax.axis_index("ch").astype(jnp.int32).reshape(1)
     gain = 1.0 / math.sqrt(seq_total) / seq_total
@@ -309,7 +332,7 @@
                 pltpu.VMEM((rows, width), bf16),
                 pltpu.VMEM((rows, width), f32),
                 pltpu.VMEM((rows, width), bf16),
-                pltpu.VMEM((rows + EDGE, WIDE), f32),
+                pltpu.VMEM((rows + EDGE, LANES), f32),
                 pltpu.SemaphoreType.DMA((8,)),
             ],
             compiler_params=params,
@@ -355,29 +378,37 @@
     theirs = lax.ppermute(other, "ch", swap)
 
     with jax.named_scope("project"):
-        grad_filter, mine, tq, tk, tv = pl.pallas_call(
+        grad_filter, mine, ends, oq, ok, ov = pl.pallas_call(
             project_kernel,
             in_specs=[vmem] * 7,
-            out_specs=[vmem] * 5,
-            out_shape=[flat] * 5,
-            scratch_shapes=[pltpu.VMEM((rows + EDGE, WIDE), f32)],
+            out_specs=[hbm, vmem, vmem, hbm, hbm, hbm],
+            out_shape=[flat, flat, jax.ShapeDtypeStruct((3, TAIL, width), f32), half, half, half],
+            scratch_shapes=[
+                pltpu.VMEM((rows + EDGE, LANES), f32),
+                pltpu.VMEM((rows, width), f32),
+                pltpu.VMEM((3, rows, width), bf16),
+                pltpu.SemaphoreType.DMA((4,)),
+            ],
             compiler_params=params,
             cost_estimate=cost,
         )(landed, gated, wm, gq, gk, gv, taps_near)
 
     with jax.named_scope("close"):
-        column = pl.BlockSpec((rows, WIDE), lambda i: (0, i))
-        edge = pl.BlockSpec((3, TAIL, WIDE), lambda i: (0, 0, i))
-        taps_spec = pl.BlockSpec((3, reach, WIDE), lambda i: (0, 0, i))
+        begun = [pltpu.with_memory_space_constraint(x, pltpu.HBM) for x in (oq, ok, ov)]
         block_out, grad_query, grad_key, grad_value = pl.pallas_call(
             close_kernel,
-            grid=(width // WIDE,),
-            in_specs=[column] * 3 + [edge, taps_spec, column, column],
-            out_specs=[column] * 4,
+            in_specs=[vmem] * 5 + [hbm] * 3,
+            out_specs=[hbm] * 4,
             out_shape=[half] * 4,
-            scratch_shapes=[pltpu.VMEM((2 * EDGE, WIDE), f32)],
-            compiler_params=params,
-        )(tq, tk, tv, after, taps_near, mine, theirs)
+            input_output_aliases={5: 1, 6: 2, 7: 3},
+            scratch_shapes=[
+                pltpu.VMEM((2 * EDGE, width), f32),
+                pltpu.VMEM((3, TAIL, width), bf16),
+                pltpu.VMEM((rows, width), bf16),
+                pltpu.SemaphoreType.DMA((4,)),
+            ],
+            compiler_params=params,
+        )(ends, after, taps_near, mine, theirs, *begun)
     return (block_out, grad_query, grad_key, grad_value, grad_filter)
 
 

time: 98.3 us -> 97.4 us (level)
  Pallas kernels: 16.3 us -> 15 us
  transfers between devices with their start and end apart: 4 -> 4, of which waited for: 1 -> 2; matrix products, arithmetic and copies ran while one was open for 0% -> 0% of each run, Pallas kernels for 7% -> 7%
where the time goes in v5:
time: 97.4 us; the launch traced here: 97.2 us
  blocking collectives  68.3 us (70%)
  Pallas kernels  15 us (15%)
  waiting for transfers between devices  7.38 us (8%)
  starting transfers between devices  5.51 us (6%)
    all_to_all x1, blocking collectives, on_device(): lax.all_to_all(send, 'ctx', split_axis=0, concat_axis=0, tiled=True, axis...  37.9 us
    all_to_all x1, blocking collectives, on_device(): lax.all_to_all(solved, 'ctx', split_axis=0, concat_axis=0, tiled=True, ax...  30.5 us
    ppermute x2, waiting for transfers between devices, shifted(): lax.ppermute(value, axis, [(source, source + steps) for source in range(f...  7.38 us
    pallas_call x1, Pallas kernels, on_device(): pl.pallas_call(spectral_kernel, out_shape=fields, scratch_shapes=[pltpu.V...  6.13 us
    ppermute x2, starting transfers between devices, shifted(): lax.ppermute(value, axis, [(source, source + steps) for source in range(f...  5.32 us
    pallas_call x1, Pallas kernels, on_device(): pl.pallas_call(fetch_kernel, in_specs=[smem] + [hbm] * 7, out_specs=[vmem...  3.07 us
    pallas_call x1, Pallas kernels, on_device(): pl.pallas_call(project_kernel, in_specs=[vmem] * 7, out_specs=[hbm, vmem,...  2.58 us
  transfers between devices with their start and end apart: 4, of which 2 were waited for; matrix products, arithmetic and copies ran while one was open for 0% of the time, Pallas kernels for 7%

profile of v5, /device:TPU:30, one launch (start us, length us, event | category | flops | bytes accessed | tf_op | source)
XLA Modules:
  0.0 97.2 jit_solution(6918634464811240610)
XLA Ops:
  0.6 0.1 collective-permute-start.1
  0.7 0.8 tails.1
  1.6 3.4 %collective-permute-start = (bf16[3,16,1024]{2,1,0:T(8,128)(2,1)S(1)}, bf16[3,16,1024]{2,1,0:T(8,128)(2,1)S(1)}, u32[]{:S(2)}, u32[]{:S(2)}) collective-permute-start(bf16[3,16,1024]{2,1,0:T(8,128)(2,1)S(1)} %tails.1), channel_id=1, source_target_pairs={{0,2},{2,4},{4,6},{6,8},{8,10},{10,12},{12,14},{14,16},{16,18},{18... | collective-permute-start | bytes 294920 | tf_op jit(solution)/shard_map/ppermute | solution.py:24
  5.0 3.1 %fetch.1 = (f32[128,1024]{1,0:T(8,128)S(1)}, f32[128,1024]{1,0:T(8,128)S(1)}, f32[128,1024]{1,0:T(8,128)S(1)}, f32[128,1024]{1,0:T(8,128)S(1)}, f32[1024,128]{1,...) custom-call(s32[1]{0:T(128)} %bitcast.here, ...), custom_call_target="tpu_custom_call" | custom-call | flops 536870912 | bytes 8388608 | tf_op jit(solution)/shard_map/fetch/pallas_call | solution.py:315
  8.0 0.6 collective-permute-done.halo
  8.6 0.0 collective-permute-done.1.other
  8.6 0.0 copy-start
  8.6 0.0 copy-start.1
  8.7 0.0 copy-start.2
  8.7 0.0 copy-start.3
  8.7 0.0 copy-start.4
  8.7 1.0 %prepare.1 = (bf16[128,24,128]{2,1,0:T(8,128)(2,1)S(1)}, f32[128,1024]{1,0:T(8,128)S(1)}, f32[128,1024]{1,0:T(8,128)S(1)}, f32[128,1024]{1,0:T(8,128)S(1)}, f32[128,1024]{1,0:T(8,128)S(1)}) custom-call(bf16[3,16,1024]{2,1,0:T(8,128)(2,1)S(1)} %collective-permute-done.halo, f32[3,7,1024]{2,1,0:T(8,128)S(1)} %get-tuple-element.34.taps, ...), custom_call_target="tpu_custom_call" | custom-call | tf_op jit(solution)/shard_map/prepare/pallas_call | solution.py:343
  9.7 37.9 %all_to_all.10.x = bf16[128,24,128]{2,1,0:T(8,128)(2,1)S(1)} all-to-all(bf16[128,24,128]{2,1,0:T(8,128)(2,1)S(1)} %get-tuple-element.41), channel_id=1, replica_groups={{0,128,64,192,32,160,96,224,2,130,66,194,34,162,98,226,4,132,68,196,36,..., dimensions={0} | all-to-all | bytes 1572864 | tf_op jit(solution)/shard_map/all_to_all | solution.py:352
  47.6 0.0 copy-done
  47.6 0.0 copy-done.1
  47.6 0.0 copy-done.2
  47.6 0.0 copy-done.3
  47.6 0.0 copy-done.4
  47.6 6.1 %spectral.1 = bf16[128,24,128]{2,1,0:T(8,128)(2,1)S(1)} custom-call(bf16[128,24,128]{2,1,0:T(8,128)(2,1)S(1)} %all_to_all.10.x, bf16[256,256]{1,0:T(8,128)(2,1)S(1)} %copy-done.4, bf16[2,256,256]{2,1,0:T(8,128)(2,1)S(1)} %copy-done.1, bf16[2,256,256]{2,1,0:T(8,128)(2,1)S(1)} %copy-done, bf16[256,256]{1,0:T(8,128)(2,1)S(1)} %copy-done.3, ...), custom_call_target="tpu_custom_call" | custom-call | tf_op jit(solution)/shard_map/spectral/pallas_call | solution.py:357
  53.8 30.5 %all_to_all.11.landed = bf16[128,24,128]{2,1,0:T(8,128)(2,1)S(1)} all-to-all(bf16[128,24,128]{2,1,0:T(8,128)(2,1)S(1)} %spectral.1), channel_id=1, replica_groups={{0,128,64,192,32,160,96,224,2,130,66,194,34,162,98,226,4,132,68,196,36,..., dimensions={0} | all-to-all | bytes 1572864 | tf_op jit(solution)/shard_map/all_to_all | solution.py:364
  84.2 0.5 gate.1
  84.7 0.1 collective-permute-start.3
  84.8 1.9 %collective-permute-start.2 = (bf16[3,16,1024]{2,1,0:T(8,128)(2,1)S(1)}, bf16[3,16,1024]{2,1,0:T(8,128)(2,1)S(1)}, u32[]{:S(2)}, u32[]{:S(2)}) collective-permute-start(bf16[3,16,1024]{2,1,0:T(8,128)(2,1)S(1)} %get-tuple-element.52), channel_id=1, source_target_pairs={{2,0},{4,2},{6,4},{8,6},{10,8},{12,10},{14,12},{16,14},{18,16},{20... | collective-permute-start | bytes 294920 | tf_op jit(solution)/shard_map/ppermute | solution.py:24
  86.8 2.6 %project.1 = (f32[128,1024]{1,0:T(8,128)}, f32[128,1024]{1,0:T(8,128)S(1)}, f32[3,16,1024]{2,1,0:T(8,128)S(1)}, bf16[128,1024]{1,0:T(8,128)(2,1)}, bf16[128,1024]{1,0:T(8,128)(2,1)}, /*index=5*/bf16[128,1024]{1,0:T(8,128)(2,1)}) custom-call(bf16[128,24,128]{2,1,0:T(8,128)(2,1)S(1)} %all_to_all.11.landed, bf16[128,1024]{1,0:T(8,128)(2,1)S(1)} %get-tuple-element.46.gated, ...), custom_call_target="tpu_custom_call" | custom-call | flops 536870912 | bytes 8388608 | tf_op jit(solution)/shard_map/project/pallas_call | solution.py:381
  89.3 6.8 %collective-permute-done.2.after = bf16[3,16,1024]{2,1,0:T(8,128)(2,1)S(1)} collective-permute-done((bf16[3,16,1024]{2,1,0:T(8,128)(2,1)S(1)}, bf16[3,16,1024]{2,1,0:T(8,128)(2,1)S(1)}, u32[]{:S(2)}, u32[]{:S(2)}) %collective-permute-start.2) | collective-permute-done | bytes 98336 | tf_op jit(solution)/shard_map/ppermute | solution.py:24
  96.1 0.0 collective-permute-done.3.other
  96.1 0.9 close.1
Async XLA Ops:
  0.6 8.0 %collective-permute-start.1 = (bf16[128,1024]{1,0:T(8,128)(2,1)}, bf16[128,1024]{1,0:T(8,128)(2,1)S(1)}, u32[]{:S(2)}, u32[]{:S(2)}) collective-permute-start(bf16[128,1024]{1,0:T(8,128)(2,1)} %mine.1), channel_id=1, source_target_pairs={{0,1},{1,0},{2,3},{3,2},{4,5},{5,4},{6,7},{7,6},{8,9},{9,8},{10,11... | collective-permute-start | bytes 786440 | tf_op jit(solution)/shard_map/ppermute | solution.py:298
  1.6 7.1 %collective-permute-start = (bf16[3,16,1024]{2,1,0:T(8,128)(2,1)S(1)}, bf16[3,16,1024]{2,1,0:T(8,128)(2,1)S(1)}, u32[]{:S(2)}, u32[]{:S(2)}) collective-permute-start(bf16[3,16,1024]{2,1,0:T(8,128)(2,1)S(1)} %tails.1), channel_id=1, source_target_pairs={{0,2},{2,4},{4,6},{6,8},{8,10},{10,12},{12,14},{14,16},{16,18},{18... | collective-permute-start | bytes 294920 | tf_op jit(solution)/shard_map/ppermute | solution.py:24
  8.6 38.9 %copy-start = (bf16[2,256,256]{2,1,0:T(8,128)(2,1)S(1)}, bf16[2,256,256]{2,1,0:T(8,128)(2,1)}, u32[]{:S(2)}) copy-start(bf16[2,256,256]{2,1,0:T(8,128)(2,1)} %constant.16.clone.back) | copy-start | bytes 786436
  8.6 38.9 %copy-start.1 = (bf16[2,256,256]{2,1,0:T(8,128)(2,1)S(1)}, bf16[2,256,256]{2,1,0:T(8,128)(2,1)}, u32[]{:S(2)}) copy-start(bf16[2,256,256]{2,1,0:T(8,128)(2,1)} %constant.15.clone.second) | copy-start | bytes 786436
  8.7 38.9 %copy-start.2 = (f32[2,128,128]{2,1,0:T(8,128)S(1)}, f32[2,128,128]{2,1,0:T(8,128)}, u32[]{:S(2)}) copy-start(f32[2,128,128]{2,1,0:T(8,128)} %constant.18.clone.twist) | copy-start | bytes 393220
  8.7 38.9 %copy-start.3 = (bf16[256,256]{1,0:T(8,128)(2,1)S(1)}, bf16[256,256]{1,0:T(8,128)(2,1)}, u32[]{:S(2)}) copy-start(bf16[256,256]{1,0:T(8,128)(2,1)} %constant.17.clone.last) | copy-start | bytes 393220
  8.7 38.9 %copy-start.4 = (bf16[256,256]{1,0:T(8,128)(2,1)S(1)}, bf16[256,256]{1,0:T(8,128)(2,1)}, u32[]{:S(2)}) copy-start(bf16[256,256]{1,0:T(8,128)(2,1)} %constant.14.clone.first) | copy-start | bytes 393220
  84.7 11.4 %collective-permute-start.3 = (f32[128,1024]{1,0:T(8,128)S(1)}, f32[128,1024]{1,0:T(8,128)S(1)}, u32[]{:S(2)}, u32[]{:S(2)}) collective-permute-start(f32[128,1024]{1,0:T(8,128)S(1)} %get-tuple-element.54), channel_id=1, source_target_pairs={{0,1},{1,0},{2,3},{3,2},{4,5},{5,4},{6,7},{7,6},{8,9},{9,8},{10,11... | collective-permute-start | bytes 1572872 | tf_op jit(solution)/shard_map/ppermute | solution.py:378
  84.8 11.3 %collective-permute-start.2 = (bf16[3,16,1024]{2,1,0:T(8,128)(2,1)S(1)}, bf16[3,16,1024]{2,1,0:T(8,128)(2,1)S(1)}, u32[]{:S(2)}, u32[]{:S(2)}) collective-permute-start(bf16[3,16,1024]{2,1,0:T(8,128)(2,1)S(1)} %get-tuple-element.52), channel_id=1, source_target_pairs={{2,0},{4,2},{6,4},{8,6},{10,8},{12,10},{14,12},{16,14},{18,16},{20... | collective-permute-start | bytes 294920 | tf_op jit(solution)/shard_map/ppermute | solution.py:24

commit v6 on v5

--- a/solution.py
+++ b/solution.py
@@ -63,16 +63,17 @@
     return high, low
 
 
-def tails_kernel(q, k, v, out, sems):
+def tails_kernel(q, k, v, out, near, sems):
     rows = q.shape[0]
     copies = [
-        pltpu.make_async_copy(x.at[pl.ds(rows - TAIL, TAIL), :], out.at[which], sems.at[which])
+        pltpu.make_async_copy(x.at[pl.ds(rows - TAIL, TAIL), :], near.at[which], sems.at[which])
         for which, x in enumerate((q, k, v))
     ]
     for copy in copies:
         copy.start()
-    for copy in copies:
+    for which, copy in enumerate(copies):
         copy.wait()
+        out[which] = near[which].astype(f32)[TAIL - EDGE :, :].astype(bf16)
 
 
 ACROSS = (((1,), (1,)), ((), ()))
@@ -124,7 +125,7 @@
         gg[:, part] = grad
         shorts = []
         for which, (before, after) in enumerate(((qs_in, qs), (ks_in, ks), (vs_in, vs))):
-            pad[0:EDGE, :] = halo[which, :, part].astype(f32)[TAIL - EDGE :, :]
+            pad[0:EDGE, :] = halo[which, :, part].astype(f32)
             top = before[0:EDGE, part]
             for shift in range(1, taps.shape[1]):
                 top = top + taps[which, shift : shift + 1, part] * pad[EDGE - shift : 2 * EDGE - shift, :]
@@ -213,7 +214,7 @@
             )
         ):
             to[:, part] = value
-            heads[which, :, part] = value[:TAIL, :].astype(bf16)
+            heads[which, :, part] = value[:EDGE, :].astype(bf16)
     for first in range(0, width, WIDE):
         part = slice(first, first + WIDE)
         other[:, part] = jnp.dot(gated[...], wo[:, part], preferred_element_type=f32)
@@ -260,7 +261,7 @@
     copies[0].start()
     pad[0:EDGE, :] = jnp.zeros((EDGE, width), f32)
     for which, to in enumerate((oq, ok, ov)):
-        pad[EDGE : 2 * EDGE, :] = after[which].astype(f32)[:EDGE, :]
+        pad[EDGE : 2 * EDGE, :] = after[which].astype(f32)
         end = ends[which, TAIL - EDGE :, :]
         for shift in range(1, taps.shape[1]):
             end = end + taps[which, shift : shift + 1, :] * pad[shift : shift + EDGE, :]
@@ -291,7 +292,7 @@
     flat = jax.ShapeDtypeStruct((rows, width), f32)
     half = jax.ShapeDtypeStruct((rows, width), bf16)
     fields = jax.ShapeDtypeStruct((parts, lines, rows), bf16)
-    edges = jax.ShapeDtypeStruct((3, TAIL, width), bf16)
+    edges = jax.ShapeDtypeStruct((3, EDGE, width), bf16)
     weights = jax.ShapeDtypeStruct((width, outs // 2), bf16)
     cost = pl.CostEstimate(flops=2 * rows * width * outs, bytes_accessed=8 * 2**20, transcendentals=0)
 
@@ -306,7 +307,7 @@
             in_specs=[hbm] * 3,
             out_specs=vmem,
             out_shape=edges,
-            scratch_shapes=[pltpu.SemaphoreType.DMA((3,))],
+            scratch_shapes=[pltpu.VMEM((3, TAIL, width), bf16), pltpu.SemaphoreType.DMA((3,))],
             compiler_params=params,
         )(*far[:3])
     halo = shifted(tails, "ctx", 1)

time: 97.4 us -> 95.9 us (0.985)
  waiting for transfers between devices: 7.38 us -> 5.73 us
    ppermute x2, waiting for transfers between devices: 7.38 us -> 5.73 us  [shifted(): lax.ppermute(value, axis, [(source, source + steps) for source in range(f...]
  transfers between devices with their start and end apart: 4 -> 4, of which waited for: 2 -> 1; matrix products, arithmetic and copies ran while one was open for 0% -> 0% of each run, Pallas kernels for 7% -> 7%
where the time goes in v6:
time: 95.9 us; the launch traced here: 95.6 us
  blocking collectives  68.4 us (71%)
  Pallas kernels  15 us (16%)
  waiting for transfers between devices  5.73 us (6%)
  starting transfers between devices  5.51 us (6%)
    all_to_all x1, blocking collectives, on_device(): lax.all_to_all(send, 'ctx', split_axis=0, concat_axis=0, tiled=True, axis...  37.6 us
    all_to_all x1, blocking collectives, on_device(): lax.all_to_all(solved, 'ctx', split_axis=0, concat_axis=0, tiled=True, ax...  30.8 us
    pallas_call x1, Pallas kernels, on_device(): pl.pallas_call(spectral_kernel, out_shape=fields, scratch_shapes=[pltpu.V...  6.13 us
    ppermute x2, waiting for transfers between devices, shifted(): lax.ppermute(value, axis, [(source, source + steps) for source in range(f...  5.73 us
    ppermute x2, starting transfers between devices, shifted(): lax.ppermute(value, axis, [(source, source + steps) for source in range(f...  5.32 us
    pallas_call x1, Pallas kernels, on_device(): pl.pallas_call(fetch_kernel, in_specs=[smem] + [hbm] * 7, out_specs=[vmem...  3.07 us
    pallas_call x1, Pallas kernels, on_device(): pl.pallas_call(project_kernel, in_specs=[vmem] * 7, out_specs=[hbm, vmem,...  2.58 us
  transfers between devices with their start and end apart: 4, of which 1 were waited for; matrix products, arithmetic and copies ran while one was open for 0% of the time, Pallas kernels for 7%

profile of v6, /device:TPU:30, one launch (start us, length us, event | category | flops | bytes accessed | tf_op | source)
XLA Modules:
  0.0 95.6 jit_solution(10246920608952320626)
XLA Ops:
  0.6 0.1 collective-permute-start.1
  0.7 0.8 tails.1
  1.6 3.4 %collective-permute-start = (bf16[3,8,1024]{2,1,0:T(8,128)(2,1)S(1)}, bf16[3,8,1024]{2,1,0:T(8,128)(2,1)S(1)}, u32[]{:S(2)}, u32[]{:S(2)}) collective-permute-start(bf16[3,8,1024]{2,1,0:T(8,128)(2,1)S(1)} %tails.1), channel_id=1, source_target_pairs={{0,2},{2,4},{4,6},{6,8},{8,10},{10,12},{12,14},{14,16},{16,18},{18... | collective-permute-start | bytes 147464 | tf_op jit(solution)/shard_map/ppermute | solution.py:24
  5.0 3.1 %fetch.1 = (f32[128,1024]{1,0:T(8,128)S(1)}, f32[128,1024]{1,0:T(8,128)S(1)}, f32[128,1024]{1,0:T(8,128)S(1)}, f32[128,1024]{1,0:T(8,128)S(1)}, f32[1024,128]{1,...) custom-call(s32[1]{0:T(128)} %bitcast.here, ...), custom_call_target="tpu_custom_call" | custom-call | flops 536870912 | bytes 8388608 | tf_op jit(solution)/shard_map/fetch/pallas_call | solution.py:316
  8.0 0.0 collective-permute-done.halo
  8.1 0.0 collective-permute-done.1.other
  8.1 0.0 copy-start
  8.1 0.0 copy-start.1
  8.1 0.0 copy-start.2
  8.1 0.0 copy-start.3
  8.1 0.0 copy-start.4
  8.1 1.0 %prepare.1 = (bf16[128,24,128]{2,1,0:T(8,128)(2,1)S(1)}, f32[128,1024]{1,0:T(8,128)S(1)}, f32[128,1024]{1,0:T(8,128)S(1)}, f32[128,1024]{1,0:T(8,128)S(1)}, f32[128,1024]{1,0:T(8,128)S(1)}) custom-call(bf16[3,8,1024]{2,1,0:T(8,128)(2,1)S(1)} %collective-permute-done.halo, f32[3,7,1024]{2,1,0:T(8,128)S(1)} %get-tuple-element.34.taps, ...), custom_call_target="tpu_custom_call" | custom-call | tf_op jit(solution)/shard_map/prepare/pallas_call | solution.py:344
  9.2 37.6 %all_to_all.10.x = bf16[128,24,128]{2,1,0:T(8,128)(2,1)S(1)} all-to-all(bf16[128,24,128]{2,1,0:T(8,128)(2,1)S(1)} %get-tuple-element.41), channel_id=1, replica_groups={{0,128,64,192,32,160,96,224,2,130,66,194,34,162,98,226,4,132,68,196,36,..., dimensions={0} | all-to-all | bytes 1572864 | tf_op jit(solution)/shard_map/all_to_all | solution.py:353
  46.8 0.0 copy-done
  46.8 0.0 copy-done.1
  46.8 0.0 copy-done.2
  46.8 0.0 copy-done.3
  46.8 0.0 copy-done.4
  46.9 6.1 %spectral.1 = bf16[128,24,128]{2,1,0:T(8,128)(2,1)S(1)} custom-call(bf16[128,24,128]{2,1,0:T(8,128)(2,1)S(1)} %all_to_all.10.x, bf16[256,256]{1,0:T(8,128)(2,1)S(1)} %copy-done.4, bf16[2,256,256]{2,1,0:T(8,128)(2,1)S(1)} %copy-done.1, bf16[2,256,256]{2,1,0:T(8,128)(2,1)S(1)} %copy-done, bf16[256,256]{1,0:T(8,128)(2,1)S(1)} %copy-done.3, ...), custom_call_target="tpu_custom_call" | custom-call | tf_op jit(solution)/shard_map/spectral/pallas_call | solution.py:358
  53.0 30.8 %all_to_all.11.landed = bf16[128,24,128]{2,1,0:T(8,128)(2,1)S(1)} all-to-all(bf16[128,24,128]{2,1,0:T(8,128)(2,1)S(1)} %spectral.1), channel_id=1, replica_groups={{0,128,64,192,32,160,96,224,2,130,66,194,34,162,98,226,4,132,68,196,36,..., dimensions={0} | all-to-all | bytes 1572864 | tf_op jit(solution)/shard_map/all_to_all | solution.py:365
  83.7 0.5 gate.1
  84.2 0.1 collective-permute-start.3
  84.3 1.9 %collective-permute-start.2 = (bf16[3,8,1024]{2,1,0:T(8,128)(2,1)S(1)}, bf16[3,8,1024]{2,1,0:T(8,128)(2,1)S(1)}, u32[]{:S(2)}, u32[]{:S(2)}) collective-permute-start(bf16[3,8,1024]{2,1,0:T(8,128)(2,1)S(1)} %get-tuple-element.52), channel_id=1, source_target_pairs={{2,0},{4,2},{6,4},{8,6},{10,8},{12,10},{14,12},{16,14},{18,16},{20... | collective-permute-start | bytes 147464 | tf_op jit(solution)/shard_map/ppermute | solution.py:24
  86.3 2.6 %project.1 = (f32[128,1024]{1,0:T(8,128)}, f32[128,1024]{1,0:T(8,128)S(1)}, f32[3,16,1024]{2,1,0:T(8,128)S(1)}, bf16[128,1024]{1,0:T(8,128)(2,1)}, bf16[128,1024]{1,0:T(8,128)(2,1)}, /*index=5*/bf16[128,1024]{1,0:T(8,128)(2,1)}) custom-call(bf16[128,24,128]{2,1,0:T(8,128)(2,1)S(1)} %all_to_all.11.landed, bf16[128,1024]{1,0:T(8,128)(2,1)S(1)} %get-tuple-element.46.gated, ...), custom_call_target="tpu_custom_call" | custom-call | flops 536870912 | bytes 8388608 | tf_op jit(solution)/shard_map/project/pallas_call | solution.py:382
  88.9 5.7 %collective-permute-done.2.after = bf16[3,8,1024]{2,1,0:T(8,128)(2,1)S(1)} collective-permute-done((bf16[3,8,1024]{2,1,0:T(8,128)(2,1)S(1)}, bf16[3,8,1024]{2,1,0:T(8,128)(2,1)S(1)}, u32[]{:S(2)}, u32[]{:S(2)}) %collective-permute-start.2) | collective-permute-done | bytes 49184 | tf_op jit(solution)/shard_map/ppermute | solution.py:24
  94.6 0.0 collective-permute-done.3.other
  94.6 0.9 close.1
Async XLA Ops:
  0.6 7.4 %collective-permute-start.1 = (bf16[128,1024]{1,0:T(8,128)(2,1)}, bf16[128,1024]{1,0:T(8,128)(2,1)S(1)}, u32[]{:S(2)}, u32[]{:S(2)}) collective-permute-start(bf16[128,1024]{1,0:T(8,128)(2,1)} %mine.1), channel_id=1, source_target_pairs={{0,1},{1,0},{2,3},{3,2},{4,5},{5,4},{6,7},{7,6},{8,9},{9,8},{10,11... | collective-permute-start | bytes 786440 | tf_op jit(solution)/shard_map/ppermute | solution.py:299
  1.6 6.5 %collective-permute-start = (bf16[3,8,1024]{2,1,0:T(8,128)(2,1)S(1)}, bf16[3,8,1024]{2,1,0:T(8,128)(2,1)S(1)}, u32[]{:S(2)}, u32[]{:S(2)}) collective-permute-start(bf16[3,8,1024]{2,1,0:T(8,128)(2,1)S(1)} %tails.1), channel_id=1, source_target_pairs={{0,2},{2,4},{4,6},{6,8},{8,10},{10,12},{12,14},{14,16},{16,18},{18... | collective-permute-start | bytes 147464 | tf_op jit(solution)/shard_map/ppermute | solution.py:24
  8.1 38.8 %copy-start = (bf16[2,256,256]{2,1,0:T(8,128)(2,1)S(1)}, bf16[2,256,256]{2,1,0:T(8,128)(2,1)}, u32[]{:S(2)}) copy-start(bf16[2,256,256]{2,1,0:T(8,128)(2,1)} %constant.16.clone.back) | copy-start | bytes 786436
  8.1 38.7 %copy-start.1 = (bf16[2,256,256]{2,1,0:T(8,128)(2,1)S(1)}, bf16[2,256,256]{2,1,0:T(8,128)(2,1)}, u32[]{:S(2)}) copy-start(bf16[2,256,256]{2,1,0:T(8,128)(2,1)} %constant.15.clone.second) | copy-start | bytes 786436
  8.1 38.7 %copy-start.2 = (f32[2,128,128]{2,1,0:T(8,128)S(1)}, f32[2,128,128]{2,1,0:T(8,128)}, u32[]{:S(2)}) copy-start(f32[2,128,128]{2,1,0:T(8,128)} %constant.18.clone.twist) | copy-start | bytes 393220
  8.1 38.7 %copy-start.3 = (bf16[256,256]{1,0:T(8,128)(2,1)S(1)}, bf16[256,256]{1,0:T(8,128)(2,1)}, u32[]{:S(2)}) copy-start(bf16[256,256]{1,0:T(8,128)(2,1)} %constant.17.clone.last) | copy-start | bytes 393220
  8.1 38.7 %copy-start.4 = (bf16[256,256]{1,0:T(8,128)(2,1)S(1)}, bf16[256,256]{1,0:T(8,128)(2,1)}, u32[]{:S(2)}) copy-start(bf16[256,256]{1,0:T(8,128)(2,1)} %constant.14.clone.first) | copy-start | bytes 393220
  84.2 10.3 %collective-permute-start.3 = (f32[128,1024]{1,0:T(8,128)S(1)}, f32[128,1024]{1,0:T(8,128)S(1)}, u32[]{:S(2)}, u32[]{:S(2)}) collective-permute-start(f32[128,1024]{1,0:T(8,128)S(1)} %get-tuple-element.54), channel_id=1, source_target_pairs={{0,1},{1,0},{2,3},{3,2},{4,5},{5,4},{6,7},{7,6},{8,9},{9,8},{10,11... | collective-permute-start | bytes 1572872 | tf_op jit(solution)/shard_map/ppermute | solution.py:379
  84.3 10.2 %collective-permute-start.2 = (bf16[3,8,1024]{2,1,0:T(8,128)(2,1)S(1)}, bf16[3,8,1024]{2,1,0:T(8,128)(2,1)S(1)}, u32[]{:S(2)}, u32[]{:S(2)}) collective-permute-start(bf16[3,8,1024]{2,1,0:T(8,128)(2,1)S(1)} %get-tuple-element.52), channel_id=1, source_target_pairs={{2,0},{4,2},{6,4},{8,6},{10,8},{12,10},{14,12},{16,14},{18,16},{20... | collective-permute-start | bytes 147464 | tf_op jit(solution)/shard_map/ppermute | solution.py:24

commit v7 on v6

--- a/solution.py
+++ b/solution.py
@@ -350,6 +350,7 @@
             compiler_params=params,
         )(halo, taps_near, qs, ks, vs, gg, ft, grad_other, wo)
 
+    send = pltpu.with_memory_space_constraint(send, pltpu.HBM)
     arrived = lax.all_to_all(
         send, "ctx", split_axis=0, concat_axis=0, tiled=True, axis_index_groups=[order]
     )
@@ -362,6 +363,7 @@
             compiler_params=params,
         )(arrived, *tables(parts, rows, gain, order))
 
+    solved = pltpu.with_memory_space_constraint(solved, pltpu.HBM)
     landed = lax.all_to_all(
         solved, "ctx", split_axis=0, concat_axis=0, tiled=True, axis_index_groups=[order]
     )

time: 95.9 us -> 99.1 us (1.033)
  Pallas kernels: 15 us -> 18.4 us
  waiting for transfers between devices: 5.73 us -> 4.61 us
    pallas_call x1, Pallas kernels: 6.13 us -> 7.29 us  [on_device(): pl.pallas_call(spectral_kernel, out_shape=fields, scratch_shapes=[pltpu.V...]
    pallas_call x1, Pallas kernels: 0.49 us -> 1.62 us  [on_device(): pl.pallas_call(gate_kernel, in_specs=[vmem] * 6, out_specs=[vmem] * 6, ou...]
    ppermute x2, waiting for transfers between devices: 5.73 us -> 4.6 us  [shifted(): lax.ppermute(value, axis, [(source, source + steps) for source in range(f...]
    pallas_call x1, Pallas kernels: 2.58 us -> 3.71 us  [on_device(): pl.pallas_call(project_kernel, in_specs=[vmem] * 7, out_specs=[hbm, vmem,...]
  transfers between devices with their start and end apart: 4 -> 4, of which waited for: 1 -> 1; matrix products, arithmetic and copies ran while one was open for 0% -> 0% of each run, Pallas kernels for 7% -> 8%
where the time goes in v7:
time: 99.1 us; the launch traced here: 98.1 us
  blocking collectives  68.6 us (69%)
  Pallas kernels  18.4 us (19%)
  starting transfers between devices  5.51 us (6%)
  waiting for transfers between devices  4.61 us (5%)
    all_to_all x1, blocking collectives, on_device(): lax.all_to_all(send, 'ctx', split_axis=0, concat_axis=0, tiled=True, axis...  37.8 us
    all_to_all x1, blocking collectives, on_device(): lax.all_to_all(solved, 'ctx', split_axis=0, concat_axis=0, tiled=True, ax...  30.9 us
    pallas_call x1, Pallas kernels, on_device(): pl.pallas_call(spectral_kernel, out_shape=fields, scratch_shapes=[pltpu.V...  7.29 us
    ppermute x2, starting transfers between devices, shifted(): lax.ppermute(value, axis, [(source, source + steps) for source in range(f...  5.32 us
    ppermute x2, waiting for transfers between devices, shifted(): lax.ppermute(value, axis, [(source, source + steps) for source in range(f...  4.6 us
    pallas_call x1, Pallas kernels, on_device(): pl.pallas_call(project_kernel, in_specs=[vmem] * 7, out_specs=[hbm, vmem,...  3.71 us
    pallas_call x1, Pallas kernels, on_device(): pl.pallas_call(fetch_kernel, in_specs=[smem] + [hbm] * 7, out_specs=[vmem...  3.06 us
  transfers between devices with their start and end apart: 4, of which 1 were waited for; matrix products, arithmetic and copies ran while one was open for 0% of the time, Pallas kernels for 8%

profile of v7, /device:TPU:30, one launch (start us, length us, event | category | flops | bytes accessed | tf_op | source)
XLA Modules:
  0.0 98.1 jit_solution(12686303448357635732)
XLA Ops:
  0.6 0.1 collective-permute-start.1
  0.7 0.8 tails.1
  1.6 3.4 %collective-permute-start = (bf16[3,8,1024]{2,1,0:T(8,128)(2,1)S(1)}, bf16[3,8,1024]{2,1,0:T(8,128)(2,1)S(1)}, u32[]{:S(2)}, u32[]{:S(2)}) collective-permute-start(bf16[3,8,1024]{2,1,0:T(8,128)(2,1)S(1)} %tails.1), channel_id=1, source_target_pairs={{0,2},{2,4},{4,6},{6,8},{8,10},{10,12},{12,14},{14,16},{16,18},{18... | collective-permute-start | bytes 147464 | tf_op jit(solution)/shard_map/ppermute | solution.py:24
  5.0 3.1 %fetch.1 = (f32[128,1024]{1,0:T(8,128)S(1)}, f32[128,1024]{1,0:T(8,128)S(1)}, f32[128,1024]{1,0:T(8,128)S(1)}, f32[128,1024]{1,0:T(8,128)S(1)}, f32[1024,128]{1,...) custom-call(s32[1]{0:T(128)} %bitcast.here, ...), custom_call_target="tpu_custom_call" | custom-call | flops 536870912 | bytes 8388608 | tf_op jit(solution)/shard_map/fetch/pallas_call | solution.py:316
  8.0 0.0 collective-permute-done.halo
  8.1 0.0 collective-permute-done.1.other
  8.1 0.0 copy-start
  8.1 0.0 copy-start.1
  8.1 0.0 copy-start.2
  8.1 0.0 copy-start.3
  8.1 0.0 copy-start.4
  8.1 1.0 %prepare.1 = (bf16[128,24,128]{2,1,0:T(8,128)(2,1)S(1)}, f32[128,1024]{1,0:T(8,128)S(1)}, f32[128,1024]{1,0:T(8,128)S(1)}, f32[128,1024]{1,0:T(8,128)S(1)}, f32[128,1024]{1,0:T(8,128)S(1)}) custom-call(bf16[3,8,1024]{2,1,0:T(8,128)(2,1)S(1)} %collective-permute-done.halo, f32[3,7,1024]{2,1,0:T(8,128)S(1)} %get-tuple-element.34.taps, ...), custom_call_target="tpu_custom_call" | custom-call | tf_op jit(solution)/shard_map/prepare/pallas_call | solution.py:344
  9.2 37.8 %all_to_all.10.x = bf16[128,24,128]{2,1,0:T(8,128)(2,1)} all-to-all(bf16[128,24,128]{2,1,0:T(8,128)(2,1)S(1)} %get-tuple-element.41), channel_id=1, replica_groups={{0,128,64,192,32,160,96,224,2,130,66,194,34,162,98,226,4,132,68,196,36,..., dimensions={0} | all-to-all | bytes 1572864 | tf_op jit(solution)/shard_map/all_to_all | solution.py:354
  46.9 0.0 copy-done
  46.9 0.0 copy-done.1
  46.9 0.0 copy-done.2
  46.9 0.0 copy-done.3
  46.9 0.0 copy-done.4
  47.0 7.3 %spectral.1 = bf16[128,24,128]{2,1,0:T(8,128)(2,1)S(1)} custom-call(bf16[128,24,128]{2,1,0:T(8,128)(2,1)} %all_to_all.10.x, bf16[256,256]{1,0:T(8,128)(2,1)S(1)} %copy-done.4, bf16[2,256,256]{2,1,0:T(8,128)(2,1)S(1)} %copy-done.1, bf16[2,256,256]{2,1,0:T(8,128)(2,1)S(1)} %copy-done, bf16[256,256]{1,0:T(8,128)(2,1)S(1)} %copy-done.3, f32[2,128,128]{2,1,0:T(8,128)S(1)} %copy-done.2), custom_call_target="tpu_custom_call" | custom-call | tf_op jit(solution)/shard_map/spectral/pallas_call | solution.py:359
  54.3 30.9 %all_to_all.11.landed = bf16[128,24,128]{2,1,0:T(8,128)(2,1)} all-to-all(bf16[128,24,128]{2,1,0:T(8,128)(2,1)S(1)} %spectral.1), channel_id=1, replica_groups={{0,128,64,192,32,160,96,224,2,130,66,194,34,162,98,226,4,132,68,196,36,..., dimensions={0} | all-to-all | bytes 1572864 | tf_op jit(solution)/shard_map/all_to_all | solution.py:367
  85.1 1.6 %gate.1 = (f32[128,1024]{1,0:T(8,128)S(1)}, f32[128,1024]{1,0:T(8,128)S(1)}, f32[128,1024]{1,0:T(8,128)S(1)}, bf16[3,8,1024]{2,1,0:T(8,128)(2,1)S(1)}, bf16[128,...) custom-call(bf16[128,24,128]{2,1,0:T(8,128)(2,1)} %all_to_all.11.landed, f32[128,1024]{1,0:T(8,128)S(1)} %get-tuple-element.42.qs, ...), custom_call_target="tpu_custom_call" | custom-call | tf_op jit(solution)/shard_map/gate/pallas_call | solution.py:372
  86.7 0.1 collective-permute-start.3
  86.8 1.9 %collective-permute-start.2 = (bf16[3,8,1024]{2,1,0:T(8,128)(2,1)S(1)}, bf16[3,8,1024]{2,1,0:T(8,128)(2,1)S(1)}, u32[]{:S(2)}, u32[]{:S(2)}) collective-permute-start(bf16[3,8,1024]{2,1,0:T(8,128)(2,1)S(1)} %get-tuple-element.52), channel_id=1, source_target_pairs={{2,0},{4,2},{6,4},{8,6},{10,8},{12,10},{14,12},{16,14},{18,16},{20... | collective-permute-start | bytes 147464 | tf_op jit(solution)/shard_map/ppermute | solution.py:24
  88.8 3.7 %project.1 = (f32[128,1024]{1,0:T(8,128)}, f32[128,1024]{1,0:T(8,128)S(1)}, f32[3,16,1024]{2,1,0:T(8,128)S(1)}, bf16[128,1024]{1,0:T(8,128)(2,1)}, bf16[128,1024]{1,0:T(8,128)(2,1)}, /*index=5*/bf16[128,1024]{1,0:T(8,128)(2,1)}) custom-call(bf16[128,24,128]{2,1,0:T(8,128)(2,1)} %all_to_all.11.landed, bf16[128,1024]{1,0:T(8,128)(2,1)S(1)} %get-tuple-element.46.gated, ...), custom_call_target="tpu_custom_call" | custom-call | flops 536870912 | bytes 8388608 | tf_op jit(solution)/shard_map/project/pallas_call | solution.py:384
  92.5 4.6 %collective-permute-done.2.after = bf16[3,8,1024]{2,1,0:T(8,128)(2,1)S(1)} collective-permute-done((bf16[3,8,1024]{2,1,0:T(8,128)(2,1)S(1)}, bf16[3,8,1024]{2,1,0:T(8,128)(2,1)S(1)}, u32[]{:S(2)}, u32[]{:S(2)}) %collective-permute-start.2) | collective-permute-done | bytes 49184 | tf_op jit(solution)/shard_map/ppermute | solution.py:24
  97.1 0.0 collective-permute-done.3.other
  97.1 0.9 close.1
Async XLA Ops:
  0.6 7.4 %collective-permute-start.1 = (bf16[128,1024]{1,0:T(8,128)(2,1)}, bf16[128,1024]{1,0:T(8,128)(2,1)S(1)}, u32[]{:S(2)}, u32[]{:S(2)}) collective-permute-start(bf16[128,1024]{1,0:T(8,128)(2,1)} %mine.1), channel_id=1, source_target_pairs={{0,1},{1,0},{2,3},{3,2},{4,5},{5,4},{6,7},{7,6},{8,9},{9,8},{10,11... | collective-permute-start | bytes 786440 | tf_op jit(solution)/shard_map/ppermute | solution.py:299
  1.6 6.5 %collective-permute-start = (bf16[3,8,1024]{2,1,0:T(8,128)(2,1)S(1)}, bf16[3,8,1024]{2,1,0:T(8,128)(2,1)S(1)}, u32[]{:S(2)}, u32[]{:S(2)}) collective-permute-start(bf16[3,8,1024]{2,1,0:T(8,128)(2,1)S(1)} %tails.1), channel_id=1, source_target_pairs={{0,2},{2,4},{4,6},{6,8},{8,10},{10,12},{12,14},{14,16},{16,18},{18... | collective-permute-start | bytes 147464 | tf_op jit(solution)/shard_map/ppermute | solution.py:24
  8.1 38.9 %copy-start = (bf16[2,256,256]{2,1,0:T(8,128)(2,1)S(1)}, bf16[2,256,256]{2,1,0:T(8,128)(2,1)}, u32[]{:S(2)}) copy-start(bf16[2,256,256]{2,1,0:T(8,128)(2,1)} %constant.16.clone.back) | copy-start | bytes 786436
  8.1 38.9 %copy-start.1 = (bf16[2,256,256]{2,1,0:T(8,128)(2,1)S(1)}, bf16[2,256,256]{2,1,0:T(8,128)(2,1)}, u32[]{:S(2)}) copy-start(bf16[2,256,256]{2,1,0:T(8,128)(2,1)} %constant.15.clone.second) | copy-start | bytes 786436
  8.1 38.8 %copy-start.2 = (f32[2,128,128]{2,1,0:T(8,128)S(1)}, f32[2,128,128]{2,1,0:T(8,128)}, u32[]{:S(2)}) copy-start(f32[2,128,128]{2,1,0:T(8,128)} %constant.18.clone.twist) | copy-start | bytes 393220
  8.1 38.8 %copy-start.3 = (bf16[256,256]{1,0:T(8,128)(2,1)S(1)}, bf16[256,256]{1,0:T(8,128)(2,1)}, u32[]{:S(2)}) copy-start(bf16[256,256]{1,0:T(8,128)(2,1)} %constant.17.clone.last) | copy-start | bytes 393220
  8.1 38.8 %copy-start.4 = (bf16[256,256]{1,0:T(8,128)(2,1)S(1)}, bf16[256,256]{1,0:T(8,128)(2,1)}, u32[]{:S(2)}) copy-start(bf16[256,256]{1,0:T(8,128)(2,1)} %constant.14.clone.first) | copy-start | bytes 393220
  86.7 10.3 %collective-permute-start.3 = (f32[128,1024]{1,0:T(8,128)S(1)}, f32[128,1024]{1,0:T(8,128)S(1)}, u32[]{:S(2)}, u32[]{:S(2)}) collective-permute-start(f32[128,1024]{1,0:T(8,128)S(1)} %get-tuple-element.54), channel_id=1, source_target_pairs={{0,1},{1,0},{2,3},{3,2},{4,5},{5,4},{6,7},{7,6},{8,9},{9,8},{10,11... | collective-permute-start | bytes 1572872 | tf_op jit(solution)/shard_map/ppermute | solution.py:381
  86.8 10.2 %collective-permute-start.2 = (bf16[3,8,1024]{2,1,0:T(8,128)(2,1)S(1)}, bf16[3,8,1024]{2,1,0:T(8,128)(2,1)S(1)}, u32[]{:S(2)}, u32[]{:S(2)}) collective-permute-start(bf16[3,8,1024]{2,1,0:T(8,128)(2,1)S(1)} %get-tuple-element.52), channel_id=1, source_target_pairs={{2,0},{4,2},{6,4},{8,6},{10,8},{12,10},{14,12},{16,14},{18,16},{20... | collective-permute-start | bytes 147464 | tf_op jit(solution)/shard_map/ppermute | solution.py:24

commit v8 on v6

--- a/solution.py
+++ b/solution.py
@@ -138,7 +138,7 @@
         send[first // group : (first + WIDE) // group] = jnp.concatenate(turned, axis=1).astype(bf16)
 
 
-BATCH = 4
+BATCH = 8
 
 
 def spectral_kernel(x, first, second, back, last, twist, out, buf):
@@ -233,7 +233,11 @@
     copies = [pltpu.make_async_copy(turned, gf, sems.at[3])]
     copies[0].start()
     pad[rows : rows + EDGE, :] = jnp.zeros((EDGE, LANES), f32)
+    chunks = range(0, width, WIDE)
     for which, (value, to) in enumerate(((gq, oq), (gk, ok), (gv, ov))):
+        for first in chunks[which::3]:
+            part = slice(first, first + WIDE)
+            mine[:, part] = jnp.dot(gated[...], wm[:, part], preferred_element_type=f32)
         for first in range(0, width, LANES):
             part = slice(first, first + LANES)
             pad[0:rows, :] = value[:, part]
@@ -245,9 +249,6 @@
         copy = pltpu.make_async_copy(rounded.at[which], to, sems.at[which])
         copy.start()
         copies.append(copy)
-    for first in range(0, width, WIDE):
-        part = slice(first, first + WIDE)
-        mine[:, part] = jnp.dot(gated[...], wm[:, part], preferred_element_type=f32)
     for copy in copies:
         copy.wait()
 

time: 95.9 us -> 95.7 us (level)
  no operation moved by 1% of the time
where the time goes in v8:
time: 95.7 us; the launch traced here: 95.4 us
  blocking collectives  68.4 us (71%)
  Pallas kernels  14.8 us (15%)
  waiting for transfers between devices  5.73 us (6%)
  starting transfers between devices  5.51 us (6%)
    all_to_all x1, blocking collectives, on_device(): lax.all_to_all(send, 'ctx', split_axis=0, concat_axis=0, tiled=True, axis...  37.6 us
    all_to_all x1, blocking collectives, on_device(): lax.all_to_all(solved, 'ctx', split_axis=0, concat_axis=0, tiled=True, ax...  30.7 us
    pallas_call x1, Pallas kernels, on_device(): pl.pallas_call(spectral_kernel, out_shape=fields, scratch_shapes=[pltpu.V...  5.95 us
    ppermute x2, waiting for transfers between devices, shifted(): lax.ppermute(value, axis, [(source, source + steps) for source in range(f...  5.73 us
    ppermute x2, starting transfers between devices, shifted(): lax.ppermute(value, axis, [(source, source + steps) for source in range(f...  5.32 us
    pallas_call x1, Pallas kernels, on_device(): pl.pallas_call(fetch_kernel, in_specs=[smem] + [hbm] * 7, out_specs=[vmem...  3.07 us
    pallas_call x1, Pallas kernels, on_device(): pl.pallas_call(project_kernel, in_specs=[vmem] * 7, out_specs=[hbm, vmem,...  2.58 us
  transfers between devices with their start and end apart: 4, of which 1 were waited for; matrix products, arithmetic and copies ran while one was open for 0% of the time, Pallas kernels for 7%

profile of v8, /device:TPU:30, one launch (start us, length us, event | category | flops | bytes accessed | tf_op | source)
XLA Modules:
  0.0 95.4 jit_solution(16126637138015664973)
XLA Ops:
  0.6 0.1 collective-permute-start.1
  0.7 0.8 tails.1
  1.6 3.4 %collective-permute-start = (bf16[3,8,1024]{2,1,0:T(8,128)(2,1)S(1)}, bf16[3,8,1024]{2,1,0:T(8,128)(2,1)S(1)}, u32[]{:S(2)}, u32[]{:S(2)}) collective-permute-start(bf16[3,8,1024]{2,1,0:T(8,128)(2,1)S(1)} %tails.1), channel_id=1, source_target_pairs={{0,2},{2,4},{4,6},{6,8},{8,10},{10,12},{12,14},{14,16},{16,18},{18... | collective-permute-start | bytes 147464 | tf_op jit(solution)/shard_map/ppermute | solution.py:24
  5.0 3.1 %fetch.1 = (f32[128,1024]{1,0:T(8,128)S(1)}, f32[128,1024]{1,0:T(8,128)S(1)}, f32[128,1024]{1,0:T(8,128)S(1)}, f32[128,1024]{1,0:T(8,128)S(1)}, f32[1024,128]{1,...) custom-call(s32[1]{0:T(128)} %bitcast.here, ...), custom_call_target="tpu_custom_call" | custom-call | flops 536870912 | bytes 8388608 | tf_op jit(solution)/shard_map/fetch/pallas_call | solution.py:317
  8.0 0.0 collective-permute-done.halo
  8.1 0.0 collective-permute-done.1.other
  8.1 0.0 copy-start
  8.1 0.0 copy-start.1
  8.1 0.0 copy-start.2
  8.1 0.0 copy-start.3
  8.1 0.0 copy-start.4
  8.1 1.0 %prepare.1 = (bf16[128,24,128]{2,1,0:T(8,128)(2,1)S(1)}, f32[128,1024]{1,0:T(8,128)S(1)}, f32[128,1024]{1,0:T(8,128)S(1)}, f32[128,1024]{1,0:T(8,128)S(1)}, f32[128,1024]{1,0:T(8,128)S(1)}) custom-call(bf16[3,8,1024]{2,1,0:T(8,128)(2,1)S(1)} %collective-permute-done.halo, f32[3,7,1024]{2,1,0:T(8,128)S(1)} %get-tuple-element.34.taps, ...), custom_call_target="tpu_custom_call" | custom-call | tf_op jit(solution)/shard_map/prepare/pallas_call | solution.py:345
  9.2 37.6 %all_to_all.10.x = bf16[128,24,128]{2,1,0:T(8,128)(2,1)S(1)} all-to-all(bf16[128,24,128]{2,1,0:T(8,128)(2,1)S(1)} %get-tuple-element.41), channel_id=1, replica_groups={{0,128,64,192,32,160,96,224,2,130,66,194,34,162,98,226,4,132,68,196,36,..., dimensions={0} | all-to-all | bytes 1572864 | tf_op jit(solution)/shard_map/all_to_all | solution.py:354
  46.8 0.0 copy-done
  46.8 0.0 copy-done.1
  46.8 0.0 copy-done.2
  46.8 0.0 copy-done.3
  46.8 0.0 copy-done.4
  46.9 5.9 %spectral.1 = bf16[128,24,128]{2,1,0:T(8,128)(2,1)S(1)} custom-call(bf16[128,24,128]{2,1,0:T(8,128)(2,1)S(1)} %all_to_all.10.x, bf16[256,256]{1,0:T(8,128)(2,1)S(1)} %copy-done.4, bf16[2,256,256]{2,1,0:T(8,128)(2,1)S(1)} %copy-done.1, bf16[2,256,256]{2,1,0:T(8,128)(2,1)S(1)} %copy-done, bf16[256,256]{1,0:T(8,128)(2,1)S(1)} %copy-done.3, ...), custom_call_target="tpu_custom_call" | custom-call | tf_op jit(solution)/shard_map/spectral/pallas_call | solution.py:359
  52.8 30.7 %all_to_all.11.landed = bf16[128,24,128]{2,1,0:T(8,128)(2,1)S(1)} all-to-all(bf16[128,24,128]{2,1,0:T(8,128)(2,1)S(1)} %spectral.1), channel_id=1, replica_groups={{0,128,64,192,32,160,96,224,2,130,66,194,34,162,98,226,4,132,68,196,36,..., dimensions={0} | all-to-all | bytes 1572864 | tf_op jit(solution)/shard_map/all_to_all | solution.py:366
  83.6 0.5 gate.1
  84.1 0.1 collective-permute-start.3
  84.2 1.9 %collective-permute-start.2 = (bf16[3,8,1024]{2,1,0:T(8,128)(2,1)S(1)}, bf16[3,8,1024]{2,1,0:T(8,128)(2,1)S(1)}, u32[]{:S(2)}, u32[]{:S(2)}) collective-permute-start(bf16[3,8,1024]{2,1,0:T(8,128)(2,1)S(1)} %get-tuple-element.52), channel_id=1, source_target_pairs={{2,0},{4,2},{6,4},{8,6},{10,8},{12,10},{14,12},{16,14},{18,16},{20... | collective-permute-start | bytes 147464 | tf_op jit(solution)/shard_map/ppermute | solution.py:24
  86.1 2.6 %project.1 = (f32[128,1024]{1,0:T(8,128)}, f32[128,1024]{1,0:T(8,128)S(1)}, f32[3,16,1024]{2,1,0:T(8,128)S(1)}, bf16[128,1024]{1,0:T(8,128)(2,1)}, bf16[128,1024]{1,0:T(8,128)(2,1)}, /*index=5*/bf16[128,1024]{1,0:T(8,128)(2,1)}) custom-call(bf16[128,24,128]{2,1,0:T(8,128)(2,1)S(1)} %all_to_all.11.landed, bf16[128,1024]{1,0:T(8,128)(2,1)S(1)} %get-tuple-element.46.gated, ...), custom_call_target="tpu_custom_call" | custom-call | flops 536870912 | bytes 8388608 | tf_op jit(solution)/shard_map/project/pallas_call | solution.py:383
  88.7 5.7 %collective-permute-done.2.after = bf16[3,8,1024]{2,1,0:T(8,128)(2,1)S(1)} collective-permute-done((bf16[3,8,1024]{2,1,0:T(8,128)(2,1)S(1)}, bf16[3,8,1024]{2,1,0:T(8,128)(2,1)S(1)}, u32[]{:S(2)}, u32[]{:S(2)}) %collective-permute-start.2) | collective-permute-done | bytes 49184 | tf_op jit(solution)/shard_map/ppermute | solution.py:24
  94.4 0.0 collective-permute-done.3.other
  94.4 0.9 close.1
Async XLA Ops:
  0.6 7.4 %collective-permute-start.1 = (bf16[128,1024]{1,0:T(8,128)(2,1)}, bf16[128,1024]{1,0:T(8,128)(2,1)S(1)}, u32[]{:S(2)}, u32[]{:S(2)}) collective-permute-start(bf16[128,1024]{1,0:T(8,128)(2,1)} %mine.1), channel_id=1, source_target_pairs={{0,1},{1,0},{2,3},{3,2},{4,5},{5,4},{6,7},{7,6},{8,9},{9,8},{10,11... | collective-permute-start | bytes 786440 | tf_op jit(solution)/shard_map/ppermute | solution.py:300
  1.6 6.5 %collective-permute-start = (bf16[3,8,1024]{2,1,0:T(8,128)(2,1)S(1)}, bf16[3,8,1024]{2,1,0:T(8,128)(2,1)S(1)}, u32[]{:S(2)}, u32[]{:S(2)}) collective-permute-start(bf16[3,8,1024]{2,1,0:T(8,128)(2,1)S(1)} %tails.1), channel_id=1, source_target_pairs={{0,2},{2,4},{4,6},{6,8},{8,10},{10,12},{12,14},{14,16},{16,18},{18... | collective-permute-start | bytes 147464 | tf_op jit(solution)/shard_map/ppermute | solution.py:24
  8.1 38.8 %copy-start = (bf16[2,256,256]{2,1,0:T(8,128)(2,1)S(1)}, bf16[2,256,256]{2,1,0:T(8,128)(2,1)}, u32[]{:S(2)}) copy-start(bf16[2,256,256]{2,1,0:T(8,128)(2,1)} %constant.16.clone.back) | copy-start | bytes 786436
  8.1 38.7 %copy-start.1 = (bf16[2,256,256]{2,1,0:T(8,128)(2,1)S(1)}, bf16[2,256,256]{2,1,0:T(8,128)(2,1)}, u32[]{:S(2)}) copy-start(bf16[2,256,256]{2,1,0:T(8,128)(2,1)} %constant.15.clone.second) | copy-start | bytes 786436
  8.1 38.7 %copy-start.2 = (f32[2,128,128]{2,1,0:T(8,128)S(1)}, f32[2,128,128]{2,1,0:T(8,128)}, u32[]{:S(2)}) copy-start(f32[2,128,128]{2,1,0:T(8,128)} %constant.18.clone.twist) | copy-start | bytes 393220
  8.1 38.7 %copy-start.3 = (bf16[256,256]{1,0:T(8,128)(2,1)S(1)}, bf16[256,256]{1,0:T(8,128)(2,1)}, u32[]{:S(2)}) copy-start(bf16[256,256]{1,0:T(8,128)(2,1)} %constant.17.clone.last) | copy-start | bytes 393220
  8.1 38.7 %copy-start.4 = (bf16[256,256]{1,0:T(8,128)(2,1)S(1)}, bf16[256,256]{1,0:T(8,128)(2,1)}, u32[]{:S(2)}) copy-start(bf16[256,256]{1,0:T(8,128)(2,1)} %constant.14.clone.first) | copy-start | bytes 393220
  84.1 10.3 %collective-permute-start.3 = (f32[128,1024]{1,0:T(8,128)S(1)}, f32[128,1024]{1,0:T(8,128)S(1)}, u32[]{:S(2)}, u32[]{:S(2)}) collective-permute-start(f32[128,1024]{1,0:T(8,128)S(1)} %get-tuple-element.54), channel_id=1, source_target_pairs={{0,1},{1,0},{2,3},{3,2},{4,5},{5,4},{6,7},{7,6},{8,9},{9,8},{10,11... | collective-permute-start | bytes 1572872 | tf_op jit(solution)/shard_map/ppermute | solution.py:380
  84.2 10.2 %collective-permute-start.2 = (bf16[3,8,1024]{2,1,0:T(8,128)(2,1)S(1)}, bf16[3,8,1024]{2,1,0:T(8,128)(2,1)S(1)}, u32[]{:S(2)}, u32[]{:S(2)}) collective-permute-start(bf16[3,8,1024]{2,1,0:T(8,128)(2,1)S(1)} %get-tuple-element.52), channel_id=1, source_target_pairs={{2,0},{4,2},{6,4},{8,6},{10,8},{12,10},{14,12},{16,14},{18,16},{20... | collective-permute-start | bytes 147464 | tf_op jit(solution)/shard_map/ppermute | solution.py:24

commit v9 on v6

--- a/solution.py
+++ b/solution.py
@@ -130,7 +130,7 @@
             for shift in range(1, taps.shape[1]):
                 top = top + taps[which, shift : shift + 1, part] * pad[EDGE - shift : 2 * EDGE - shift, :]
             value = jnp.concatenate([top, before[EDGE:, part]], 0)
-            after[:, part] = value
+            after[0:EDGE, part] = top
             shorts.append(value)
         mixed = (shorts[1] * shorts[2]).T
         grad_long = (grad * shorts[0]).T
@@ -346,6 +346,7 @@
             in_specs=[vmem] * 9,
             out_specs=[vmem] * 5,
             out_shape=[fields, flat, flat, flat, flat],
+            input_output_aliases={2: 1, 3: 2, 4: 3},
             scratch_shapes=[pltpu.VMEM((2 * EDGE, WIDE), f32)],
             compiler_params=params,
         )(halo, taps_near, qs, ks, vs, gg, ft, grad_other, wo)

time: 95.9 us -> 95.9 us (level)
  no operation moved by 1% of the time
where the time goes in v9:
time: 95.9 us; the launch traced here: 95.6 us
  blocking collectives  68.4 us (71%)
  Pallas kernels  15.1 us (16%)
  waiting for transfers between devices  5.67 us (6%)
  starting transfers between devices  5.51 us (6%)
    all_to_all x1, blocking collectives, on_device(): lax.all_to_all(send, 'ctx', split_axis=0, concat_axis=0, tiled=True, axis...  37.7 us
    all_to_all x1, blocking collectives, on_device(): lax.all_to_all(solved, 'ctx', split_axis=0, concat_axis=0, tiled=True, ax...  30.7 us
    pallas_call x1, Pallas kernels, on_device(): pl.pallas_call(spectral_kernel, out_shape=fields, scratch_shapes=[pltpu.V...  6.15 us
    ppermute x2, waiting for transfers between devices, shifted(): lax.ppermute(value, axis, [(source, source + steps) for source in range(f...  5.66 us
    ppermute x2, starting transfers between devices, shifted(): lax.ppermute(value, axis, [(source, source + steps) for source in range(f...  5.32 us
    pallas_call x1, Pallas kernels, on_device(): pl.pallas_call(fetch_kernel, in_specs=[smem] + [hbm] * 7, out_specs=[vmem...  3.1 us
    pallas_call x1, Pallas kernels, on_device(): pl.pallas_call(project_kernel, in_specs=[vmem] * 7, out_specs=[hbm, vmem,...  2.65 us
  transfers between devices with their start and end apart: 4, of which 1 were waited for; matrix products, arithmetic and copies ran while one was open for 0% of the time, Pallas kernels for 7%

profile of v9, /device:TPU:30, one launch (start us, length us, event | category | flops | bytes accessed | tf_op | source)
XLA Modules:
  0.0 95.6 jit_solution(9017711916832950121)
XLA Ops:
  0.6 0.1 collective-permute-start.1
  0.7 0.8 tails.1
  1.6 3.4 %collective-permute-start = (bf16[3,8,1024]{2,1,0:T(8,128)(2,1)S(1)}, bf16[3,8,1024]{2,1,0:T(8,128)(2,1)S(1)}, u32[]{:S(2)}, u32[]{:S(2)}) collective-permute-start(bf16[3,8,1024]{2,1,0:T(8,128)(2,1)S(1)} %tails.1), channel_id=1, source_target_pairs={{0,2},{2,4},{4,6},{6,8},{8,10},{10,12},{12,14},{14,16},{16,18},{18... | collective-permute-start | bytes 147464 | tf_op jit(solution)/shard_map/ppermute | solution.py:24
  5.0 3.1 %fetch.1 = (f32[128,1024]{1,0:T(8,128)S(1)}, f32[128,1024]{1,0:T(8,128)S(1)}, f32[128,1024]{1,0:T(8,128)S(1)}, f32[128,1024]{1,0:T(8,128)S(1)}, f32[1024,128]{1,...) custom-call(s32[1]{0:T(128)} %bitcast.here, ...), custom_call_target="tpu_custom_call" | custom-call | flops 536870912 | bytes 8388608 | tf_op jit(solution)/shard_map/fetch/pallas_call | solution.py:316
  8.1 0.0 collective-permute-done.halo
  8.1 0.0 collective-permute-done.1.other
  8.1 0.0 copy-start
  8.1 0.0 copy-start.1
  8.1 0.0 copy-start.2
  8.1 0.0 copy-start.3
  8.2 0.0 copy-start.4
  8.2 1.0 %prepare.1 = (bf16[128,24,128]{2,1,0:T(8,128)(2,1)S(1)}, f32[128,1024]{1,0:T(8,128)S(1)}, f32[128,1024]{1,0:T(8,128)S(1)}, f32[128,1024]{1,0:T(8,128)S(1)}, f32[128,1024]{1,0:T(8,128)S(1)}) custom-call(bf16[3,8,1024]{2,1,0:T(8,128)(2,1)S(1)} %collective-permute-done.halo, ...), custom_call_target="tpu_custom_call", output_to_operand_aliasing={{1}: (2, {}), {2}: (3, {}), {3}: (4, {})} | custom-call | tf_op jit(solution)/shard_map/prepare/pallas_call | solution.py:344
  9.1 37.7 %all_to_all.10.x = bf16[128,24,128]{2,1,0:T(8,128)(2,1)S(1)} all-to-all(bf16[128,24,128]{2,1,0:T(8,128)(2,1)S(1)} %get-tuple-element.41), channel_id=1, replica_groups={{0,128,64,192,32,160,96,224,2,130,66,194,34,162,98,226,4,132,68,196,36,..., dimensions={0} | all-to-all | bytes 1572864 | tf_op jit(solution)/shard_map/all_to_all | solution.py:354
  46.8 0.0 copy-done
  46.8 0.0 copy-done.1
  46.8 0.0 copy-done.2
  46.8 0.0 copy-done.3
  46.8 0.0 copy-done.4
  46.8 6.1 %spectral.1 = bf16[128,24,128]{2,1,0:T(8,128)(2,1)S(1)} custom-call(bf16[128,24,128]{2,1,0:T(8,128)(2,1)S(1)} %all_to_all.10.x, bf16[256,256]{1,0:T(8,128)(2,1)S(1)} %copy-done.4, bf16[2,256,256]{2,1,0:T(8,128)(2,1)S(1)} %copy-done.1, bf16[2,256,256]{2,1,0:T(8,128)(2,1)S(1)} %copy-done, bf16[256,256]{1,0:T(8,128)(2,1)S(1)} %copy-done.3, ...), custom_call_target="tpu_custom_call" | custom-call | tf_op jit(solution)/shard_map/spectral/pallas_call | solution.py:359
  53.0 30.7 %all_to_all.11.landed = bf16[128,24,128]{2,1,0:T(8,128)(2,1)S(1)} all-to-all(bf16[128,24,128]{2,1,0:T(8,128)(2,1)S(1)} %spectral.1), channel_id=1, replica_groups={{0,128,64,192,32,160,96,224,2,130,66,194,34,162,98,226,4,132,68,196,36,..., dimensions={0} | all-to-all | bytes 1572864 | tf_op jit(solution)/shard_map/all_to_all | solution.py:366
  83.7 0.5 gate.1
  84.3 0.1 collective-permute-start.3
  84.4 1.9 %collective-permute-start.2 = (bf16[3,8,1024]{2,1,0:T(8,128)(2,1)S(1)}, bf16[3,8,1024]{2,1,0:T(8,128)(2,1)S(1)}, u32[]{:S(2)}, u32[]{:S(2)}) collective-permute-start(bf16[3,8,1024]{2,1,0:T(8,128)(2,1)S(1)} %get-tuple-element.52), channel_id=1, source_target_pairs={{2,0},{4,2},{6,4},{8,6},{10,8},{12,10},{14,12},{16,14},{18,16},{20... | collective-permute-start | bytes 147464 | tf_op jit(solution)/shard_map/ppermute | solution.py:24
  86.3 2.6 %project.1 = (f32[128,1024]{1,0:T(8,128)}, f32[128,1024]{1,0:T(8,128)S(1)}, f32[3,16,1024]{2,1,0:T(8,128)S(1)}, bf16[128,1024]{1,0:T(8,128)(2,1)}, bf16[128,1024]{1,0:T(8,128)(2,1)}, /*index=5*/bf16[128,1024]{1,0:T(8,128)(2,1)}) custom-call(bf16[128,24,128]{2,1,0:T(8,128)(2,1)S(1)} %all_to_all.11.landed, bf16[128,1024]{1,0:T(8,128)(2,1)S(1)} %get-tuple-element.46.gated, ...), custom_call_target="tpu_custom_call" | custom-call | flops 536870912 | bytes 8388608 | tf_op jit(solution)/shard_map/project/pallas_call | solution.py:383
  88.9 5.7 %collective-permute-done.2.after = bf16[3,8,1024]{2,1,0:T(8,128)(2,1)S(1)} collective-permute-done((bf16[3,8,1024]{2,1,0:T(8,128)(2,1)S(1)}, bf16[3,8,1024]{2,1,0:T(8,128)(2,1)S(1)}, u32[]{:S(2)}, u32[]{:S(2)}) %collective-permute-start.2) | collective-permute-done | bytes 49184 | tf_op jit(solution)/shard_map/ppermute | solution.py:24
  94.6 0.0 collective-permute-done.3.other
  94.6 0.9 close.1
Async XLA Ops:
  0.6 7.5 %collective-permute-start.1 = (bf16[128,1024]{1,0:T(8,128)(2,1)}, bf16[128,1024]{1,0:T(8,128)(2,1)S(1)}, u32[]{:S(2)}, u32[]{:S(2)}) collective-permute-start(bf16[128,1024]{1,0:T(8,128)(2,1)} %mine.1), channel_id=1, source_target_pairs={{0,1},{1,0},{2,3},{3,2},{4,5},{5,4},{6,7},{7,6},{8,9},{9,8},{10,11... | collective-permute-start | bytes 786440 | tf_op jit(solution)/shard_map/ppermute | solution.py:299
  1.6 6.5 %collective-permute-start = (bf16[3,8,1024]{2,1,0:T(8,128)(2,1)S(1)}, bf16[3,8,1024]{2,1,0:T(8,128)(2,1)S(1)}, u32[]{:S(2)}, u32[]{:S(2)}) collective-permute-start(bf16[3,8,1024]{2,1,0:T(8,128)(2,1)S(1)} %tails.1), channel_id=1, source_target_pairs={{0,2},{2,4},{4,6},{6,8},{8,10},{10,12},{12,14},{14,16},{16,18},{18... | collective-permute-start | bytes 147464 | tf_op jit(solution)/shard_map/ppermute | solution.py:24
  8.1 38.7 %copy-start = (bf16[2,256,256]{2,1,0:T(8,128)(2,1)S(1)}, bf16[2,256,256]{2,1,0:T(8,128)(2,1)}, u32[]{:S(2)}) copy-start(bf16[2,256,256]{2,1,0:T(8,128)(2,1)} %constant.16.clone.back) | copy-start | bytes 786436
  8.1 38.7 %copy-start.1 = (bf16[2,256,256]{2,1,0:T(8,128)(2,1)S(1)}, bf16[2,256,256]{2,1,0:T(8,128)(2,1)}, u32[]{:S(2)}) copy-start(bf16[2,256,256]{2,1,0:T(8,128)(2,1)} %constant.15.clone.second) | copy-start | bytes 786436
  8.1 38.7 %copy-start.2 = (f32[2,128,128]{2,1,0:T(8,128)S(1)}, f32[2,128,128]{2,1,0:T(8,128)}, u32[]{:S(2)}) copy-start(f32[2,128,128]{2,1,0:T(8,128)} %constant.18.clone.twist) | copy-start | bytes 393220
  8.1 38.7 %copy-start.3 = (bf16[256,256]{1,0:T(8,128)(2,1)S(1)}, bf16[256,256]{1,0:T(8,128)(2,1)}, u32[]{:S(2)}) copy-start(bf16[256,256]{1,0:T(8,128)(2,1)} %constant.17.clone.last) | copy-start | bytes 393220
  8.2 38.7 %copy-start.4 = (bf16[256,256]{1,0:T(8,128)(2,1)S(1)}, bf16[256,256]{1,0:T(8,128)(2,1)}, u32[]{:S(2)}) copy-start(bf16[256,256]{1,0:T(8,128)(2,1)} %constant.14.clone.first) | copy-start | bytes 393220
  84.3 10.3 %collective-permute-start.3 = (f32[128,1024]{1,0:T(8,128)S(1)}, f32[128,1024]{1,0:T(8,128)S(1)}, u32[]{:S(2)}, u32[]{:S(2)}) collective-permute-start(f32[128,1024]{1,0:T(8,128)S(1)} %get-tuple-element.54), channel_id=1, source_target_pairs={{0,1},{1,0},{2,3},{3,2},{4,5},{5,4},{6,7},{7,6},{8,9},{9,8},{10,11... | collective-permute-start | bytes 1572872 | tf_op jit(solution)/shard_map/ppermute | solution.py:380
  84.4 10.2 %collective-permute-start.2 = (bf16[3,8,1024]{2,1,0:T(8,128)(2,1)S(1)}, bf16[3,8,1024]{2,1,0:T(8,128)(2,1)S(1)}, u32[]{:S(2)}, u32[]{:S(2)}) collective-permute-start(bf16[3,8,1024]{2,1,0:T(8,128)(2,1)S(1)} %get-tuple-element.52), channel_id=1, source_target_pairs={{2,0},{4,2},{6,4},{8,6},{10,8},{12,10},{14,12},{16,14},{18,16},{20... | collective-permute-start | bytes 147464 | tf_op jit(solution)/shard_map/ppermute | solution.py:24
